TPU v7x, 256 devices: a whole 4x4x8 slice. The times are simulated.
256 devices in a mesh: dp: 64 (over z, x, core), fsdp: 4 (over y).
Axes of the slice: x: 4, y: 4, z: 8, core: 2. Of those that a mesh axis runs over, the one named last changes fastest.
Arguments:
- tokens: bfloat16 [4, 128, 256, 3584], P('fsdp', 'dp'), may hold values from -6 to 6
- lengths: int32 [4, 128], P('fsdp', 'dp'), may hold values from 64 to 256, as said below
- queries: bfloat16 [4, 128, 1792], P('fsdp', 'dp'), may hold values from -6 to 6
- positives: int32 [4, 128], P('fsdp', 'dp'), may hold values from 0 to 127, as said below
- kv_weight: bfloat16 [3584, 512], P('fsdp'), may hold values from -0.09375 to 0.09375
Outputs:
- document_loss: float32 [4, 128], P('fsdp', 'dp')
- grad_tokens: bfloat16 [4, 128, 256, 3584], P('fsdp', 'dp')
- grad_queries: bfloat16 [4, 128, 1792], P('fsdp', 'dp')
- grad_weight: float32 [3584, 512], P(None, ('dp', 'fsdp'))
Inputs may be any that keep to these rules, and one draw needn't show every extreme that they name: The lengths of document j of device h and of document j of device h + 64/2 (along dp, same batch, 0 <= h < 32) add up to 320. `positives`: A document is never its own positive.
All inputs are finite; a program needn't handle non-finite values.
Results may differ from a plain program's by a relative error of at most 0.015.
Values may be sent and summed in bfloat16 or wider, within the bound.
No kernel may reach another device: no remote copies, remote signals or barrier semaphores. Data moves between devices by JAX's collectives and lax.ppermute only.
A program may use at most 128 MiB of HBM per device.

v0:
```python
import jax
import jax.numpy as jnp
from jax import lax
from jax.sharding import PartitionSpec as P

QH = 14
KVH = 2
HD = 128
QW = 1792


SOFTMAX_TEMPER = 0.05


def attend(query_rows, keyval, row_slot):
    slot_count = query_rows.shape[0]
    row_count = keyval.shape[0]
    group_size = QH // KVH
    query_heads = query_rows.reshape(slot_count, KVH, group_size, HD)
    key_heads = keyval[:, : KVH * HD].reshape(row_count, KVH, HD)
    value_heads = keyval[:, KVH * HD :].reshape(row_count, KVH, HD)
    scores = jnp.einsum(
        "skgd,rkd->skgr", query_heads, key_heads, preferred_element_type=jnp.float32
    ) * HD ** (-0.5)
    row_mask = (row_slot[None, :] == jnp.arange(slot_count)[:, None])[:, None, None, :]
    expvals = jnp.where(row_mask, jnp.exp(jnp.where(row_mask, scores, 0.0)), 0.0)
    attn = expvals / jnp.sum(expvals, axis=-1, keepdims=True)
    attn_b = attn.astype(jnp.bfloat16)
    readout = jnp.einsum("skgr,rkd->skgd", attn_b, value_heads, preferred_element_type=jnp.float32)
    return (query_heads, key_heads, value_heads, attn, attn_b, readout.reshape(slot_count, QW))


def attend_back(grad_read, query_heads, key_heads, value_heads, attn, attn_b):
    slot_count = query_heads.shape[0]
    row_count = key_heads.shape[0]
    grad_heads = grad_read.reshape(slot_count, KVH, QH // KVH, HD)
    grad_w = jnp.einsum(
        "skgd,rkd->skgr", grad_heads, value_heads, preferred_element_type=jnp.float32
    )
    grad_score = attn * (grad_w - jnp.sum(attn * grad_w, axis=-1, keepdims=True)) * HD ** (-0.5)
    grad_score = grad_score.astype(jnp.bfloat16)
    grad_query = jnp.einsum(
        "skgr,rkd->skgd", grad_score, key_heads, preferred_element_type=jnp.float32
    )
    grad_key = jnp.einsum(
        "skgr,skgd->rkd", grad_score, query_heads, preferred_element_type=jnp.float32
    )
    grad_value = jnp.einsum(
        "skgr,skgd->rkd", attn_b, grad_heads, preferred_element_type=jnp.float32
    )
    grad_keyval = jnp.concatenate(
        [grad_key.reshape(row_count, KVH * HD), grad_value.reshape(row_count, KVH * HD)], axis=-1
    )
    return (
        grad_query.reshape(slot_count, QW).astype(jnp.bfloat16),
        grad_keyval.astype(jnp.bfloat16),
    )


def contrast(emb_local, own_positives):
    slot_count = emb_local.shape[0]
    everyone = lax.all_gather(emb_local, "dp", axis=0, tiled=True)
    doc_total = everyone.shape[0]
    own_ids = lax.axis_index("dp") * slot_count + jnp.arange(slot_count)
    columns = jnp.arange(doc_total)
    similarity_matrix = (
        jnp.einsum("sd,nd->sn", emb_local, everyone, preferred_element_type=jnp.float32)
        / SOFTMAX_TEMPER
    )
    self_pair = columns[None, :] == own_ids[:, None]
    sim_exp = jnp.where(self_pair, 0.0, jnp.exp(similarity_matrix))
    row_total = jnp.sum(sim_exp, axis=-1)
    picked = columns[None, :] == own_positives[:, None]
    document_loss = jnp.log(row_total) - jnp.sum(jnp.where(picked, similarity_matrix, 0.0), axis=-1)
    probability = (sim_exp / row_total[:, None]).astype(jnp.bfloat16)
    chosen_partner = picked.astype(jnp.bfloat16)
    row_portion = jnp.dot(probability, everyone, preferred_element_type=jnp.float32) - jnp.dot(
        chosen_partner, everyone, preferred_element_type=jnp.float32
    )
    column_portion = lax.psum_scatter(
        jnp.einsum("sn,sd->nd", probability, emb_local, preferred_element_type=jnp.float32)
        - jnp.einsum("sn,sd->nd", chosen_partner, emb_local, preferred_element_type=jnp.float32),
        "dp",
        scatter_dimension=0,
        tiled=True,
    )
    return (document_loss, (row_portion + column_portion) / SOFTMAX_TEMPER)


def embed(readout):
    length_norm = jnp.sqrt(jnp.sum(readout * readout, axis=-1, keepdims=True) + 1e-06)
    unit_vec = readout / length_norm
    return (unit_vec, length_norm, unit_vec.astype(jnp.bfloat16))


def local(tokens, lengths, queries, positives, kv_weight):
    own_tokens = tokens[0]
    own_lengths = lengths[0]
    own_queries = queries[0]
    own_positives = positives[0]
    slot_count = own_tokens.shape[0]
    block_rows = own_tokens.shape[1]
    model_width = own_tokens.shape[2]
    weight = lax.all_gather(kv_weight, "fsdp", axis=0, tiled=True)
    block_range = jnp.arange(block_rows)
    slot_range = jnp.arange(slot_count)
    row_data = own_tokens.reshape(-1, model_width)
    live_home = block_range[None, :] < own_lengths[:, None]
    row_slot = jnp.where(live_home, slot_range[:, None], -1).reshape(-1)
    keyval = jnp.dot(row_data, weight, preferred_element_type=jnp.float32).astype(jnp.bfloat16)
    query_heads, key_heads, value_heads, attn, attn_b, readout = attend(
        own_queries, keyval, row_slot
    )
    unit_vec, length_norm, emb_sel = embed(readout)
    document_loss, grad_home = contrast(emb_sel, own_positives)
    grad_read = (
        (grad_home - unit_vec * jnp.sum(unit_vec * grad_home, axis=-1, keepdims=True)) / length_norm
    ).astype(jnp.bfloat16)
    grad_query, grad_keyval = attend_back(
        grad_read, query_heads, key_heads, value_heads, attn, attn_b
    )
    grad_rows = jnp.dot(grad_keyval, weight.T, preferred_element_type=jnp.float32).astype(
        jnp.bfloat16
    )
    weight_part = jnp.dot(row_data.T, grad_keyval, preferred_element_type=jnp.float32)
    grad_tok = grad_rows.reshape(slot_count, block_rows, model_width)
    grad_weight = lax.psum_scatter(weight_part, ("dp", "fsdp"), scatter_dimension=1, tiled=True)
    return (document_loss[None], grad_tok[None], grad_query[None], grad_weight)


def solution(mesh):
    placed = (
        P("fsdp", "dp", None, None),
        P("fsdp", "dp"),
        P("fsdp", "dp", None),
        P("fsdp", "dp"),
        P("fsdp", None),
    )
    return jax.shard_map(
        local,
        mesh=mesh,
        in_specs=placed,
        out_specs=(
            P("fsdp", "dp"),
            P("fsdp", "dp", None, None),
            P("fsdp", "dp", None),
            P(None, ("dp", "fsdp")),
        ),
        check_vma=False,
    )
```

profile of v0, /device:TPU:1, one launch (start us, length us, event | category | flops | bytes accessed | tf_op | source)
XLA Modules:
  0.0 592.1 jit_solution(3866670211496206527)
XLA Ops:
  7.2 0.0 all-gather.3.cloned.1.call-start
  7.2 0.7 all-gather.3.cloned.1.call-update
  7.9 0.0 all-reduce.5.cloned.1.call-start
  7.9 0.7 fusion.27
  8.7 0.7 reshape_squeeze.7
  9.4 50.7 %all-gather.3.cloned.1.call-done = bf16[3584,512]{1,0:T(8,128)(2,1)} async-done(((bf16[896,512]{1,0:T(8,128)(2,1)}), bf16[3584,512]{1,0:T(8,128)(2,1)}) %all-gather.3.cloned.1.call-update) | async-done | bytes 3670032 | tf_op jit(solution)/shard_map/all_gather | solution.py:104
  60.1 0.0 copy-start
  60.1 5.3 convolution_convert_fusion.1
  65.4 0.0 copy-start.1
  65.5 0.2 fusion.41
  65.7 0.3 multiply_reduce_fusion.1
  66.0 0.1 fusion.39
  66.1 51.3 %all-gather = bf16[64,2,1792]{2,1,0:T(2,128)(2,1)S(1)} all-gather(bf16[1,2,1792]{2,1,0:T(2,128)(2,1)S(1)} %bitcast.82), channel_id=1, replica_groups=mesh['dp'=64,'fsdp'=4] {'dp'}, dimensions={0}, use_global_device_ids=true | all-gather | bytes 465920 | tf_op jit(solution)/shard_map/all_gather | solution.py:62
  117.4 0.2 reshape.119
  117.6 0.0 copy-done
  117.6 0.4 fusion.38
  118.0 0.4 fusion.36
  118.4 1.3 convolution_subtract_fusion
  119.8 0.0 all-reduce.5.cloned.1.call-update
  119.8 0.0 all-reduce.7.cloned.1.call-start
  119.8 0.0 copy-done.1
  119.8 0.6 dynamic-slice
  121.1 0.2 fusion.37
  121.3 179.1 %all-reduce.5.cloned.1.call-done = f32[128,1792]{1,0:T(8,128)} async-done(((f32[128,1792]{1,0:T(8,128)}), f32[128,1792]{1,0:T(8,128)}) %all-reduce.5.cloned.1.call-update) | async-done | bytes 917520
  300.5 1.2 multiply_reduce_fusion.2
  301.6 0.1 fusion.23
  301.7 0.1 convolution_bitcast_fusion.3
  301.9 0.3 fusion.4
  302.2 0.3 fusion.3
  302.5 7.1 %convolution_bitcast_fusion = f32[3584,512]{0,1:T(8,128)} fusion(bf16[512,3584]{1,0:T(8,128)(2,1)} %bitcast.73, bf16[512,256]{0,1:T(8,128)(2,1)S(1)} %bitcast.76, bf16[512,256]{0,1:T(8,128)(2,1)S(1)} %bitcast.78), kind=kOutput, calls=%fused_computation.1 | convolution fusion | flops 1880096768 | bytes 11534336 | tf_op jit(solution)/shard_map/dot_general | solution.py:125
  309.6 0.0 all-reduce.7.cloned.1.call-update
  309.7 0.5 subtract_bitcast_fusion
  310.2 0.2 fusion.13
  310.4 0.6 convert_element_type.48
  311.0 6.0 %convolution_convert_fusion = bf16[512,3584]{1,0:T(8,128)(2,1)} fusion(bf16[3584,512]{1,0:T(8,128)(2,1)} %all-gather.3.cloned.1.call-done, bf16[512,256]{0,1:T(8,128)(2,1)S(1)} %bitcast.77, bf16[512,256]{0,1:T(8,128)(2,1)S(1)} %bitcast.79), kind=kOutput, calls=%fused_computation.2 | convolution fusion | flops 1881931776 | bytes 7864320 | tf_op jit(solution)/shard_map/dot_general | solution.py:122
  317.1 267.0 %all-reduce.7.cloned.1.call-done = f32[3584,512]{0,1:T(8,128)} async-done(((f32[3584,512]{0,1:T(8,128)}), f32[3584,512]{0,1:T(8,128)}) %all-reduce.7.cloned.1.call-update) | async-done | bytes 7340048
  584.0 1.5 constant_dynamic-slice_fusion
  (9 shorter events, 0.1 us)
Async XLA Ops:
  7.2 53.0 %all-gather.3.cloned.1.call-start = ((), (), s32[]{:S(2)}) async-start(), calls=%async_computation | async-start | bytes 4587520 | tf_op jit(solution)/shard_map/all_gather | solution.py:104
  7.9 292.6 %all-reduce.5.cloned.1.call-start = ((), (), s32[]{:S(2)}) async-start(), calls=%async_computation.1 | async-start | bytes 1835008
  60.1 57.5 %copy-start = (s32[1,2]{1,0:T(1,128)S(1)}, s32[1,2]{1,0:T(1,128)}, u32[]{:S(2)}) copy-start(s32[1,2]{1,0:T(1,128)} %param.8) | copy-start | bytes 28
  65.4 54.4 %copy-start.1 = (u32[256]{0:T(256)S(1)}, u32[256]{0:T(256)}, u32[]{:S(2)}) copy-start(u32[256]{0:T(256)} %constant.27) | copy-start | bytes 3076
  119.8 464.2 %all-reduce.7.cloned.1.call-start = ((), (), s32[]{:S(2)}) async-start(), calls=%async_computation.2 | async-start | bytes 14680064
Sparse Core Ops, SparseCore 0:
  9.8 50.2 all-gather.2
  119.9 180.5 all-reduce.4
  309.8 274.1 all-reduce.6
where the time goes:
time: 593 us; the launch traced here: 592 us
  waiting for transfers between devices  498 us (84%)
  blocking collectives  51.3 us (9%)
  matrix products  23.4 us (4%)
  between operations  14.5 us (2%)
    unnamed x5, waiting for transfers between devices  447 us
    all_gather x1, blocking collectives, contrast(): everyone = lax.all_gather(emb_local, 'dp', axis=0, tiled=True)  51.3 us
    all_gather x1, waiting for transfers between devices, local(): weight = lax.all_gather(kv_weight, 'fsdp', axis=0, tiled=True)  50.7 us
  transfers between devices with their start and end apart: 3, of which 3 were waited for; matrix products, arithmetic and copies ran while one was open for 2% of the time, Pallas kernels for 0%

commit v1 on v0

v1 whole, which is shorter than its diff:
```python
import jax
import jax.numpy as jnp
from jax import lax
from jax.sharding import PartitionSpec as P

QH = 14
KVH = 2
GRP = QH // KVH
HD = 128
QW = QH * HD
KVW = 2 * KVH * HD
HALF = QW // 2
TYPES = 2 * KVH

SOFTMAX_TEMPER = 0.05

NZ, NX, NC, NY = 8, 4, 2, 4
N_DP = NZ * NX * NC


def dp_index(z, x, c):
    return (z * NX + x) * NC + c


OTHER_CORE = [(i, i ^ 1) for i in range(N_DP)]
CHIPS = [[dp_index(z, x, c) for z in range(NZ) for x in range(NX)] for c in range(NC)]


def y_shift(k):
    return [(i, (i + k) % NY) for i in range(NY)]


def z_shift(k):
    return [
        (dp_index(z, x, c), dp_index((z + k) % NZ, x, c))
        for z in range(NZ)
        for x in range(NX)
        for c in range(NC)
    ]


OWNERS = [
    [
        dp_index(2 * t + p, x, c) * NY + y
        for p in range(2)
        for x in range(NX)
        for y in range(NY)
    ]
    for t in range(TYPES)
    for c in range(NC)
]


def pick_core(core, mine, other):
    return (jnp.where(core == 0, mine, other), jnp.where(core == 0, other, mine))


def gather_weight(kv_weight, core, y):
    rows = kv_weight.shape[0]
    half = lax.dynamic_slice(kv_weight, (0, core * (KVW // 2)), (rows, KVW // 2))
    got = [lax.ppermute(half, "fsdp", y_shift(k)) for k in (3, 2, 1)]
    mine = jnp.concatenate(got, axis=0)
    other = lax.ppermute(mine, "dp", OTHER_CORE)
    rest = jnp.concatenate(pick_core(core, mine, other), axis=1)
    ring = jnp.concatenate([kv_weight, rest, kv_weight, rest], axis=0)
    start = (NY - y) % NY
    return lax.dynamic_slice(ring, (start * rows, 0), (NY * rows, KVW))


def gather_docs(rows, core):
    docs = rows.shape[0]
    other = lax.ppermute(rows, "dp", OTHER_CORE)
    chip = jnp.concatenate(pick_core(core, rows, other), axis=0)
    width = chip.shape[1] // 2
    half = lax.dynamic_slice(chip, (0, core * width), (NC * docs, width))
    spread = jnp.broadcast_to(half[None], (NZ * NX, NC * docs, width))
    got = lax.all_to_all(spread, "dp", 0, 0, axis_index_groups=CHIPS)
    got = got.reshape(NZ * NX * NC * docs, width)
    return pick_core(core, got, lax.ppermute(got, "dp", OTHER_CORE))


def contrast(unit, norm, own_positives, core):
    docs = unit.shape[0]
    emb = unit.astype(jnp.bfloat16)
    mark = jnp.broadcast_to(own_positives.astype(jnp.bfloat16)[:, None], (docs, HD))
    packed = jnp.concatenate([emb[:, :HALF], mark, emb[:, HALF:], mark], axis=1)
    first, second = gather_docs(packed, core)
    everyone = jnp.concatenate([first[:, :HALF], second[:, :HALF]], axis=1)
    positives = first[:, HALF].astype(jnp.int32)
    total_docs = everyone.shape[0]
    sim = (
        lax.dot_general(
            everyone, everyone, (((1,), (1,)), ((), ())), preferred_element_type=jnp.float32
        )
        / SOFTMAX_TEMPER
    )
    ids = jnp.arange(total_docs)
    sim_exp = jnp.where(ids[:, None] == ids[None, :], 0.0, jnp.exp(sim))
    total = jnp.sum(sim_exp, axis=-1)
    picked = positives[:, None] == ids[None, :]
    loss = jnp.log(total) - jnp.sum(jnp.where(picked, sim, 0.0), axis=-1)
    prob = (sim_exp / total[:, None]).astype(jnp.bfloat16)
    pick = picked.astype(jnp.bfloat16)
    first_id = lax.axis_index("dp") * docs
    own = lambda a: lax.dynamic_slice_in_dim(a, first_id, docs, 0)
    coef = jnp.concatenate([own(prob), own(prob.T), own(pick), own(pick.T)], axis=0)
    parts = jnp.dot(coef, everyone, preferred_element_type=jnp.float32).reshape(4, docs, QW)
    grad_unit = (parts[0] + parts[1] - parts[2] - parts[3]) / SOFTMAX_TEMPER
    grad_read = (
        (grad_unit - unit * jnp.sum(unit * grad_unit, axis=-1, keepdims=True)) / norm
    ).astype(jnp.bfloat16)
    return own(loss), grad_read


def exchange_types(factors):
    z = lax.axis_index("dp") // (NX * NC)
    quad = z // 2
    take = lambda t: lax.dynamic_index_in_dim(factors, t, 0, keepdims=False)
    got = [take(quad)]
    for k in (1, 2, 3):
        got.append(lax.ppermute(take((quad + k) % TYPES), "dp", z_shift(2 * k)))
    return jnp.concatenate(got, axis=0)


def reduce_weight(factors, width, core):
    quads = exchange_types(factors)
    both = jnp.concatenate([quads, lax.ppermute(quads, "dp", OTHER_CORE)], axis=0)
    heads = both[:, width:].reshape(-1, 2, NX, NC, NY, HD // (2 * NX * NC * NY))
    heads = lax.dynamic_index_in_dim(heads, core, 3, keepdims=False)
    heads = heads.reshape(both.shape[0], HD // NC)
    part = lax.dot_general(
        heads, both[:, :width], (((0,), (0,)), ((), ())), preferred_element_type=jnp.float32
    ).astype(jnp.bfloat16)
    pieces = part.reshape(2 * NX * NY, -1, width)
    got = lax.all_to_all(pieces, ("dp", "fsdp"), 0, 0, axis_index_groups=OWNERS)
    return jnp.sum(got.astype(jnp.float32), axis=0).T


def local(tokens, lengths, queries, positives, kv_weight):
    own_tokens = tokens[0]
    docs, block, width = own_tokens.shape
    core = lax.axis_index("dp") % NC
    y = lax.axis_index("fsdp")
    weight = gather_weight(kv_weight, core, y)
    rows = own_tokens.reshape(-1, width)
    live = jnp.arange(block)[None, :] < lengths[0][:, None]
    mask = live[:, None, None, :]
    keyval = jnp.dot(rows, weight, preferred_element_type=jnp.float32).astype(jnp.bfloat16)
    keyval = keyval.reshape(docs, block, 2, KVH, HD)
    keys, values = keyval[:, :, 0], keyval[:, :, 1]
    heads = queries[0].reshape(docs, KVH, GRP, HD)
    scores = jnp.einsum("nkgd,nrkd->nkgr", heads, keys, preferred_element_type=jnp.float32)
    scores = scores * HD ** (-0.5)
    expvals = jnp.where(mask, jnp.exp(jnp.where(mask, scores, 0.0)), 0.0)
    attn = expvals / jnp.sum(expvals, axis=-1, keepdims=True)
    attn_b = attn.astype(jnp.bfloat16)
    readout = jnp.einsum("nkgr,nrkd->nkgd", attn_b, values, preferred_element_type=jnp.float32)
    readout = readout.reshape(docs, QW)
    norm = jnp.sqrt(jnp.sum(readout * readout, axis=-1, keepdims=True) + 1e-06)
    unit = readout / norm
    loss, grad_read = contrast(unit, norm, positives[0], core)
    grad_heads = grad_read.reshape(docs, KVH, GRP, HD)
    grad_w = jnp.einsum("nkgd,nrkd->nkgr", grad_heads, values, preferred_element_type=jnp.float32)
    grad_score = attn * (grad_w - jnp.sum(attn * grad_w, axis=-1, keepdims=True)) * HD ** (-0.5)
    grad_score = grad_score.astype(jnp.bfloat16)
    grad_query = jnp.einsum("nkgr,nrkd->nkgd", grad_score, keys, preferred_element_type=jnp.float32)
    grad_query = grad_query.reshape(docs, QW).astype(jnp.bfloat16)

    mix = jnp.stack([grad_score, attn_b], axis=1)
    right = jnp.stack([heads, grad_heads], axis=1)
    left = jnp.einsum("ntkgr,nrw->tkngw", mix, own_tokens, preferred_element_type=jnp.float32)
    factors = jnp.concatenate(
        [left.astype(jnp.bfloat16), right.transpose(1, 2, 0, 3, 4)], axis=-1
    ).reshape(TYPES, docs * GRP, width + HD)
    factors = jnp.pad(factors, ((0, 0), (0, 2), (0, 0)))
    grad_weight = reduce_weight(factors, width, core)

    grad_keyval = jnp.einsum(
        "ntkgr,ntkgd->nrtkd", mix, right, preferred_element_type=jnp.float32
    ).astype(jnp.bfloat16)
    grad_tok = lax.dot_general(
        grad_keyval.reshape(docs * block, KVW),
        weight,
        (((1,), (1,)), ((), ())),
        preferred_element_type=jnp.float32,
    ).astype(jnp.bfloat16)
    grad_tok = grad_tok.reshape(docs, block, width)
    return (loss[None], grad_tok[None], grad_query[None], grad_weight)


def solution(mesh):
    placed = (
        P("fsdp", "dp", None, None),
        P("fsdp", "dp"),
        P("fsdp", "dp", None),
        P("fsdp", "dp"),
        P("fsdp", None),
    )
    return jax.shard_map(
        local,
        mesh=mesh,
        in_specs=placed,
        out_specs=(
            P("fsdp", "dp"),
            P("fsdp", "dp", None, None),
            P("fsdp", "dp", None),
            P(None, ("dp", "fsdp")),
        ),
        check_vma=False,
    )
```

time: 593 us -> 128 us (0.22)
  waiting for transfers between devices: 498 us -> 53.1 us
  blocking collectives: 51.3 us -> 0 us
  starting transfers between devices: 0.12 us -> 29.3 us
  other arithmetic: 1.43 us -> 21.4 us
  between operations: 14.5 us -> 1.2 us
  matrix products: 23.4 us -> 12.8 us
  local copies, waits for them, and re-layouts: 3.73 us -> 9.84 us
    unnamed x5 -> x0, waiting for transfers between devices: 447 us -> none
    all_gather x1 -> x0, blocking collectives: 51.3 us -> none  [contrast(): everyone = lax.all_gather(emb_local, 'dp', axis=0, tiled=True)]
    all_gather x1 -> x0, waiting for transfers between devices: 50.7 us -> none  [local(): weight = lax.all_gather(kv_weight, 'fsdp', axis=0, tiled=True)]
    ppermute x0 -> x10, waiting for transfers between devices: none -> 40.2 us  [the longest x3 22.6 us: gather_weight(): got = [lax.ppermute(half, 'fsdp', y_shift(k)) for k in (3, 2, 1)]]
    concatenate x0 -> x5, other arithmetic: none -> 17.8 us  [the longest x1 17.6 us: gather_weight(): ring = jnp.concatenate([kv_weight, rest, kv_weight, rest], axis=0)]
    all_to_all x0 -> x2, starting transfers between devices: none -> 15.2 us  [the longest x1 11 us: gather_docs(): got = lax.all_to_all(spread, 'dp', 0, 0, axis_index_groups=CHIPS)]
    ppermute x0 -> x10, starting transfers between devices: none -> 14.1 us  [the longest x3 4.87 us: exchange_types(): got.append(lax.ppermute(take((quad + k) % TYPES), 'dp', z_shift(2 * k)))]
    all_to_all x0 -> x2, waiting for transfers between devices: none -> 13 us  [the longest x1 11.5 us: gather_docs(): got = lax.all_to_all(spread, 'dp', 0, 0, axis_index_groups=CHIPS)]
  transfers between devices with their start and end apart: 3 -> 12, of which waited for: 3 -> 11; matrix products, arithmetic and copies ran while one was open for 2% -> 7% of each run, Pallas kernels for 0% -> 0%
where the time goes in v1:
time: 128 us
  waiting for transfers between devices  53.1 us (41%)
  starting transfers between devices  29.3 us (23%)
  other arithmetic  21.4 us (17%)
  matrix products  12.8 us (10%)
  local copies, waits for them, and re-layouts  9.84 us (8%)
    ppermute x3, waiting for transfers between devices, gather_weight(): got = [lax.ppermute(half, 'fsdp', y_shift(k)) for k in (3, 2, 1)]  22.6 us
    concatenate x1, other arithmetic, gather_weight(): ring = jnp.concatenate([kv_weight, rest, kv_weight, rest], axis=0)  17.6 us
    ppermute x3, waiting for transfers between devices, exchange_types(): got.append(lax.ppermute(take((quad + k) % TYPES), 'dp', z_shift(2 * k)))  11.7 us
    all_to_all x1, waiting for transfers between devices, gather_docs(): got = lax.all_to_all(spread, 'dp', 0, 0, axis_index_groups=CHIPS)  11.5 us
    all_to_all x1, starting transfers between devices, gather_docs(): got = lax.all_to_all(spread, 'dp', 0, 0, axis_index_groups=CHIPS)  11 us
    dot_general x1, matrix products, local(): lax.dot_general(grad_keyval.reshape(docs * block, KVW), weight, (((1,), (...  5.98 us
    ppermute x3, starting transfers between devices, exchange_types(): got.append(lax.ppermute(take((quad + k) % TYPES), 'dp', z_shift(2 * k)))  4.87 us
    ppermute x3, starting transfers between devices, gather_weight(): got = [lax.ppermute(half, 'fsdp', y_shift(k)) for k in (3, 2, 1)]  4.68 us
  transfers between devices with their start and end apart: 12, of which 11 were waited for; matrix products, arithmetic and copies ran while one was open for 7% of the time, Pallas kernels for 0%

profile of v1, /device:TPU:1, one launch (start us, length us, event | category | flops | bytes accessed | tf_op | source)
XLA Modules:
  0.0 127.6 jit_solution(2410863181379172590)
XLA Ops:
  0.7 1.1 constant_dynamic-slice_fusion.5
  1.7 3.6 %collective-permute-start = (bf16[896,256]{1,0:T(8,128)(2,1)S(1)}, bf16[896,256]{1,0:T(8,128)(2,1)S(1)}, u32[]{:S(2)}, u32[]{:S(2)}) collective-permute-start(bf16[896,256]{1,0:T(8,128)(2,1)S(1)} %constant_dynamic-slice_fusion.5), channel_id=1, source_target_pairs={{0,3},{1,0},{2,1},{3,2},{4,7},{5,4},{6,5},{7,6},{8,11},{9,8},{10,9... | collective-permute-start | bytes 1376264 | tf_op jit(solution)/shard_map/ppermute | solution.py:61
  5.4 0.3 collective-permute-start.1
  5.7 0.7 collective-permute-start.2
  6.4 17.8 %collective-permute-done = bf16[896,256]{1,0:T(8,128)(2,1)S(1)} collective-permute-done((bf16[896,256]{1,0:T(8,128)(2,1)S(1)}, bf16[896,256]{1,0:T(8,128)(2,1)S(1)}, u32[]{:S(2)}, u32[]{:S(2)}) %collective-permute-start) | collective-permute-done | bytes 458784 | tf_op jit(solution)/shard_map/ppermute | solution.py:61
  24.4 4.8 %collective-permute-done.2 = bf16[896,256]{1,0:T(8,128)(2,1)S(1)} collective-permute-done((bf16[896,256]{1,0:T(8,128)(2,1)S(1)}, bf16[896,256]{1,0:T(8,128)(2,1)S(1)}, u32[]{:S(2)}, u32[]{:S(2)}) %collective-permute-start.2) | collective-permute-done | bytes 458784 | tf_op jit(solution)/shard_map/ppermute | solution.py:61
  29.2 0.8 collective-permute-start.3
  30.1 2.8 %collective-permute-done.3 = bf16[2688,256]{1,0:T(8,128)(2,1)} collective-permute-done((bf16[2688,256]{1,0:T(8,128)(2,1)S(1)}, bf16[2688,256]{1,0:T(8,128)(2,1)}, u32[]{:S(2)}, u32[]{:S(2)}) %collective-permute-start.3) | collective-permute-done | bytes 1376288 | tf_op jit(solution)/shard_map/ppermute | solution.py:63
  32.8 1.5 %broadcast_select_fusion = (bf16[2688,256]{1,0:T(8,128)(2,1)S(1)}, bf16[2688,256]{1,0:T(8,128)(2,1)S(1)}) fusion(bf16[2688,256]{1,0:T(8,128)(2,1)} %collective-permute-done.3, bf16[2688,256]{1,0:T(8,128)(2,1)S(1)} %constant_dynamic-update-slice_fusion, pred[]{:T(512)S(6)} %eq.48), kind=kLoop, calls=%fused_computation.17 | loop fusion | flops 1376256 | bytes 5505025 | tf_op jit(solution)/shard_map/jit(_where)/select_n | solution.py:55
  34.4 17.6 %fusion.4 = bf16[3584,512]{1,0:T(8,128)(2,1)S(1)} fusion(s32[]{:T(128)S(6)} %select_n.126, bf16[896,512]{1,0:T(8,128)(2,1)S(1)} %copy-done.2, bf16[2688,256]{1,0:T(8,128)(2,1)S(1)} %get-tuple-element.9, bf16[2688,256]{1,0:T(8,128)(2,1)S(1)} %get-tuple-element.8), kind=kLoop, calls=%fused_computation.13 | loop fusion | flops 22020096 | bytes 7340036 | tf_op jit(solution)/shard_map/concatenate | solution.py:65
  52.0 1.8 %copy-done.1 = bf16[3584,512]{1,0:T(8,128)(2,1)} copy-done((bf16[3584,512]{1,0:T(8,128)(2,1)}, bf16[3584,512]{1,0:T(8,128)(2,1)S(1)}, u32[]{:S(2)}) %copy-start.1) | copy-done | bytes 3670040
  53.8 2.1 %fusion.9 = bf16[512,512]{0,1:T(8,128)(2,1)S(1)} fusion(bf16[3584,512]{1,0:T(8,128)(2,1)S(1)} %fusion.4, bf16[512,3584]{1,0:T(8,128)(2,1)S(1)} %bitcast.73), kind=kOutput, calls=%fused_computation.22 | convolution fusion | flops 1879310336 | bytes 7864320 | tf_op jit(solution)/shard_map/dot_general | solution.py:148
  56.0 0.4 fusion.49
  56.4 0.2 copy.44
  56.6 0.2 copy.45
  57.0 0.3 multiply_reduce_fusion.2
  57.5 0.5 collective-permute-start.4
  58.0 0.8 collective-permute-done.4
  58.9 0.8 broadcast_in_dim.32
  59.7 11.0 %all-to-all-start = ((bf16[32,4,1024]{2,1,0:T(4,128)(2,1)}), bf16[32,4,1024]{2,1,0:T(4,128)(2,1)S(1)}, u32[]{:S(2)}, u32[]{:S(2)}) async-start(bf16[32,4,1024]{2,1,0:T(4,128)(2,1)} %broadcast_in_dim.32), calls=%async_computation | async-start | bytes 524288 | tf_op jit(solution)/shard_map/all_to_all | solution.py:77
  70.9 11.5 %all-to-all-done = bf16[32,4,1024]{2,1,0:T(4,128)(2,1)S(1)} async-done(((bf16[32,4,1024]{2,1,0:T(4,128)(2,1)}), bf16[32,4,1024]{2,1,0:T(4,128)(2,1)S(1)}, u32[]{:S(2)}, u32[]{:S(2)}) %all-to-all-start) | async-done | bytes 262176 | tf_op jit(solution)/shard_map/all_to_all | solution.py:77
  82.4 2.4 %collective-permute-start.5 = (bf16[128,1024]{1,0:T(8,128)(2,1)S(1)}, bf16[128,1024]{1,0:T(8,128)(2,1)S(1)}, u32[]{:S(2)}, u32[]{:S(2)}) collective-permute-start(bf16[128,1024]{1,0:T(8,128)(2,1)S(1)} %reshape.161), channel_id=1, source_target_pairs={{0,4},{4,0},{8,12},{12,8},{16,20},{20,16},{24,28},{28,24},{32,36},... | collective-permute-start | bytes 786440 | tf_op jit(solution)/shard_map/ppermute | solution.py:79
  84.8 0.3 fusion.33
  85.1 0.8 collective-permute-done.5
  86.2 0.3 fusion.27
  86.8 0.2 fusion.19
  87.6 2.7 %fusion.1 = bf16[2,2,2,7,3584]{4,3,1,0,2:T(8,128)(2,1)S(1)} fusion(bf16[1,2,256,3584]{3,2,1,0:T(8,128)(2,1)} %param.5, bf16[2,1,2,7,256]{4,3,2,0,1:T(8,128)(2,1)S(1)} %convert_bitcast_fusion, bf16[2,1,2,7,256]{4,3,2,0,1:T(8,128)(2,1)S(1)} %bitcast.74), kind=kOutput, calls=%fused_computation.10 | convolution fusion | flops 102975488 | bytes 4100096 | tf_op jit(solution)/shard_map/ntkgr,nrw->tkngw/dot_general | solution.py:171
  90.5 0.3 copy.37
  91.0 1.1 pad_dynamic-slice_fusion.6
  92.2 0.9 collective-permute-start.6
  93.1 2.0 %collective-permute-start.7 = (bf16[16,3712]{1,0:T(8,128)(2,1)S(1)}, bf16[16,3712]{1,0:T(8,128)(2,1)S(1)}, u32[]{:S(2)}, u32[]{:S(2)}) collective-permute-start(bf16[16,3712]{1,0:T(8,128)(2,1)S(1)} %bitcast.77), channel_id=1, source_target_pairs={{0,128},{4,132},{8,136},{12,140},{16,144},{20,148},{24,152},{28,15... | collective-permute-start | bytes 356360 | tf_op jit(solution)/shard_map/ppermute | solution.py:121
  95.2 1.9 %collective-permute-start.8 = (bf16[16,3712]{1,0:T(8,128)(2,1)S(1)}, bf16[16,3712]{1,0:T(8,128)(2,1)S(1)}, u32[]{:S(2)}, u32[]{:S(2)}) collective-permute-start(bf16[16,3712]{1,0:T(8,128)(2,1)S(1)} %bitcast.78), channel_id=1, source_target_pairs={{0,192},{4,196},{8,200},{12,204},{16,208},{20,212},{24,216},{28,22... | collective-permute-start | bytes 356360 | tf_op jit(solution)/shard_map/ppermute | solution.py:121
  97.1 0.3 fusion.8
  97.4 4.6 %collective-permute-done.6 = bf16[16,3712]{1,0:T(8,128)(2,1)S(1)} collective-permute-done((bf16[16,3712]{1,0:T(8,128)(2,1)S(1)}, bf16[16,3712]{1,0:T(8,128)(2,1)S(1)}, u32[]{:S(2)}, u32[]{:S(2)}) %collective-permute-start.6) | collective-permute-done | bytes 118816 | tf_op jit(solution)/shard_map/ppermute | solution.py:121
  102.0 1.6 %collective-permute-done.7 = bf16[16,3712]{1,0:T(8,128)(2,1)S(1)} collective-permute-done((bf16[16,3712]{1,0:T(8,128)(2,1)S(1)}, bf16[16,3712]{1,0:T(8,128)(2,1)S(1)}, u32[]{:S(2)}, u32[]{:S(2)}) %collective-permute-start.7) | collective-permute-done | bytes 118816 | tf_op jit(solution)/shard_map/ppermute | solution.py:121
  103.6 5.5 %collective-permute-done.8 = bf16[16,3712]{1,0:T(8,128)(2,1)S(1)} collective-permute-done((bf16[16,3712]{1,0:T(8,128)(2,1)S(1)}, bf16[16,3712]{1,0:T(8,128)(2,1)S(1)}, u32[]{:S(2)}, u32[]{:S(2)}) %collective-permute-start.8) | collective-permute-done | bytes 118816 | tf_op jit(solution)/shard_map/ppermute | solution.py:121
  109.2 0.9 collective-permute-start.9
  110.2 1.4 %collective-permute-done.9 = bf16[64,3712]{1,0:T(8,128)(2,1)S(1)} collective-permute-done((bf16[64,3712]{1,0:T(8,128)(2,1)S(1)}, bf16[64,3712]{1,0:T(8,128)(2,1)S(1)}, u32[]{:S(2)}, u32[]{:S(2)}) %collective-permute-start.9) | collective-permute-done | bytes 475168 | tf_op jit(solution)/shard_map/ppermute | solution.py:127
  111.8 0.3 convolution_convert_fusion.2
  112.1 1.0 reshape.166
  113.0 4.1 %all-to-all-start.1 = ((bf16[32,2,3584]{2,1,0:T(2,128)(2,1)}), bf16[32,2,3584]{2,1,0:T(2,128)(2,1)S(1)}, u32[]{:S(2)}, u32[]{:S(2)}) async-start(bf16[32,2,3584]{2,1,0:T(2,128)(2,1)} %reshape.166), calls=%async_computation.1 | async-start | bytes 917504 | tf_op jit(solution)/shard_map/all_to_all | solution.py:135
  117.3 0.6 convert_element_type.92
  117.9 0.4 copy.34
  118.4 0.2 reshape.162
  118.6 0.6 dynamic-slice_bitcast_fusion
  119.2 6.0 %convolution_convert_fusion = bf16[512,3584]{1,0:T(8,128)(2,1)} fusion(bf16[512,512]{1,0:T(8,128)(2,1)S(1)} %reshape.162, bf16[3584,512]{1,0:T(8,128)(2,1)} %copy-done.1), kind=kOutput, calls=%fused_computation.7 | convolution fusion | flops 1880883200 | bytes 7864320 | tf_op jit(solution)/shard_map/dot_general | solution.py:181
  125.1 1.5 %all-to-all-done.1 = bf16[32,2,3584]{2,1,0:T(2,128)(2,1)S(1)} async-done(((bf16[32,2,3584]{2,1,0:T(2,128)(2,1)}), bf16[32,2,3584]{2,1,0:T(2,128)(2,1)S(1)}, u32[]{:S(2)}, u32[]{:S(2)}) %all-to-all-start.1) | async-done | bytes 458784 | tf_op jit(solution)/shard_map/all_to_all | solution.py:135
  126.6 1.0 convert_reduce_fusion
  (64 shorter events, 2.7 us)
Async XLA Ops:
  0.6 29.3 %copy-start.3 = (bf16[1,2,1792]{2,1,0:T(2,128)(2,1)S(1)}, bf16[1,2,1792]{2,1,0:T(2,128)(2,1)}, u32[]{:S(2)}) copy-start(bf16[1,2,1792]{2,1,0:T(2,128)(2,1)} %param.7) | copy-start | bytes 21508
  0.6 29.3 %copy-start.4 = (s32[1,2]{1,0:T(1,128)S(1)}, s32[1,2]{1,0:T(1,128)}, u32[]{:S(2)}) copy-start(s32[1,2]{1,0:T(1,128)} %param.8) | copy-start | bytes 28
  0.7 29.4 %copy-start.5 = (s32[1,2]{1,0:T(1,128)S(1)}, s32[1,2]{1,0:T(1,128)}, u32[]{:S(2)}) copy-start(s32[1,2]{1,0:T(1,128)} %param.6) | copy-start | bytes 28
  1.7 22.5 %collective-permute-start = (bf16[896,256]{1,0:T(8,128)(2,1)S(1)}, bf16[896,256]{1,0:T(8,128)(2,1)S(1)}, u32[]{:S(2)}, u32[]{:S(2)}) collective-permute-start(bf16[896,256]{1,0:T(8,128)(2,1)S(1)} %constant_dynamic-slice_fusion.5), channel_id=1, source_target_pairs={{0,3},{1,0},{2,1},{3,2},{4,7},{5,4},{6,5},{7,6},{8,11},{9,8},{10,9... | collective-permute-start | bytes 1376264 | tf_op jit(solution)/shard_map/ppermute | solution.py:61
  5.4 18.9 %collective-permute-start.1 = (bf16[896,256]{1,0:T(8,128)(2,1)S(1)}, bf16[896,256]{1,0:T(8,128)(2,1)S(1)}, u32[]{:S(2)}, u32[]{:S(2)}) collective-permute-start(bf16[896,256]{1,0:T(8,128)(2,1)S(1)} %constant_dynamic-slice_fusion.5), channel_id=1, source_target_pairs={{0,2},{1,3},{2,0},{3,1},{4,6},{5,7},{6,4},{7,5},{8,10},{9,11},{10,... | collective-permute-start | bytes 1376264 | tf_op jit(solution)/shard_map/ppermute | solution.py:61
  5.7 23.4 %collective-permute-start.2 = (bf16[896,256]{1,0:T(8,128)(2,1)S(1)}, bf16[896,256]{1,0:T(8,128)(2,1)S(1)}, u32[]{:S(2)}, u32[]{:S(2)}) collective-permute-start(bf16[896,256]{1,0:T(8,128)(2,1)S(1)} %constant_dynamic-slice_fusion.5), channel_id=1, source_target_pairs={{0,1},{1,2},{2,3},{3,0},{4,5},{5,6},{6,7},{7,4},{8,9},{9,10},{10,1... | collective-permute-start | bytes 1376264 | tf_op jit(solution)/shard_map/ppermute | solution.py:61
  24.3 10.1 %copy-start.2 = (bf16[896,512]{1,0:T(8,128)(2,1)S(1)}, bf16[896,512]{1,0:T(8,128)(2,1)}, u32[]{:S(2)}) copy-start(bf16[896,512]{1,0:T(8,128)(2,1)} %param.9) | copy-start | bytes 2752516
  29.2 3.6 %collective-permute-start.3 = (bf16[2688,256]{1,0:T(8,128)(2,1)S(1)}, bf16[2688,256]{1,0:T(8,128)(2,1)}, u32[]{:S(2)}, u32[]{:S(2)}) collective-permute-start(bf16[2688,256]{1,0:T(8,128)(2,1)S(1)} %constant_dynamic-update-slice_fusion), channel_id=1, source_target_pairs={{0,4},{4,0},{8,12},{12,8},{16,20},{20,16},{24,28},{28,24},{32,36},... | collective-permute-start | bytes 4128776 | tf_op jit(solution)/shard_map/ppermute | solution.py:63
  34.4 19.4 %copy-start = (bf16[1,2,256,3584]{3,2,1,0:T(8,128)(2,1)S(1)}, bf16[1,2,256,3584]{3,2,1,0:T(8,128)(2,1)}, u32[]{:S(2)}) copy-start(bf16[1,2,256,3584]{3,2,1,0:T(8,128)(2,1)} %param.5) | copy-start | bytes 11010052
  52.0 1.8 %copy-start.1 = (bf16[3584,512]{1,0:T(8,128)(2,1)}, bf16[3584,512]{1,0:T(8,128)(2,1)S(1)}, u32[]{:S(2)}) copy-start(bf16[3584,512]{1,0:T(8,128)(2,1)S(1)} %fusion.4) | copy-start | bytes 11010052
  57.5 1.3 %collective-permute-start.4 = (bf16[2,2048]{1,0:T(2,128)(2,1)S(1)}, bf16[2,2048]{1,0:T(2,128)(2,1)S(1)}, u32[]{:S(2)}, u32[]{:S(2)}) collective-permute-start(bf16[2,2048]{1,0:T(2,128)(2,1)S(1)} %pad_maximum_fusion.7), channel_id=1, source_target_pairs={{0,4},{4,0},{8,12},{12,8},{16,20},{20,16},{24,28},{28,24},{32,36},... | collective-permute-start | bytes 24584 | tf_op jit(solution)/shard_map/ppermute | solution.py:72
  59.7 22.7 %all-to-all-start = ((bf16[32,4,1024]{2,1,0:T(4,128)(2,1)}), bf16[32,4,1024]{2,1,0:T(4,128)(2,1)S(1)}, u32[]{:S(2)}, u32[]{:S(2)}) async-start(bf16[32,4,1024]{2,1,0:T(4,128)(2,1)} %broadcast_in_dim.32), calls=%async_computation | async-start | bytes 524288 | tf_op jit(solution)/shard_map/all_to_all | solution.py:77
  82.4 3.5 %collective-permute-start.5 = (bf16[128,1024]{1,0:T(8,128)(2,1)S(1)}, bf16[128,1024]{1,0:T(8,128)(2,1)S(1)}, u32[]{:S(2)}, u32[]{:S(2)}) collective-permute-start(bf16[128,1024]{1,0:T(8,128)(2,1)S(1)} %reshape.161), channel_id=1, source_target_pairs={{0,4},{4,0},{8,12},{12,8},{16,20},{20,16},{24,28},{28,24},{32,36},... | collective-permute-start | bytes 786440 | tf_op jit(solution)/shard_map/ppermute | solution.py:79
  92.2 9.8 %collective-permute-start.6 = (bf16[16,3712]{1,0:T(8,128)(2,1)S(1)}, bf16[16,3712]{1,0:T(8,128)(2,1)S(1)}, u32[]{:S(2)}, u32[]{:S(2)}) collective-permute-start(bf16[16,3712]{1,0:T(8,128)(2,1)S(1)} %bitcast.76), channel_id=1, source_target_pairs={{0,64},{4,68},{8,72},{12,76},{16,80},{20,84},{24,88},{28,92},{32,9... | collective-permute-start | bytes 356360 | tf_op jit(solution)/shard_map/ppermute | solution.py:121
  93.1 10.5 %collective-permute-start.7 = (bf16[16,3712]{1,0:T(8,128)(2,1)S(1)}, bf16[16,3712]{1,0:T(8,128)(2,1)S(1)}, u32[]{:S(2)}, u32[]{:S(2)}) collective-permute-start(bf16[16,3712]{1,0:T(8,128)(2,1)S(1)} %bitcast.77), channel_id=1, source_target_pairs={{0,128},{4,132},{8,136},{12,140},{16,144},{20,148},{24,152},{28,15... | collective-permute-start | bytes 356360 | tf_op jit(solution)/shard_map/ppermute | solution.py:121
  95.2 13.9 %collective-permute-start.8 = (bf16[16,3712]{1,0:T(8,128)(2,1)S(1)}, bf16[16,3712]{1,0:T(8,128)(2,1)S(1)}, u32[]{:S(2)}, u32[]{:S(2)}) collective-permute-start(bf16[16,3712]{1,0:T(8,128)(2,1)S(1)} %bitcast.78), channel_id=1, source_target_pairs={{0,192},{4,196},{8,200},{12,204},{16,208},{20,212},{24,216},{28,22... | collective-permute-start | bytes 356360 | tf_op jit(solution)/shard_map/ppermute | solution.py:121
  109.2 2.4 %collective-permute-start.9 = (bf16[64,3712]{1,0:T(8,128)(2,1)S(1)}, bf16[64,3712]{1,0:T(8,128)(2,1)S(1)}, u32[]{:S(2)}, u32[]{:S(2)}) collective-permute-start(bf16[64,3712]{1,0:T(8,128)(2,1)S(1)} %pad_maximum_fusion.1), channel_id=1, source_target_pairs={{0,4},{4,0},{8,12},{12,8},{16,20},{20,16},{24,28},{28,24},{32,36},... | collective-permute-start | bytes 1425416 | tf_op jit(solution)/shard_map/ppermute | solution.py:127
  113.0 13.6 %all-to-all-start.1 = ((bf16[32,2,3584]{2,1,0:T(2,128)(2,1)}), bf16[32,2,3584]{2,1,0:T(2,128)(2,1)S(1)}, u32[]{:S(2)}, u32[]{:S(2)}) async-start(bf16[32,2,3584]{2,1,0:T(2,128)(2,1)} %reshape.166), calls=%async_computation.1 | async-start | bytes 917504 | tf_op jit(solution)/shard_map/all_to_all | solution.py:135

commit v2 on v1

v2 whole, which is shorter than its diff:
```python
import jax
import jax.numpy as jnp
from jax import lax
from jax.experimental import pallas as pl
from jax.experimental.pallas import tpu as pltpu
from jax.sharding import PartitionSpec as P

QH = 14
KVH = 2
GRP = QH // KVH
SLOT = 8
HD = 128
QW = QH * HD
KVW = 2 * KVH * HD
HALF = QW // 2
TYPES = 2 * KVH
DOCS = 2
SIDE = DOCS * SLOT
ROWS = KVH * SIDE
SOFTMAX_TEMPER = 0.05

NZ, NX, NC, NY = 8, 4, 2, 4
N_DP = NZ * NX * NC

F32 = jnp.float32
BF16 = jnp.bfloat16


def dp_index(z, x, c):
    return (z * NX + x) * NC + c


OTHER_CORE = [(i, i ^ 1) for i in range(N_DP)]
X_MATE = [(i, i ^ NC) for i in range(N_DP)]


Y_ACROSS = [(i, (i + 2) % NY) for i in range(NY)]


def y_mirror():
    return [
        (dp * NY + y, dp * NY + (y + (1 if dp % NC else NY - 1)) % NY)
        for dp in range(N_DP)
        for y in range(NY)
    ]


def plane_shift(dz=0, dx=0, mirror=False):
    pairs = []
    for z in range(NZ):
        for x in range(NX):
            for c in range(NC):
                sign = -1 if mirror and c == 0 else 1
                to = dp_index((z + sign * dz) % NZ, (x + sign * dx) % NX, c)
                pairs.append((dp_index(z, x, c), to))
    return pairs


OWNERS = [
    [
        dp_index(2 * t + p, x, c) * NY + y
        for p in range(2)
        for x in range(NX)
        for y in range(NY)
    ]
    for t in range(TYPES)
    for c in range(NC)
]


def parity_shift(k):
    pairs = []
    for z in range(NZ):
        to = (z + (k if z % 2 == 0 else -k)) % NZ
        pairs += [(dp_index(z, x, c), dp_index(to, x, c)) for x in range(NX) for c in range(NC)]
    return pairs


def dot_nn(a, b):
    return jnp.dot(a, b, preferred_element_type=F32)


def tie(a, *after):
    return lax.optimization_barrier((a, *after))[0]


def dot_tn(a, b):
    return lax.dot_general(a, b, (((0,), (0,)), ((), ())), preferred_element_type=F32)


def dot_nt(a, b):
    return lax.dot_general(a, b, (((1,), (1,)), ((), ())), preferred_element_type=F32)


def call(body, scalars, arrays, outs, scratch=(), flops=0):
    smem = [pl.BlockSpec(memory_space=pltpu.SMEM)] * len(scalars)
    vmem = [pl.BlockSpec(memory_space=pltpu.VMEM)] * len(arrays)
    return pl.pallas_call(
        body,
        out_shape=[jax.ShapeDtypeStruct(s, d) for s, d in outs],
        in_specs=smem + vmem,
        out_specs=[pl.BlockSpec(memory_space=pltpu.VMEM)] * len(outs),
        scratch_shapes=list(scratch),
        compiler_params=pltpu.CompilerParams(vmem_limit_bytes=20 * 1024 * 1024),
        cost_estimate=pl.CostEstimate(flops=flops, bytes_accessed=0, transcendentals=0),
    )(*scalars, *arrays)


def row_mask(lens, block):
    rows = lax.broadcasted_iota(jnp.int32, (ROWS, DOCS * block), 0)
    cols = lax.broadcasted_iota(jnp.int32, (ROWS, DOCS * block), 1)
    row_doc = (rows // SLOT) % DOCS
    length = jnp.where(row_doc == 0, lens[0], lens[1])
    at = cols - row_doc * block
    return (at >= 0) & (at < length)


def block_at(place, k, shard):
    return pl.multiple_of(lax.rem(place[0] + k, NY) * shard, shard)


def near_at(place, shard):
    return block_at(place, jnp.where(place[1] == 0, 1, NY - 1), shard)


def near_other_at(place, shard):
    return block_at(place, jnp.where(place[1] == 0, NY - 1, 1), shard)


def across_block(place, mine, mate, other, other_mate):
    low, first = place[3] == 0, place[1] == 0
    a = [jnp.where(low, mine[...], mate[...]), jnp.where(low, mate[...], mine[...])]
    b = [jnp.where(low, other[...], other_mate[...]), jnp.where(low, other_mate[...], other[...])]
    keys = [jnp.where(first, p, q) for p, q in zip(a, b)]
    values = [jnp.where(first, q, p) for p, q in zip(a, b)]
    return jnp.concatenate(keys + values, axis=1)


def own_body(place, tokens, weight, queries, out, rows, flat):
    shard = weight.shape[0]
    out[...] = dot_nn(tokens[:, pl.ds(block_at(place, 0, shard), shard)], weight[...])
    from_lanes(queries[...].astype(F32), flat)
    rows[...] = flat[...].astype(BF16)


def near_body(place, tokens, weight, before, out):
    shard = weight.shape[0]
    part = dot_nn(tokens[:, pl.ds(near_at(place, shard), shard)], weight[...])
    out[...] = before[...] + part


def from_lanes(a, out):
    out[...] = jnp.zeros_like(out)
    for kvh in range(KVH):
        for doc in range(DOCS):
            for g in range(GRP):
                i = kvh * GRP + g
                r = kvh * SIDE + doc * SLOT + g
                out[r : r + 1, :] = a[doc : doc + 1, i * HD : (i + 1) * HD]


def to_lanes(rows, kvh, out):
    for doc in range(DOCS):
        for g in range(GRP):
            head = kvh * GRP + g
            r = doc * SLOT + g
            out[doc : doc + 1, head * HD : (head + 1) * HD] = rows[r : r + 1]


def head(a, i):
    return a[:, i * HD : (i + 1) * HD]


def attend_body(
    place, lens, marks, tokens, before, near_other, w0, w1, w2, w3, queries,
    keyval, attn, packed, unit, norm, flat,
):
    shard = near_other.shape[0]
    blocks = [
        (near_other_at(place, shard), near_other[...]),
        (block_at(place, 2, shard), across_block(place, w0, w1, w2, w3)),
    ]
    total = before[...]
    for at, block in blocks:
        total += dot_nn(tokens[:, pl.ds(at, shard)], block)
    both = total.astype(BF16)
    keyval[...] = both
    scores = jnp.concatenate(
        [dot_nt(queries[h * SIDE : (h + 1) * SIDE, :], head(both, h)) for h in range(KVH)], axis=0
    ) * HD ** (-0.5)
    mask = row_mask(lens, both.shape[0] // DOCS)
    expvals = jnp.where(mask, jnp.exp(jnp.where(mask, scores, 0.0)), 0.0)
    probs = expvals / jnp.sum(expvals, axis=-1, keepdims=True)
    attn[...] = probs
    probs = probs.astype(BF16)
    flat[...] = jnp.zeros_like(flat)
    for h in range(KVH):
        to_lanes(dot_nn(probs[h * SIDE : (h + 1) * SIDE], head(both, KVH + h)), h, flat)
    readout = flat[...]
    length = jnp.sqrt(jnp.sum(readout * readout, axis=-1, keepdims=True) + 1e-06)
    vec = readout / length
    unit[...] = vec
    norm[...] = jnp.broadcast_to(length, norm.shape)
    emb = vec.astype(BF16)
    doc_at = lax.broadcasted_iota(jnp.int32, (SLOT, HD), 0)
    mark = jnp.where(doc_at == 0, marks[0], marks[1]).astype(F32).astype(BF16)
    whole = jnp.concatenate([emb[:, :HALF], mark, emb[:, HALF:], mark], axis=1)
    packed[...] = whole[:DOCS]


def mix_body(tokens, attn, mixed):
    mixed[...] = dot_nn(attn[...].astype(BF16), tokens[...]).astype(BF16)


def backward_body(
    place, tokens, attn, mixed, queries, keyval, unit, norm,
    ring, e0, e1, e2, e3, f0, f1, f2, f3,
    loss, grad_score, grad_rows, grad_query, factors, flat, lanes,
):
    first = place[1] == 0
    gathered = join_docs(first, ring, (e0, e1, e2, e3), (f0, f1, f2, f3))
    span = HALF + HD
    everyone = jnp.concatenate([gathered[:, :HALF], gathered[:, span : span + HALF]], axis=1)
    total_docs = everyone.shape[0]
    marks = gathered[:, HALF:span].astype(F32)
    ids = lax.broadcasted_iota(jnp.int32, (total_docs, total_docs), 0)
    cols = lax.broadcasted_iota(jnp.int32, (total_docs, total_docs), 1)
    sim = dot_nt(everyone, everyone) / SOFTMAX_TEMPER
    sim_exp = jnp.where(ids == cols, 0.0, jnp.exp(sim))
    total = jnp.sum(sim_exp, axis=-1, keepdims=True)
    picked = marks == doc_ids(place, cols).astype(F32)
    all_loss = jnp.log(total) - jnp.sum(jnp.where(picked, sim, 0.0), axis=-1, keepdims=True)
    prob = (sim_exp / total).astype(BF16)
    pick = jnp.where(picked, 1.0, 0.0).astype(BF16)
    at = place[1] * DOCS
    slots = lax.broadcasted_iota(jnp.int32, (SLOT, total_docs), 0)
    here = lax.broadcasted_iota(jnp.int32, (SLOT, total_docs), 1)
    chosen = (here == at + slots) & (slots < DOCS)
    own_rows = jnp.where(chosen, 1.0, 0.0).astype(BF16)
    lane = lax.broadcasted_iota(jnp.int32, (total_docs, HD), 0)
    slot = lax.broadcasted_iota(jnp.int32, (total_docs, HD), 1)
    loss[...] = jnp.sum(jnp.where(lane == at + slot, all_loss, 0.0), axis=0, keepdims=True)
    coef = jnp.concatenate(
        [
            dot_nn(own_rows, prob),
            dot_nt(own_rows, prob),
            dot_nn(own_rows, pick),
            dot_nt(own_rows, pick),
        ],
        axis=0,
    ).astype(BF16)
    parts = dot_nn(coef, everyone)
    grad_unit = (parts[:8] + parts[8:16] - parts[16:24] - parts[24:]) / SOFTMAX_TEMPER
    vec = unit[...]
    along = jnp.sum(vec * grad_unit, axis=-1, keepdims=True)
    grad_read = (grad_unit - vec * along) / norm[:, :1]
    from_lanes(grad_read, flat)
    heads = flat[...].astype(BF16)
    grad_rows[...] = heads
    sides = [slice(h * SIDE, (h + 1) * SIDE) for h in range(KVH)]
    grad_w = jnp.concatenate(
        [dot_nt(heads[sides[h]], head(keyval, KVH + h)) for h in range(KVH)], axis=0
    )
    probs = attn[...]
    inner = jnp.sum(probs * grad_w, axis=-1, keepdims=True)
    score = (probs * (grad_w - inner) * HD ** (-0.5)).astype(BF16)
    grad_score[...] = score
    for h in range(KVH):
        to_lanes(dot_nn(score[sides[h]], head(keyval, h)), h, lanes)
    grad_query[...] = lanes[:DOCS, :].astype(BF16)
    wide = GRP * HD
    slot_rows = lax.broadcasted_iota(jnp.int32, (SIDE, wide), 0)
    halves = [dot_nn(score, tokens[...]), mixed[...].astype(F32)]
    tails = [queries[...].astype(F32), grad_read]
    for kind in range(2):
        for h in range(KVH):
            tail = tails[kind][:, h * wide : (h + 1) * wide]
            tail = jnp.where(slot_rows < SLOT, tail[0:1], tail[1:2])
            part = halves[kind][sides[h]]
            joined = jnp.where(slot_rows % SLOT == GRP, tail, part[:, :wide])
            factors[kind * KVH + h, :, :wide] = joined.astype(BF16)
            factors[kind * KVH + h, :, wide:] = part[:, wide:].astype(BF16)


def token_body(
    place, grad_score, attn, query_rows, grad_rows, own, near, near_other, w0, w1, w2, w3, out, done
):
    shard = own.shape[0]
    probs = attn[...].astype(BF16)
    sides = [slice(h * SIDE, (h + 1) * SIDE) for h in range(KVH)]
    parts = [dot_tn(grad_score[s, :], query_rows[s, :]) for s in sides]
    parts += [dot_tn(probs[s], grad_rows[s, :]) for s in sides]
    grad_keyval = jnp.concatenate(parts, axis=1).astype(BF16)
    blocks = [
        (block_at(place, 0, shard), own[...]),
        (near_at(place, shard), near[...]),
        (near_other_at(place, shard), near_other[...]),
        (block_at(place, 2, shard), across_block(place, w0, w1, w2, w3)),
    ]
    for at, block in blocks:
        out[:, pl.ds(at, shard)] = dot_nt(grad_keyval, block).astype(BF16)
    done[...] = probs[:SLOT, :HD].astype(F32)


def chip_body(place, mine, other, chip, half):
    first = place[1] == 0
    a, b = mine[...].astype(F32), other[...].astype(F32)
    whole = jnp.concatenate([jnp.where(first, a, b), jnp.where(first, b, a)], axis=0).astype(BF16)
    chip[...] = whole
    width = half.shape[1]
    half[...] = jnp.where(first, whole[:, :width], whole[:, width:])


def ring_body(place, chip, near, far, near_other, far_other, ring, half):
    first = place[1] == 0
    a, b = near[...].astype(F32), near_other[...].astype(F32)
    c, d = far[...].astype(F32), far_other[...].astype(F32)
    plus, minus = jnp.where(first, a, b), jnp.where(first, b, a)
    across = jnp.concatenate([jnp.where(first, c, d), jnp.where(first, d, c)], axis=1)
    whole = jnp.concatenate([chip[...].astype(F32), plus, across, minus], axis=0).astype(BF16)
    ring[...] = whole
    width = half.shape[1]
    half[...] = jnp.where(first, whole[:, :width], whole[:, width:])


def gather_docs(packed, place, before_ring):
    docs, wide = packed.shape
    swap = lambda a: lax.ppermute(a, "dp", OTHER_CORE)
    count = NC * docs
    chip, half = call(
        chip_body, (place,), (packed, swap(packed)),
        [((count, wide), BF16), ((count, wide // 2), BF16)],
    )
    near = lax.ppermute(chip, "dp", plane_shift(dx=1, mirror=True))
    far = lax.ppermute(half, "dp", plane_shift(dx=2))
    far = tie(far, before_ring)
    count *= NX
    ring, half = call(
        ring_body, (place,), (chip, near, far, swap(near), swap(far)),
        [((count, wide), BF16), ((count, wide // 2), BF16)],
    )
    blocks = [lax.ppermute(ring, "dp", plane_shift(dz=k, mirror=True)) for k in (1, 2, 3)]
    blocks.append(lax.ppermute(half, "dp", plane_shift(dz=4)))
    return (ring, *blocks, *[swap(a) for a in blocks])


def join_docs(first, ring, blocks, others):
    pairs = [(a[...], b[...]) for a, b in zip(blocks, others)]
    plus = [jnp.where(first, a, b) for a, b in pairs]
    minus = [jnp.where(first, b, a) for a, b in pairs]
    across = jnp.concatenate([plus[3], minus[3]], axis=1)
    return jnp.concatenate(
        [ring[...], plus[0], plus[1], plus[2], across, minus[2], minus[1], minus[0]], axis=0
    )


def doc_ids(place, slots):
    dp = place[2] // DOCS
    z, x = dp // (NX * NC), (dp // NC) % NX
    count = NC * DOCS
    at_z = (z + slots // (NX * count)) % NZ
    at_x = (x + (slots // count) % NX) % NX
    return (at_z * NX + at_x) * count + slots % count


def outer_body(place, a0, a1, a2, a3, b0, b1, b2, b3, out):
    rows = jnp.concatenate([a[...] for a in (a0, a1, a2, a3, b0, b1, b2, b3)], axis=0)
    count = rows.shape[0]
    to = lax.broadcasted_iota(jnp.int32, (count, count), 0)
    at = lax.broadcasted_iota(jnp.int32, (count, count), 1)
    spread = jnp.where(at == (to // SLOT) * SLOT + GRP, 1.0, 0.0).astype(BF16)
    tails = dot_nn(spread, rows[:, : GRP * HD])
    slot = lax.broadcasted_iota(jnp.int32, (count, HD), 0) % SLOT
    heads = jnp.zeros((count, HD), F32)
    for g in range(GRP):
        heads = jnp.where(slot == g, tails[:, g * HD : (g + 1) * HD], heads)
    slots = lax.broadcasted_iota(jnp.int32, (HD // NC, HD), 0)
    cols = lax.broadcasted_iota(jnp.int32, (HD // NC, HD), 1)
    cell = HD // (2 * NX * NC)
    chosen = cols == ((slots // cell) * NC + place[1]) * cell + slots % cell
    chosen = jnp.where(chosen, 1.0, 0.0).astype(BF16)
    left = dot_nt(chosen, heads.astype(BF16)).astype(BF16)
    out[...] = dot_nn(left, rows).astype(BF16)


def exchange_types(factors):
    z = lax.axis_index("dp") // (NX * NC)
    sign = 1 - 2 * (z % 2)
    take = lambda to: lax.dynamic_index_in_dim(factors, (to % NZ) // 2, 0, keepdims=False)
    quads = [take(z)]
    for k in (-1, -3, 2):
        quads.append(lax.ppermute(take(z + NZ + sign * k), "dp", parity_shift(k)))
    return quads


def reduce_weight(quads, place):
    swapped = [lax.ppermute(a, "dp", OTHER_CORE) for a in quads]
    width = quads[0].shape[1]
    (part,) = call(outer_body, (place,), (*quads, *swapped), [((HD // NC, width), BF16)])
    pieces = part.reshape(2 * NX * NY, -1, width)
    got = lax.all_to_all(pieces, ("dp", "fsdp"), 0, 0, axis_index_groups=OWNERS)
    return jnp.sum(got.astype(F32), axis=0).T


def local(tokens, lengths, queries, positives, kv_weight):
    docs, block, width = tokens.shape[1:]
    shard = kv_weight.shape[0]
    count = docs * block
    dp = lax.axis_index("dp")
    core = dp % NC
    parity = (dp // NC) % 2
    y = lax.axis_index("fsdp")
    place = jnp.stack([y, core, dp * docs, parity]).astype(jnp.int32)
    rows = tokens.reshape(count, width)
    swap = lambda a: lax.ppermute(a, "dp", OTHER_CORE)

    piece = lax.dynamic_slice(kv_weight, (0, (2 * core + parity) * HD), (shard, HD))
    mine = lax.ppermute(piece, "fsdp", Y_ACROSS)
    near = lax.ppermute(kv_weight, ("dp", "fsdp"), y_mirror())
    mate = lax.ppermute(mine, "dp", X_MATE)

    flops = 2 * count * shard * KVW
    part, query_rows = call(
        own_body, (place,), (rows, kv_weight, queries[0]),
        [((count, KVW), F32), ((ROWS, HD), BF16)], [pltpu.VMEM((ROWS, HD), F32)], flops=flops,
    )
    near = tie(near, mate, part)
    across = (mine, mate, swap(mine), swap(mate))
    near_other = swap(near)
    (part,) = call(near_body, (place,), (rows, near, part), [((count, KVW), F32)], flops=flops)
    keyval, attn, packed, unit, norm = call(
        attend_body,
        (place, lengths[0], positives[0]),
        (rows, part, near_other, *across, query_rows),
        [
            ((count, KVW), BF16),
            ((ROWS, count), F32),
            ((docs, 2 * (HALF + HD)), BF16),
            ((SLOT, QW), F32),
            ((SLOT, HD), F32),
        ],
        [pltpu.VMEM((SLOT, QW), F32)],
        flops=2 * flops,
    )
    (mixed,) = call(
        mix_body, (), (rows, attn), [((ROWS, width), BF16)], flops=2 * ROWS * width * count
    )
    everyone = gather_docs(packed, place, mixed)
    loss, grad_score, grad_rows, grad_query, factors = call(
        backward_body,
        (place,),
        (rows, attn, mixed, queries[0], keyval, unit, norm, *everyone),
        [
            ((1, HD), F32),
            ((ROWS, count), BF16),
            ((ROWS, HD), BF16),
            ((docs, QW), BF16),
            ((TYPES, SIDE, width), BF16),
        ],
        [pltpu.VMEM((ROWS, HD), F32), pltpu.VMEM((SLOT, QW), F32)],
        flops=2 * ROWS * width * count,
    )
    quads = exchange_types(factors)
    grad_tok, done = call(
        token_body,
        (place,),
        (grad_score, attn, query_rows, grad_rows, kv_weight, near, near_other, *across),
        [((count, width), BF16), ((SLOT, HD), F32)],
        flops=4 * flops,
    )
    quads = [quads[0], *[tie(a, done) for a in quads[1:]]]
    grad_weight = reduce_weight(quads, place)
    return (loss[:, :docs], grad_tok.reshape(tokens.shape), grad_query[None], grad_weight)


def solution(mesh):
    placed = (
        P("fsdp", "dp", None, None),
        P("fsdp", "dp"),
        P("fsdp", "dp", None),
        P("fsdp", "dp"),
        P("fsdp", None),
    )
    return jax.shard_map(
        local,
        mesh=mesh,
        in_specs=placed,
        out_specs=(
            P("fsdp", "dp"),
            P("fsdp", "dp", None, None),
            P("fsdp", "dp", None),
            P(None, ("dp", "fsdp")),
        ),
        check_vma=False,
    )
```

time: 128 us -> 103 us (0.80)
  waiting for transfers between devices: 53.1 us -> 23.6 us
  other arithmetic: 21.4 us -> 1.06 us
  Pallas kernels: 0 us -> 15.8 us
  blocking collectives: 0 us -> 13.7 us
  matrix products: 12.8 us -> 0 us
  starting transfers between devices: 29.3 us -> 36.7 us
    ppermute x10 -> x26, starting transfers between devices: 14.1 us -> 36.7 us  [the longest x7 8.84 us: gather_docs(): swap = lambda a: lax.ppermute(a, 'dp', OTHER_CORE)]
    concatenate x5 -> x0, other arithmetic: 17.8 us -> none  [the longest x1 17.6 us: gather_weight(): ring = jnp.concatenate([kv_weight, rest, kv_weight, rest], axis=0)]
    ppermute x10 -> x26, waiting for transfers between devices: 40.2 us -> 23.6 us  [the longest x1 14.8 us: local(): mine = lax.ppermute(piece, 'fsdp', Y_ACROSS)]
    pallas_call x0 -> x9, Pallas kernels: none -> 15.8 us  [call(): pl.pallas_call(body, out_shape=[jax.ShapeDtypeStruct(s, d) for s, d in ou...]
    all_to_all x2 -> x0, starting transfers between devices: 15.2 us -> none  [the longest x1 11 us: gather_docs(): got = lax.all_to_all(spread, 'dp', 0, 0, axis_index_groups=CHIPS)]
    all_to_all x0 -> x1, blocking collectives: none -> 13.7 us  [reduce_weight(): got = lax.all_to_all(pieces, ('dp', 'fsdp'), 0, 0, axis_index_groups=OWNERS)]
    all_to_all x2 -> x0, waiting for transfers between devices: 13 us -> none  [the longest x1 11.5 us: gather_docs(): got = lax.all_to_all(spread, 'dp', 0, 0, axis_index_groups=CHIPS)]
    dot_general x11 -> x0, matrix products: 12.8 us -> none  [the longest x1 5.98 us: local(): lax.dot_general(grad_keyval.reshape(docs * block, KVW), weight, (((1,), (...]
  transfers between devices with their start and end apart: 12 -> 26, of which waited for: 11 -> 10; matrix products, arithmetic and copies ran while one was open for 7% -> 1% of each run, Pallas kernels for 0% -> 8%
where the time goes in v2:
time: 103 us
  starting transfers between devices  36.7 us (36%)
  waiting for transfers between devices  23.6 us (23%)
  Pallas kernels  15.8 us (15%)
  blocking collectives  13.7 us (13%)
  local copies, waits for them, and re-layouts  11 us (11%)
  other arithmetic  1.06 us (1%)
    pallas_call x9, Pallas kernels, call(): pl.pallas_call(body, out_shape=[jax.ShapeDtypeStruct(s, d) for s, d in ou...  15.8 us
    ppermute x1, waiting for transfers between devices, local(): mine = lax.ppermute(piece, 'fsdp', Y_ACROSS)  14.8 us
    all_to_all x1, blocking collectives, reduce_weight(): got = lax.all_to_all(pieces, ('dp', 'fsdp'), 0, 0, axis_index_groups=OWNERS)  13.7 us
    unnamed x50, local copies, waits for them, and re-layouts  9.84 us
    ppermute x7, starting transfers between devices, gather_docs(): swap = lambda a: lax.ppermute(a, 'dp', OTHER_CORE)  8.84 us
    ppermute x3, starting transfers between devices, gather_docs(): lax.ppermute(ring, 'dp', plane_shift(dz=k, mirror=True))  8.47 us
    ppermute x3, starting transfers between devices, exchange_types(): quads.append(lax.ppermute(take(z + NZ + sign * k), 'dp', parity_shift(k)))  6.89 us
    ppermute x7, waiting for transfers between devices, gather_docs(): swap = lambda a: lax.ppermute(a, 'dp', OTHER_CORE)  2.87 us
  transfers between devices with their start and end apart: 26, of which 10 were waited for; matrix products, arithmetic and copies ran while one was open for 1% of the time, Pallas kernels for 8%

profile of v2, /device:TPU:1, one launch (start us, length us, event | category | flops | bytes accessed | tf_op | source)
XLA Modules:
  0.0 102.8 jit_solution(15625822172849395982)
XLA Ops:
  0.6 2.2 %collective-permute-start = (bf16[896,512]{1,0:T(8,128)(2,1)}, bf16[896,512]{1,0:T(8,128)(2,1)S(1)}, u32[]{:S(2)}, u32[]{:S(2)}) collective-permute-start(bf16[896,512]{1,0:T(8,128)(2,1)} %own.1), channel_id=1, source_target_pairs={{0,3},{1,0},{2,1},{3,2},{4,5},{5,6},{6,7},{7,4},{8,11},{9,8},{10,9... | collective-permute-start | bytes 2752520 | tf_op jit(solution)/shard_map/ppermute | solution.py:419
  2.8 1.0 constant_dynamic-slice_fusion
  3.8 2.7 %collective-permute-start.1 = (bf16[896,128]{1,0:T(8,128)(2,1)S(1)}, bf16[896,128]{1,0:T(8,128)(2,1)S(1)}, u32[]{:S(2)}, u32[]{:S(2)}) collective-permute-start(bf16[896,128]{1,0:T(8,128)(2,1)S(1)} %constant_dynamic-slice_fusion), channel_id=1, source_target_pairs={{0,2},{1,3},{2,0},{3,1},{4,6},{5,7},{6,4},{7,5},{8,10},{9,11},{10,... | collective-permute-start | bytes 688136 | tf_op jit(solution)/shard_map/ppermute | solution.py:418
  6.5 14.8 %collective-permute-done.1.w0 = bf16[896,128]{1,0:T(8,128)(2,1)S(1)} collective-permute-done((bf16[896,128]{1,0:T(8,128)(2,1)S(1)}, bf16[896,128]{1,0:T(8,128)(2,1)S(1)}, u32[]{:S(2)}, u32[]{:S(2)}) %collective-permute-start.1) | collective-permute-done | bytes 229408 | tf_op jit(solution)/shard_map/ppermute | solution.py:418
  21.4 1.2 %collective-permute-start.2 = (bf16[896,128]{1,0:T(8,128)(2,1)S(1)}, bf16[896,128]{1,0:T(8,128)(2,1)S(1)}, u32[]{:S(2)}, u32[]{:S(2)}) collective-permute-start(bf16[896,128]{1,0:T(8,128)(2,1)S(1)} %collective-permute-done.1.w0), channel_id=1, source_target_pairs={{0,8},{4,12},{8,0},{12,4},{16,24},{20,28},{24,16},{28,20},{32,40},... | collective-permute-start | bytes 688136 | tf_op jit(solution)/shard_map/ppermute | solution.py:420
  22.7 2.0 %copy-done = bf16[1,2,256,3584]{3,2,1,0:T(8,128)(2,1)S(1)} copy-done((bf16[1,2,256,3584]{3,2,1,0:T(8,128)(2,1)S(1)}, bf16[1,2,256,3584]{3,2,1,0:T(8,128)(2,1)}, u32[]{:S(2)}) %copy-start) | copy-done | bytes 3670040
  24.7 1.2 %copy-done.3 = bf16[896,512]{1,0:T(8,128)(2,1)S(1)} copy-done((bf16[896,512]{1,0:T(8,128)(2,1)S(1)}, bf16[896,512]{1,0:T(8,128)(2,1)}, u32[]{:S(2)}) %copy-start.3) | copy-done | bytes 917528
  25.9 0.7 copy-done.19
  26.6 1.2 %shard_map.84 = (f32[512,512]{1,0:T(8,128)S(1)}, bf16[32,128]{1,0:T(8,128)(2,1)S(1)}) custom-call(s32[4]{0:T(128)S(1)} %pad_add_fusion.place, bf16[512,3584]{1,0:T(8,128)(2,1)S(1)} %bitcast.20, bf16[896,512]{1,0:T(8,128)(2,1)S(1)} %copy-done.3, bf16[2,1792]{1,0:T(2,128)(2,1)S(1)} %bitcast.25), custom_call_target="tpu_custom_call" | custom-call | flops 469762048 | tf_op jit(solution)/shard_map/pallas_call | solution.py:98
  28.0 0.5 collective-permute-start.4
  28.6 1.2 %shard_map.85.before = f32[512,512]{1,0:T(8,128)S(1)} custom-call(s32[4]{0:T(128)S(1)} %pad_add_fusion.place, bf16[512,3584]{1,0:T(8,128)(2,1)S(1)} %bitcast.21, bf16[896,512]{1,0:T(8,128)(2,1)S(1)} %collective-permute-done.weight.near, f32[512,512]{1,0:T(8,128)S(1)} %get-tuple-element.27.before), custom_call_target="tpu_custom_call" | custom-call | flops 469762048 | tf_op jit(solution)/shard_map/pallas_call | solution.py:98
  29.8 0.9 collective-permute-done.4.w2
  31.1 2.3 %shard_map.86 = (bf16[512,512]{1,0:T(8,128)(2,1)S(1)}, f32[32,512]{1,0:T(8,128)S(1)}, bf16[2,2048]{1,0:T(2,128)(2,1)S(1)}, f32[8,1792]{1,0:T(8,128)S(1)}, f32[8,128]{1,0:T(8,128)S(1)}) custom-call(s32[4]{0:T(128)S(1)} %pad_add_fusion.place, s32[2]{0:T(128)S(1)} %bitcast.27, s32[2]{0:T(128)S(1)} %bitcast.28, bf16[512,3584]{1,0:T(8,128)(2,1)S(1)} %bitcast.22, ...), custom_call_target="tpu_custom_call" | custom-call | flops 939524096 | tf_op jit(solution)/shard_map/pallas_call | solution.py:98
  33.7 1.0 %collective-permute-done.6.other = bf16[2,2048]{1,0:T(2,128)(2,1)S(1)} collective-permute-done((bf16[2,2048]{1,0:T(2,128)(2,1)S(1)}, bf16[2,2048]{1,0:T(2,128)(2,1)S(1)}, u32[]{:S(2)}, u32[]{:S(2)}) %collective-permute-start.6) | collective-permute-done | bytes 8224 | tf_op jit(solution)/shard_map/ppermute | solution.py:328
  34.7 0.6 shard_map.88
  35.6 2.7 %collective-permute-start.8 = (bf16[4,1024]{1,0:T(4,128)(2,1)S(1)}, bf16[4,1024]{1,0:T(4,128)(2,1)S(1)}, u32[]{:S(2)}, u32[]{:S(2)}) collective-permute-start(bf16[4,1024]{1,0:T(4,128)(2,1)S(1)} %get-tuple-element.36), channel_id=1, source_target_pairs={{0,16},{4,20},{8,24},{12,28},{16,0},{20,4},{24,8},{28,12},{32,48},... | collective-permute-start | bytes 24584 | tf_op jit(solution)/shard_map/ppermute | solution.py:335
  38.4 0.8 collective-permute-done.7.near
  39.3 0.7 shard_map.87.mixed
  40.1 2.7 %collective-permute-start.10 = (bf16[4,1024]{1,0:T(4,128)(2,1)S(1)}, bf16[4,1024]{1,0:T(4,128)(2,1)S(1)}, u32[]{:S(2)}, u32[]{:S(2)}) collective-permute-start(bf16[4,1024]{1,0:T(4,128)(2,1)S(1)} %collective-permute-done.8.far), channel_id=1, source_target_pairs={{0,4},{4,0},{8,12},{12,8},{16,20},{20,16},{24,28},{28,24},{32,36},... | collective-permute-start | bytes 24584 | tf_op jit(solution)/shard_map/ppermute | solution.py:328
  42.8 0.8 collective-permute-done.10.far_other
  43.6 0.6 shard_map.89
  44.2 1.7 %collective-permute-start.11 = (bf16[16,2048]{1,0:T(8,128)(2,1)S(1)}, bf16[16,2048]{1,0:T(8,128)(2,1)}, u32[]{:S(2)}, u32[]{:S(2)}) collective-permute-start(bf16[16,2048]{1,0:T(8,128)(2,1)S(1)} %get-tuple-element.38.ring), channel_id=1, source_target_pairs={{0,224},{4,36},{8,232},{12,44},{16,240},{20,52},{24,248},{28,60},{... | collective-permute-start | bytes 196616 | tf_op jit(solution)/shard_map/ppermute | solution.py:342
  45.9 3.0 %collective-permute-start.12 = (bf16[16,2048]{1,0:T(8,128)(2,1)S(1)}, bf16[16,2048]{1,0:T(8,128)(2,1)}, u32[]{:S(2)}, u32[]{:S(2)}) collective-permute-start(bf16[16,2048]{1,0:T(8,128)(2,1)S(1)} %get-tuple-element.38.ring), channel_id=1, source_target_pairs={{0,192},{4,68},{8,200},{12,76},{16,208},{20,84},{24,216},{28,92},{... | collective-permute-start | bytes 196616 | tf_op jit(solution)/shard_map/ppermute | solution.py:342
  48.9 3.8 %collective-permute-start.13 = (bf16[16,2048]{1,0:T(8,128)(2,1)S(1)}, bf16[16,2048]{1,0:T(8,128)(2,1)}, u32[]{:S(2)}, u32[]{:S(2)}) collective-permute-start(bf16[16,2048]{1,0:T(8,128)(2,1)S(1)} %get-tuple-element.38.ring), channel_id=1, source_target_pairs={{0,160},{4,100},{8,168},{12,108},{16,176},{20,116},{24,184},{28,12... | collective-permute-start | bytes 196616 | tf_op jit(solution)/shard_map/ppermute | solution.py:342
  52.7 0.6 copy-done.15
  53.3 0.5 collective-permute-start.14
  53.7 4.3 %collective-permute-start.15 = (bf16[16,2048]{1,0:T(8,128)(2,1)}, bf16[16,2048]{1,0:T(8,128)(2,1)}, u32[]{:S(2)}, u32[]{:S(2)}) collective-permute-start(bf16[16,2048]{1,0:T(8,128)(2,1)} %collective-permute-done.11.e0), channel_id=1, source_target_pairs={{0,4},{4,0},{8,12},{12,8},{16,20},{20,16},{24,28},{28,24},{32,36},... | collective-permute-start | bytes 196616 | tf_op jit(solution)/shard_map/ppermute | solution.py:328
  58.6 1.9 %collective-permute-done.14.e3 = bf16[16,1024]{1,0:T(8,128)(2,1)S(1)} collective-permute-done((bf16[16,1024]{1,0:T(8,128)(2,1)S(1)}, bf16[16,1024]{1,0:T(8,128)(2,1)S(1)}, u32[]{:S(2)}, u32[]{:S(2)}) %collective-permute-start.14) | collective-permute-done | bytes 32800 | tf_op jit(solution)/shard_map/ppermute | solution.py:343
  60.5 1.0 collective-permute-start.18
  61.5 1.0 collective-permute-done.18.f3
  62.5 2.0 %copy-done.2 = bf16[1,2,256,3584]{3,2,1,0:T(8,128)(2,1)S(1)} copy-done((bf16[1,2,256,3584]{3,2,1,0:T(8,128)(2,1)S(1)}, bf16[1,2,256,3584]{3,2,1,0:T(8,128)(2,1)}, u32[]{:S(2)}) %copy-start.2) | copy-done | bytes 3670040
  64.5 0.8 copy-done.6
  65.4 0.8 copy-done.16
  66.2 0.8 copy-done.18
  67.0 3.1 %shard_map.90 = (f32[1,128]{1,0:T(1,128)}, bf16[32,512]{1,0:T(8,128)(2,1)S(1)}, bf16[32,128]{1,0:T(8,128)(2,1)S(1)}, bf16[2,1792]{1,0:T(2,128)(2,1)}, bf16[4,16,3584]{2,1,0:T(8,128)(2,1)S(1)}) custom-call(s32[4]{0:T(128)S(1)} %pad_add_fusion.place, bf16[512,3584]{1,0:T(8,128)(2,1)S(1)} %bitcast.24, f32[32,512]{1,0:T(8,128)S(1)} %copy-done.6, ...), custom_call_target="tpu_custom_call" | custom-call | flops 117440512 | tf_op jit(solution)/shard_map/pallas_call | solution.py:98
  70.2 2.2 %collective-permute-start.21 = (bf16[16,3584]{1,0:T(8,128)(2,1)S(1)}, bf16[16,3584]{1,0:T(8,128)(2,1)S(1)}, u32[]{:S(2)}, u32[]{:S(2)}) collective-permute-start(bf16[16,3584]{1,0:T(8,128)(2,1)S(1)} %get-tuple-element.50), channel_id=1, source_target_pairs={{0,64},{4,68},{8,72},{12,76},{16,80},{20,84},{24,88},{28,92},{32,2... | collective-permute-start | bytes 344072 | tf_op jit(solution)/shard_map/ppermute | solution.py:392
  72.4 3.0 %collective-permute-start.20 = (bf16[16,3584]{1,0:T(8,128)(2,1)S(1)}, bf16[16,3584]{1,0:T(8,128)(2,1)S(1)}, u32[]{:S(2)}, u32[]{:S(2)}) collective-permute-start(bf16[16,3584]{1,0:T(8,128)(2,1)S(1)} %get-tuple-element.51), channel_id=1, source_target_pairs={{0,160},{4,164},{8,168},{12,172},{16,176},{20,180},{24,184},{28,18... | collective-permute-start | bytes 344072 | tf_op jit(solution)/shard_map/ppermute | solution.py:392
  75.3 1.7 %collective-permute-start.19 = (bf16[16,3584]{1,0:T(8,128)(2,1)S(1)}, bf16[16,3584]{1,0:T(8,128)(2,1)S(1)}, u32[]{:S(2)}, u32[]{:S(2)}) collective-permute-start(bf16[16,3584]{1,0:T(8,128)(2,1)S(1)} %get-tuple-element.52), channel_id=1, source_target_pairs={{0,224},{4,228},{8,232},{12,236},{16,240},{20,244},{24,248},{28,25... | collective-permute-start | bytes 344072 | tf_op jit(solution)/shard_map/ppermute | solution.py:392
  77.1 1.2 %collective-permute-start.22 = (bf16[16,3584]{1,0:T(8,128)(2,1)S(1)}, bf16[16,3584]{1,0:T(8,128)(2,1)S(1)}, u32[]{:S(2)}, u32[]{:S(2)}) collective-permute-start(bf16[16,3584]{1,0:T(8,128)(2,1)S(1)} %get-tuple-element.53.a0), channel_id=1, source_target_pairs={{0,4},{4,0},{8,12},{12,8},{16,20},{20,16},{24,28},{28,24},{32,36},... | collective-permute-start | bytes 344072 | tf_op jit(solution)/shard_map/ppermute | solution.py:397
  78.3 0.7 copy-done.22
  79.0 4.9 %shard_map.91 = (bf16[512,3584]{1,0:T(8,128)(2,1)}, f32[8,128]{1,0:T(8,128)}) custom-call(s32[4]{0:T(128)S(1)} %pad_add_fusion.place, bf16[32,512]{1,0:T(8,128)(2,1)S(1)} %get-tuple-element.41.grad_score, f32[32,512]{1,0:T(8,128)S(1)} %copy-done.6, bf16[32,128]{1,0:T(8,128)(2,1)S(1)} %copy-done.22, bf16[32,128]{1,0:T(8,128)(2,1)S(1)} %get-tuple-element.42.grad_rows, ...), custom_call_target="tpu_custom_call" | custom-call | flops 1879048192 | tf_op jit(solution)/shard_map/pallas_call | solution.py:98
  83.9 0.5 collective-permute-start.24
  84.4 1.0 collective-permute-done.19.a1
  85.4 0.5 collective-permute-start.23
  85.9 1.0 collective-permute-done.23.b1
  86.8 1.1 %shard_map.92 = bf16[64,3584]{1,0:T(8,128)(2,1)S(1)} custom-call(s32[4]{0:T(128)S(1)} %pad_add_fusion.place, bf16[16,3584]{1,0:T(8,128)(2,1)S(1)} %get-tuple-element.53.a0, bf16[16,3584]{1,0:T(8,128)(2,1)S(1)} %collective-permute-done.19.a1, bf16[16,3584]{1,0:T(8,128)(2,1)S(1)} %collective-permute-done.20.a2, ...), custom_call_target="tpu_custom_call" | custom-call | tf_op jit(solution)/shard_map/pallas_call | solution.py:98
  88.2 13.7 %all_to_all.5 = bf16[32,2,3584]{2,1,0:T(2,128)(2,1)S(1)} all-to-all(bf16[32,2,3584]{2,1,0:T(2,128)(2,1)S(1)} %reshape.19), channel_id=1, replica_groups={{0,1,2,3,8,9,10,11,16,17,18,19,24,25,26,27,32,33,34,35,40,41,42,43,48,4..., dimensions={0} | all-to-all | bytes 917504 | tf_op jit(solution)/shard_map/all_to_all | solution.py:401
  101.8 1.0 convert_reduce_fusion
  (69 shorter events, 2.1 us)
Async XLA Ops:
  0.6 27.2 %collective-permute-start = (bf16[896,512]{1,0:T(8,128)(2,1)}, bf16[896,512]{1,0:T(8,128)(2,1)S(1)}, u32[]{:S(2)}, u32[]{:S(2)}) collective-permute-start(bf16[896,512]{1,0:T(8,128)(2,1)} %own.1), channel_id=1, source_target_pairs={{0,3},{1,0},{2,1},{3,2},{4,5},{5,6},{6,7},{7,4},{8,11},{9,8},{10,9... | collective-permute-start | bytes 2752520 | tf_op jit(solution)/shard_map/ppermute | solution.py:419
  3.8 17.5 %collective-permute-start.1 = (bf16[896,128]{1,0:T(8,128)(2,1)S(1)}, bf16[896,128]{1,0:T(8,128)(2,1)S(1)}, u32[]{:S(2)}, u32[]{:S(2)}) collective-permute-start(bf16[896,128]{1,0:T(8,128)(2,1)S(1)} %constant_dynamic-slice_fusion), channel_id=1, source_target_pairs={{0,2},{1,3},{2,0},{3,1},{4,6},{5,7},{6,4},{7,5},{8,10},{9,11},{10,... | collective-permute-start | bytes 688136 | tf_op jit(solution)/shard_map/ppermute | solution.py:418
  21.4 9.7 %copy-start.7 = (bf16[896,128]{1,0:T(8,128)(2,1)}, bf16[896,128]{1,0:T(8,128)(2,1)S(1)}, u32[]{:S(2)}) copy-start(bf16[896,128]{1,0:T(8,128)(2,1)S(1)} %collective-permute-done.1.w0) | copy-start | bytes 688132
  21.4 6.5 %collective-permute-start.2 = (bf16[896,128]{1,0:T(8,128)(2,1)S(1)}, bf16[896,128]{1,0:T(8,128)(2,1)S(1)}, u32[]{:S(2)}, u32[]{:S(2)}) collective-permute-start(bf16[896,128]{1,0:T(8,128)(2,1)S(1)} %collective-permute-done.1.w0), channel_id=1, source_target_pairs={{0,8},{4,12},{8,0},{12,4},{16,24},{20,28},{24,16},{28,20},{32,40},... | collective-permute-start | bytes 688136 | tf_op jit(solution)/shard_map/ppermute | solution.py:420
  22.6 2.0 %copy-start = (bf16[1,2,256,3584]{3,2,1,0:T(8,128)(2,1)S(1)}, bf16[1,2,256,3584]{3,2,1,0:T(8,128)(2,1)}, u32[]{:S(2)}) copy-start(bf16[1,2,256,3584]{3,2,1,0:T(8,128)(2,1)} %param.5) | copy-start | bytes 11010052
  24.7 1.2 %copy-start.3 = (bf16[896,512]{1,0:T(8,128)(2,1)S(1)}, bf16[896,512]{1,0:T(8,128)(2,1)}, u32[]{:S(2)}) copy-start(bf16[896,512]{1,0:T(8,128)(2,1)} %own.1) | copy-start | bytes 2752516
  27.8 5.6 %copy-start.21 = (bf16[32,128]{1,0:T(8,128)(2,1)}, bf16[32,128]{1,0:T(8,128)(2,1)S(1)}, u32[]{:S(2)}) copy-start(bf16[32,128]{1,0:T(8,128)(2,1)S(1)} %get-tuple-element.29.queries.query_rows) | copy-start | bytes 24580
  27.8 3.3 %copy-start.23 = (s32[1,2]{1,0:T(1,128)S(1)}, s32[1,2]{1,0:T(1,128)}, u32[]{:S(2)}) copy-start(s32[1,2]{1,0:T(1,128)} %param.6) | copy-start | bytes 28
  27.8 3.3 %copy-start.24 = (s32[1,2]{1,0:T(1,128)S(1)}, s32[1,2]{1,0:T(1,128)}, u32[]{:S(2)}) copy-start(s32[1,2]{1,0:T(1,128)} %param.8) | copy-start | bytes 28
  27.9 5.6 %copy-start.9 = (bf16[896,128]{1,0:T(8,128)(2,1)}, bf16[896,128]{1,0:T(8,128)(2,1)S(1)}, u32[]{:S(2)}) copy-start(bf16[896,128]{1,0:T(8,128)(2,1)S(1)} %collective-permute-done.2.w1) | copy-start | bytes 688132
  27.9 3.2 %collective-permute-start.3 = (bf16[896,512]{1,0:T(8,128)(2,1)S(1)}, bf16[896,512]{1,0:T(8,128)(2,1)S(1)}, u32[]{:S(2)}, u32[]{:S(2)}) collective-permute-start(bf16[896,512]{1,0:T(8,128)(2,1)S(1)} %collective-permute-done.weight.near), channel_id=1, source_target_pairs={{0,4},{4,0},{8,12},{12,8},{16,20},{20,16},{24,28},{28,24},{32,36},... | collective-permute-start | bytes 2752520 | tf_op jit(solution)/shard_map/ppermute | solution.py:415
  28.0 2.8 %collective-permute-start.4 = (bf16[896,128]{1,0:T(8,128)(2,1)S(1)}, bf16[896,128]{1,0:T(8,128)(2,1)S(1)}, u32[]{:S(2)}, u32[]{:S(2)}) collective-permute-start(bf16[896,128]{1,0:T(8,128)(2,1)S(1)} %collective-permute-done.1.w0), channel_id=1, source_target_pairs={{0,4},{4,0},{8,12},{12,8},{16,20},{20,16},{24,28},{28,24},{32,36},... | collective-permute-start | bytes 688136 | tf_op jit(solution)/shard_map/ppermute | solution.py:415
  28.5 2.6 %collective-permute-start.5 = (bf16[896,128]{1,0:T(8,128)(2,1)S(1)}, bf16[896,128]{1,0:T(8,128)(2,1)S(1)}, u32[]{:S(2)}, u32[]{:S(2)}) collective-permute-start(bf16[896,128]{1,0:T(8,128)(2,1)S(1)} %collective-permute-done.2.w1), channel_id=1, source_target_pairs={{0,4},{4,0},{8,12},{12,8},{16,20},{20,16},{24,28},{28,24},{32,36},... | collective-permute-start | bytes 688136 | tf_op jit(solution)/shard_map/ppermute | solution.py:415
  29.8 9.5 %copy-start.1 = (bf16[1,2,256,3584]{3,2,1,0:T(8,128)(2,1)S(1)}, bf16[1,2,256,3584]{3,2,1,0:T(8,128)(2,1)}, u32[]{:S(2)}) copy-start(bf16[1,2,256,3584]{3,2,1,0:T(8,128)(2,1)} %param.5) | copy-start | bytes 11010052
  30.8 9.3 %copy-start.11 = (bf16[896,128]{1,0:T(8,128)(2,1)}, bf16[896,128]{1,0:T(8,128)(2,1)S(1)}, u32[]{:S(2)}) copy-start(bf16[896,128]{1,0:T(8,128)(2,1)S(1)} %collective-permute-done.4.w2) | copy-start | bytes 688132
  31.1 8.9 %copy-start.13 = (bf16[896,128]{1,0:T(8,128)(2,1)}, bf16[896,128]{1,0:T(8,128)(2,1)S(1)}, u32[]{:S(2)}) copy-start(bf16[896,128]{1,0:T(8,128)(2,1)S(1)} %collective-permute-done.5.w3) | copy-start | bytes 688132
  33.4 6.6 %copy-start.5 = (f32[32,512]{1,0:T(8,128)}, f32[32,512]{1,0:T(8,128)S(1)}, u32[]{:S(2)}) copy-start(f32[32,512]{1,0:T(8,128)S(1)} %get-tuple-element.30.attn) | copy-start | bytes 196612
  33.5 24.9 %copy-start.17 = (f32[8,1792]{1,0:T(8,128)}, f32[8,1792]{1,0:T(8,128)S(1)}, u32[]{:S(2)}) copy-start(f32[8,1792]{1,0:T(8,128)S(1)} %get-tuple-element.32.unit) | copy-start | bytes 172036
  33.5 29.0 %copy-start.20 = (bf16[1,2,1792]{2,1,0:T(2,128)(2,1)S(1)}, bf16[1,2,1792]{2,1,0:T(2,128)(2,1)}, u32[]{:S(2)}) copy-start(bf16[1,2,1792]{2,1,0:T(2,128)(2,1)} %param.7) | copy-start | bytes 21508
  33.5 1.3 %collective-permute-start.6 = (bf16[2,2048]{1,0:T(2,128)(2,1)S(1)}, bf16[2,2048]{1,0:T(2,128)(2,1)S(1)}, u32[]{:S(2)}, u32[]{:S(2)}) collective-permute-start(bf16[2,2048]{1,0:T(2,128)(2,1)S(1)} %get-tuple-element.34.mine), channel_id=1, source_target_pairs={{0,4},{4,0},{8,12},{12,8},{16,20},{20,16},{24,28},{28,24},{32,36},... | collective-permute-start | bytes 24584 | tf_op jit(solution)/shard_map/ppermute | solution.py:328
  35.3 3.9 %collective-permute-start.7 = (bf16[4,2048]{1,0:T(4,128)(2,1)S(1)}, bf16[4,2048]{1,0:T(4,128)(2,1)S(1)}, u32[]{:S(2)}, u32[]{:S(2)}) collective-permute-start(bf16[4,2048]{1,0:T(4,128)(2,1)S(1)} %get-tuple-element.35.chip), channel_id=1, source_target_pairs={{0,24},{4,12},{8,0},{12,20},{16,8},{20,28},{24,16},{28,4},{32,56},... | collective-permute-start | bytes 49160 | tf_op jit(solution)/shard_map/ppermute | solution.py:334
  35.6 4.4 %collective-permute-start.8 = (bf16[4,1024]{1,0:T(4,128)(2,1)S(1)}, bf16[4,1024]{1,0:T(4,128)(2,1)S(1)}, u32[]{:S(2)}, u32[]{:S(2)}) collective-permute-start(bf16[4,1024]{1,0:T(4,128)(2,1)S(1)} %get-tuple-element.36), channel_id=1, source_target_pairs={{0,16},{4,20},{8,24},{12,28},{16,0},{20,4},{24,8},{28,12},{32,48},... | collective-permute-start | bytes 24584 | tf_op jit(solution)/shard_map/ppermute | solution.py:335
  39.2 4.4 %collective-permute-start.9 = (bf16[4,2048]{1,0:T(4,128)(2,1)S(1)}, bf16[4,2048]{1,0:T(4,128)(2,1)S(1)}, u32[]{:S(2)}, u32[]{:S(2)}) collective-permute-start(bf16[4,2048]{1,0:T(4,128)(2,1)S(1)} %collective-permute-done.7.near), channel_id=1, source_target_pairs={{0,4},{4,0},{8,12},{12,8},{16,20},{20,16},{24,28},{28,24},{32,36},... | collective-permute-start | bytes 49160 | tf_op jit(solution)/shard_map/ppermute | solution.py:328
  39.3 39.0 %copy-start.4 = (bf16[896,512]{1,0:T(8,128)(2,1)S(1)}, bf16[896,512]{1,0:T(8,128)(2,1)}, u32[]{:S(2)}) copy-start(bf16[896,512]{1,0:T(8,128)(2,1)} %own.1) | copy-start | bytes 2752516
  40.1 3.6 %collective-permute-start.10 = (bf16[4,1024]{1,0:T(4,128)(2,1)S(1)}, bf16[4,1024]{1,0:T(4,128)(2,1)S(1)}, u32[]{:S(2)}, u32[]{:S(2)}) collective-permute-start(bf16[4,1024]{1,0:T(4,128)(2,1)S(1)} %collective-permute-done.8.far), channel_id=1, source_target_pairs={{0,4},{4,0},{8,12},{12,8},{16,20},{20,16},{24,28},{28,24},{32,36},... | collective-permute-start | bytes 24584 | tf_op jit(solution)/shard_map/ppermute | solution.py:328
  44.2 9.5 %collective-permute-start.11 = (bf16[16,2048]{1,0:T(8,128)(2,1)S(1)}, bf16[16,2048]{1,0:T(8,128)(2,1)}, u32[]{:S(2)}, u32[]{:S(2)}) collective-permute-start(bf16[16,2048]{1,0:T(8,128)(2,1)S(1)} %get-tuple-element.38.ring), channel_id=1, source_target_pairs={{0,224},{4,36},{8,232},{12,44},{16,240},{20,52},{24,248},{28,60},{... | collective-permute-start | bytes 196616 | tf_op jit(solution)/shard_map/ppermute | solution.py:342
  45.9 12.1 %collective-permute-start.12 = (bf16[16,2048]{1,0:T(8,128)(2,1)S(1)}, bf16[16,2048]{1,0:T(8,128)(2,1)}, u32[]{:S(2)}, u32[]{:S(2)}) collective-permute-start(bf16[16,2048]{1,0:T(8,128)(2,1)S(1)} %get-tuple-element.38.ring), channel_id=1, source_target_pairs={{0,192},{4,68},{8,200},{12,76},{16,208},{20,84},{24,216},{28,92},{... | collective-permute-start | bytes 196616 | tf_op jit(solution)/shard_map/ppermute | solution.py:342
  48.9 9.4 %collective-permute-start.13 = (bf16[16,2048]{1,0:T(8,128)(2,1)S(1)}, bf16[16,2048]{1,0:T(8,128)(2,1)}, u32[]{:S(2)}, u32[]{:S(2)}) collective-permute-start(bf16[16,2048]{1,0:T(8,128)(2,1)S(1)} %get-tuple-element.38.ring), channel_id=1, source_target_pairs={{0,160},{4,100},{8,168},{12,108},{16,176},{20,116},{24,184},{28,12... | collective-permute-start | bytes 196616 | tf_op jit(solution)/shard_map/ppermute | solution.py:342
  53.3 7.2 %collective-permute-start.14 = (bf16[16,1024]{1,0:T(8,128)(2,1)S(1)}, bf16[16,1024]{1,0:T(8,128)(2,1)S(1)}, u32[]{:S(2)}, u32[]{:S(2)}) collective-permute-start(bf16[16,1024]{1,0:T(8,128)(2,1)S(1)} %get-tuple-element.39), channel_id=1, source_target_pairs={{0,128},{4,132},{8,136},{12,140},{16,144},{20,148},{24,152},{28,15... | collective-permute-start | bytes 98312 | tf_op jit(solution)/shard_map/ppermute | solution.py:343
  53.7 8.7 %collective-permute-start.15 = (bf16[16,2048]{1,0:T(8,128)(2,1)}, bf16[16,2048]{1,0:T(8,128)(2,1)}, u32[]{:S(2)}, u32[]{:S(2)}) collective-permute-start(bf16[16,2048]{1,0:T(8,128)(2,1)} %collective-permute-done.11.e0), channel_id=1, source_target_pairs={{0,4},{4,0},{8,12},{12,8},{16,20},{20,16},{24,28},{28,24},{32,36},... | collective-permute-start | bytes 196616 | tf_op jit(solution)/shard_map/ppermute | solution.py:328
  58.1 4.4 %collective-permute-start.16 = (bf16[16,2048]{1,0:T(8,128)(2,1)}, bf16[16,2048]{1,0:T(8,128)(2,1)}, u32[]{:S(2)}, u32[]{:S(2)}) collective-permute-start(bf16[16,2048]{1,0:T(8,128)(2,1)} %collective-permute-done.12.e1), channel_id=1, source_target_pairs={{0,4},{4,0},{8,12},{12,8},{16,20},{20,16},{24,28},{28,24},{32,36},... | collective-permute-start | bytes 196616 | tf_op jit(solution)/shard_map/ppermute | solution.py:328
  58.3 4.1 %collective-permute-start.17 = (bf16[16,2048]{1,0:T(8,128)(2,1)}, bf16[16,2048]{1,0:T(8,128)(2,1)}, u32[]{:S(2)}, u32[]{:S(2)}) collective-permute-start(bf16[16,2048]{1,0:T(8,128)(2,1)} %collective-permute-done.13.e2), channel_id=1, source_target_pairs={{0,4},{4,0},{8,12},{12,8},{16,20},{20,16},{24,28},{28,24},{32,36},... | collective-permute-start | bytes 196616 | tf_op jit(solution)/shard_map/ppermute | solution.py:328
  60.5 2.0 %collective-permute-start.18 = (bf16[16,1024]{1,0:T(8,128)(2,1)S(1)}, bf16[16,1024]{1,0:T(8,128)(2,1)}, u32[]{:S(2)}, u32[]{:S(2)}) collective-permute-start(bf16[16,1024]{1,0:T(8,128)(2,1)S(1)} %collective-permute-done.14.e3), channel_id=1, source_target_pairs={{0,4},{4,0},{8,12},{12,8},{16,20},{20,16},{24,28},{28,24},{32,36},... | collective-permute-start | bytes 98312 | tf_op jit(solution)/shard_map/ppermute | solution.py:328
  62.5 2.0 %copy-start.2 = (bf16[1,2,256,3584]{3,2,1,0:T(8,128)(2,1)S(1)}, bf16[1,2,256,3584]{3,2,1,0:T(8,128)(2,1)}, u32[]{:S(2)}) copy-start(bf16[1,2,256,3584]{3,2,1,0:T(8,128)(2,1)} %param.5) | copy-start | bytes 11010052
  64.5 0.8 copy-start.6
  65.4 0.8 copy-start.16
  66.2 0.8 copy-start.18
  67.0 11.2 %copy-start.8 = (bf16[896,128]{1,0:T(8,128)(2,1)S(1)}, bf16[896,128]{1,0:T(8,128)(2,1)}, u32[]{:S(2)}) copy-start(bf16[896,128]{1,0:T(8,128)(2,1)} %copy-done.7) | copy-start | bytes 688132
  67.0 11.2 %copy-start.10 = (bf16[896,128]{1,0:T(8,128)(2,1)S(1)}, bf16[896,128]{1,0:T(8,128)(2,1)}, u32[]{:S(2)}) copy-start(bf16[896,128]{1,0:T(8,128)(2,1)} %copy-done.9) | copy-start | bytes 688132
  67.0 11.2 %copy-start.12 = (bf16[896,128]{1,0:T(8,128)(2,1)S(1)}, bf16[896,128]{1,0:T(8,128)(2,1)}, u32[]{:S(2)}) copy-start(bf16[896,128]{1,0:T(8,128)(2,1)} %copy-done.11) | copy-start | bytes 688132
  67.0 11.3 %copy-start.14 = (bf16[896,128]{1,0:T(8,128)(2,1)S(1)}, bf16[896,128]{1,0:T(8,128)(2,1)}, u32[]{:S(2)}) copy-start(bf16[896,128]{1,0:T(8,128)(2,1)} %copy-done.13) | copy-start | bytes 688132
  70.2 13.7 %collective-permute-start.21 = (bf16[16,3584]{1,0:T(8,128)(2,1)S(1)}, bf16[16,3584]{1,0:T(8,128)(2,1)S(1)}, u32[]{:S(2)}, u32[]{:S(2)}) collective-permute-start(bf16[16,3584]{1,0:T(8,128)(2,1)S(1)} %get-tuple-element.50), channel_id=1, source_target_pairs={{0,64},{4,68},{8,72},{12,76},{16,80},{20,84},{24,88},{28,92},{32,2... | collective-permute-start | bytes 344072 | tf_op jit(solution)/shard_map/ppermute | solution.py:392
  72.4 11.6 %collective-permute-start.20 = (bf16[16,3584]{1,0:T(8,128)(2,1)S(1)}, bf16[16,3584]{1,0:T(8,128)(2,1)S(1)}, u32[]{:S(2)}, u32[]{:S(2)}) collective-permute-start(bf16[16,3584]{1,0:T(8,128)(2,1)S(1)} %get-tuple-element.51), channel_id=1, source_target_pairs={{0,160},{4,164},{8,168},{12,172},{16,176},{20,180},{24,184},{28,18... | collective-permute-start | bytes 344072 | tf_op jit(solution)/shard_map/ppermute | solution.py:392
  75.3 10.0 %collective-permute-start.19 = (bf16[16,3584]{1,0:T(8,128)(2,1)S(1)}, bf16[16,3584]{1,0:T(8,128)(2,1)S(1)}, u32[]{:S(2)}, u32[]{:S(2)}) collective-permute-start(bf16[16,3584]{1,0:T(8,128)(2,1)S(1)} %get-tuple-element.52), channel_id=1, source_target_pairs={{0,224},{4,228},{8,232},{12,236},{16,240},{20,244},{24,248},{28,25... | collective-permute-start | bytes 344072 | tf_op jit(solution)/shard_map/ppermute | solution.py:392
  77.1 8.8 %collective-permute-start.22 = (bf16[16,3584]{1,0:T(8,128)(2,1)S(1)}, bf16[16,3584]{1,0:T(8,128)(2,1)S(1)}, u32[]{:S(2)}, u32[]{:S(2)}) collective-permute-start(bf16[16,3584]{1,0:T(8,128)(2,1)S(1)} %get-tuple-element.53.a0), channel_id=1, source_target_pairs={{0,4},{4,0},{8,12},{12,8},{16,20},{20,16},{24,28},{28,24},{32,36},... | collective-permute-start | bytes 344072 | tf_op jit(solution)/shard_map/ppermute | solution.py:397
  83.9 2.0 %collective-permute-start.25 = (bf16[16,3584]{1,0:T(8,128)(2,1)S(1)}, bf16[16,3584]{1,0:T(8,128)(2,1)S(1)}, u32[]{:S(2)}, u32[]{:S(2)}) collective-permute-start(bf16[16,3584]{1,0:T(8,128)(2,1)S(1)} %collective-permute-done.21.a3), channel_id=1, source_target_pairs={{0,4},{4,0},{8,12},{12,8},{16,20},{20,16},{24,28},{28,24},{32,36},... | collective-permute-start | bytes 344072 | tf_op jit(solution)/shard_map/ppermute | solution.py:397
  83.9 2.0 %collective-permute-start.24 = (bf16[16,3584]{1,0:T(8,128)(2,1)S(1)}, bf16[16,3584]{1,0:T(8,128)(2,1)S(1)}, u32[]{:S(2)}, u32[]{:S(2)}) collective-permute-start(bf16[16,3584]{1,0:T(8,128)(2,1)S(1)} %collective-permute-done.20.a2), channel_id=1, source_target_pairs={{0,4},{4,0},{8,12},{12,8},{16,20},{20,16},{24,28},{28,24},{32,36},... | collective-permute-start | bytes 344072 | tf_op jit(solution)/shard_map/ppermute | solution.py:397
  85.4 1.5 %collective-permute-start.23 = (bf16[16,3584]{1,0:T(8,128)(2,1)S(1)}, bf16[16,3584]{1,0:T(8,128)(2,1)S(1)}, u32[]{:S(2)}, u32[]{:S(2)}) collective-permute-start(bf16[16,3584]{1,0:T(8,128)(2,1)S(1)} %collective-permute-done.19.a1), channel_id=1, source_target_pairs={{0,4},{4,0},{8,12},{12,8},{16,20},{20,16},{24,28},{28,24},{32,36},... | collective-permute-start | bytes 344072 | tf_op jit(solution)/shard_map/ppermute | solution.py:397
  (3 other events, 2.0 us)

commit v3 on v2

--- a/solution.py
+++ b/solution.py
@@ -17,6 +17,8 @@
 DOCS = 2
 SIDE = DOCS * SLOT
 ROWS = KVH * SIDE
+FOLD = 4
+ROUNDS = (0, -1, -3, 2)
 SOFTMAX_TEMPER = 0.05
 
 NZ, NX, NC, NY = 8, 4, 2, 4
@@ -31,6 +33,7 @@
 
 
 OTHER_CORE = [(i, i ^ 1) for i in range(N_DP)]
+CHIPS = [[dp_index(z, x, c) for z in range(NZ) for x in range(NX)] for c in range(NC)]
 X_MATE = [(i, i ^ NC) for i in range(N_DP)]
 
 
@@ -92,7 +95,7 @@
     return lax.dot_general(a, b, (((1,), (1,)), ((), ())), preferred_element_type=F32)
 
 
-def call(body, scalars, arrays, outs, scratch=(), flops=0):
+def call(body, scalars, arrays, outs, scratch=(), flops=0, limit=4):
     smem = [pl.BlockSpec(memory_space=pltpu.SMEM)] * len(scalars)
     vmem = [pl.BlockSpec(memory_space=pltpu.VMEM)] * len(arrays)
     return pl.pallas_call(
@@ -101,7 +104,7 @@
         in_specs=smem + vmem,
         out_specs=[pl.BlockSpec(memory_space=pltpu.VMEM)] * len(outs),
         scratch_shapes=list(scratch),
-        compiler_params=pltpu.CompilerParams(vmem_limit_bytes=20 * 1024 * 1024),
+        compiler_params=pltpu.CompilerParams(vmem_limit_bytes=limit * 1024 * 1024),
         cost_estimate=pl.CostEstimate(flops=flops, bytes_accessed=0, transcendentals=0),
     )(*scalars, *arrays)
 
@@ -173,7 +176,7 @@
 
 def attend_body(
     place, lens, marks, tokens, before, near_other, w0, w1, w2, w3, queries,
-    keyval, attn, packed, unit, norm, flat,
+    keyval, attn, spread, unit, norm, flat,
 ):
     shard = near_other.shape[0]
     blocks = [
@@ -201,38 +204,47 @@
     vec = readout / length
     unit[...] = vec
     norm[...] = jnp.broadcast_to(length, norm.shape)
-    emb = vec.astype(BF16)
     doc_at = lax.broadcasted_iota(jnp.int32, (SLOT, HD), 0)
-    mark = jnp.where(doc_at == 0, marks[0], marks[1]).astype(F32).astype(BF16)
-    whole = jnp.concatenate([emb[:, :HALF], mark, emb[:, HALF:], mark], axis=1)
-    packed[...] = whole[:DOCS]
-
-
-def mix_body(tokens, attn, mixed):
-    mixed[...] = dot_nn(attn[...].astype(BF16), tokens[...]).astype(BF16)
-
-
-def backward_body(
-    place, tokens, attn, mixed, queries, keyval, unit, norm,
-    ring, e0, e1, e2, e3, f0, f1, f2, f3,
-    loss, grad_score, grad_rows, grad_query, factors, flat, lanes,
+    mark = jnp.where(doc_at == 0, marks[0], marks[1]).astype(F32)
+    whole = jnp.concatenate([vec[:, :HALF], mark, vec[:, HALF:], mark], axis=1)
+    wide = spread.shape[2]
+    parts = [whole[:DOCS, i * wide : (i + 1) * wide] for i in range(FOLD)]
+    folded = jnp.concatenate(parts, axis=0).astype(BF16)
+    spread[...] = jnp.broadcast_to(folded[None], spread.shape)
+
+
+def doc_ids(place, slots, half_docs):
+    core = jnp.where(slots < half_docs, place[1], 1 - place[1])
+    own = slots % half_docs
+    return (own // DOCS) * (NC * DOCS) + core * DOCS + own % DOCS
+
+
+def contrast_body(
+    place, attn, keyval, unit, norm, mine, other,
+    loss, grad_score, grad_rows, grad_query, grad_read, flat, lanes,
 ):
-    first = place[1] == 0
-    gathered = join_docs(first, ring, (e0, e1, e2, e3), (f0, f1, f2, f3))
+    half_docs = mine.shape[0] // FOLD
+    total_docs = NC * half_docs
+    to = lax.broadcasted_iota(jnp.int32, (half_docs, mine.shape[0]), 0)
+    at = lax.broadcasted_iota(jnp.int32, (half_docs, mine.shape[0]), 1)
+    base = (to // DOCS) * (FOLD * DOCS) + to % DOCS
+    ones = [jnp.where(at == base + i * DOCS, 1.0, 0.0).astype(BF16) for i in range(FOLD)]
+    unfold = lambda a: jnp.concatenate([dot_nn(one, a[...]) for one in ones], axis=1)
+    gathered = jnp.concatenate([unfold(mine), unfold(other)], axis=0)
     span = HALF + HD
     everyone = jnp.concatenate([gathered[:, :HALF], gathered[:, span : span + HALF]], axis=1)
-    total_docs = everyone.shape[0]
-    marks = gathered[:, HALF:span].astype(F32)
+    everyone = everyone.astype(BF16)
+    marks = gathered[:, HALF:span]
     ids = lax.broadcasted_iota(jnp.int32, (total_docs, total_docs), 0)
     cols = lax.broadcasted_iota(jnp.int32, (total_docs, total_docs), 1)
     sim = dot_nt(everyone, everyone) / SOFTMAX_TEMPER
     sim_exp = jnp.where(ids == cols, 0.0, jnp.exp(sim))
     total = jnp.sum(sim_exp, axis=-1, keepdims=True)
-    picked = marks == doc_ids(place, cols).astype(F32)
+    picked = marks == doc_ids(place, cols, half_docs).astype(F32)
     all_loss = jnp.log(total) - jnp.sum(jnp.where(picked, sim, 0.0), axis=-1, keepdims=True)
     prob = (sim_exp / total).astype(BF16)
     pick = jnp.where(picked, 1.0, 0.0).astype(BF16)
-    at = place[1] * DOCS
+    at = (place[2] // (NC * DOCS)) * DOCS
     slots = lax.broadcasted_iota(jnp.int32, (SLOT, total_docs), 0)
     here = lax.broadcasted_iota(jnp.int32, (SLOT, total_docs), 1)
     chosen = (here == at + slots) & (slots < DOCS)
@@ -253,8 +265,9 @@
     grad_unit = (parts[:8] + parts[8:16] - parts[16:24] - parts[24:]) / SOFTMAX_TEMPER
     vec = unit[...]
     along = jnp.sum(vec * grad_unit, axis=-1, keepdims=True)
-    grad_read = (grad_unit - vec * along) / norm[:, :1]
-    from_lanes(grad_read, flat)
+    full = (grad_unit - vec * along) / norm[:, :1]
+    grad_read[...] = full
+    from_lanes(full, flat)
     heads = flat[...].astype(BF16)
     grad_rows[...] = heads
     sides = [slice(h * SIDE, (h + 1) * SIDE) for h in range(KVH)]
@@ -268,18 +281,31 @@
     for h in range(KVH):
         to_lanes(dot_nn(score[sides[h]], head(keyval, h)), h, lanes)
     grad_query[...] = lanes[:DOCS, :].astype(BF16)
+
+
+def factor_body(place, tokens, grad_score, attn, queries, grad_read, *outs):
+    sides = [slice(h * SIDE, (h + 1) * SIDE) for h in range(KVH)]
     wide = GRP * HD
     slot_rows = lax.broadcasted_iota(jnp.int32, (SIDE, wide), 0)
-    halves = [dot_nn(score, tokens[...]), mixed[...].astype(F32)]
-    tails = [queries[...].astype(F32), grad_read]
+    both = jnp.concatenate([grad_score[...], attn[...].astype(BF16)], axis=0)
+    mixed = dot_nn(both, tokens[...])
+    tails = [queries[...].astype(F32), grad_read[...]]
+    kinds = []
     for kind in range(2):
         for h in range(KVH):
             tail = tails[kind][:, h * wide : (h + 1) * wide]
             tail = jnp.where(slot_rows < SLOT, tail[0:1], tail[1:2])
-            part = halves[kind][sides[h]]
+            part = mixed[kind * ROWS : (kind + 1) * ROWS][sides[h]]
             joined = jnp.where(slot_rows % SLOT == GRP, tail, part[:, :wide])
-            factors[kind * KVH + h, :, :wide] = joined.astype(BF16)
-            factors[kind * KVH + h, :, wide:] = part[:, wide:].astype(BF16)
+            kinds.append(jnp.concatenate([joined, part[:, wide:]], axis=1))
+    z = place[2] // (NX * NC * DOCS)
+    sign = 1 - 2 * lax.rem(z, 2)
+    for k, out in zip(ROUNDS, outs):
+        kind = lax.rem(z + NZ + sign * k, NZ) // 2
+        picked = kinds[0]
+        for t in range(1, TYPES):
+            picked = jnp.where(kind == t, kinds[t], picked)
+        out[...] = picked.astype(BF16)
 
 
 def token_body(
@@ -302,65 +328,10 @@
     done[...] = probs[:SLOT, :HD].astype(F32)
 
 
-def chip_body(place, mine, other, chip, half):
-    first = place[1] == 0
-    a, b = mine[...].astype(F32), other[...].astype(F32)
-    whole = jnp.concatenate([jnp.where(first, a, b), jnp.where(first, b, a)], axis=0).astype(BF16)
-    chip[...] = whole
-    width = half.shape[1]
-    half[...] = jnp.where(first, whole[:, :width], whole[:, width:])
-
-
-def ring_body(place, chip, near, far, near_other, far_other, ring, half):
-    first = place[1] == 0
-    a, b = near[...].astype(F32), near_other[...].astype(F32)
-    c, d = far[...].astype(F32), far_other[...].astype(F32)
-    plus, minus = jnp.where(first, a, b), jnp.where(first, b, a)
-    across = jnp.concatenate([jnp.where(first, c, d), jnp.where(first, d, c)], axis=1)
-    whole = jnp.concatenate([chip[...].astype(F32), plus, across, minus], axis=0).astype(BF16)
-    ring[...] = whole
-    width = half.shape[1]
-    half[...] = jnp.where(first, whole[:, :width], whole[:, width:])
-
-
-def gather_docs(packed, place, before_ring):
-    docs, wide = packed.shape
-    swap = lambda a: lax.ppermute(a, "dp", OTHER_CORE)
-    count = NC * docs
-    chip, half = call(
-        chip_body, (place,), (packed, swap(packed)),
-        [((count, wide), BF16), ((count, wide // 2), BF16)],
-    )
-    near = lax.ppermute(chip, "dp", plane_shift(dx=1, mirror=True))
-    far = lax.ppermute(half, "dp", plane_shift(dx=2))
-    far = tie(far, before_ring)
-    count *= NX
-    ring, half = call(
-        ring_body, (place,), (chip, near, far, swap(near), swap(far)),
-        [((count, wide), BF16), ((count, wide // 2), BF16)],
-    )
-    blocks = [lax.ppermute(ring, "dp", plane_shift(dz=k, mirror=True)) for k in (1, 2, 3)]
-    blocks.append(lax.ppermute(half, "dp", plane_shift(dz=4)))
-    return (ring, *blocks, *[swap(a) for a in blocks])
-
-
-def join_docs(first, ring, blocks, others):
-    pairs = [(a[...], b[...]) for a, b in zip(blocks, others)]
-    plus = [jnp.where(first, a, b) for a, b in pairs]
-    minus = [jnp.where(first, b, a) for a, b in pairs]
-    across = jnp.concatenate([plus[3], minus[3]], axis=1)
-    return jnp.concatenate(
-        [ring[...], plus[0], plus[1], plus[2], across, minus[2], minus[1], minus[0]], axis=0
-    )
-
-
-def doc_ids(place, slots):
-    dp = place[2] // DOCS
-    z, x = dp // (NX * NC), (dp // NC) % NX
-    count = NC * DOCS
-    at_z = (z + slots // (NX * count)) % NZ
-    at_x = (x + (slots // count) % NX) % NX
-    return (at_z * NX + at_x) * count + slots % count
+def gather_docs(spread):
+    got = lax.all_to_all(spread, "dp", 0, 0, axis_index_groups=CHIPS)
+    got = got.reshape(-1, spread.shape[2])
+    return got, lax.ppermute(got, "dp", OTHER_CORE)
 
 
 def outer_body(place, a0, a1, a2, a3, b0, b1, b2, b3, out):
@@ -384,13 +355,8 @@
 
 
 def exchange_types(factors):
-    z = lax.axis_index("dp") // (NX * NC)
-    sign = 1 - 2 * (z % 2)
-    take = lambda to: lax.dynamic_index_in_dim(factors, (to % NZ) // 2, 0, keepdims=False)
-    quads = [take(z)]
-    for k in (-1, -3, 2):
-        quads.append(lax.ppermute(take(z + NZ + sign * k), "dp", parity_shift(k)))
-    return quads
+    moved = [lax.ppermute(a, "dp", parity_shift(k)) for a, k in zip(factors[1:], ROUNDS[1:])]
+    return [factors[0], *moved]
 
 
 def reduce_weight(quads, place):
@@ -416,49 +382,56 @@
 
     piece = lax.dynamic_slice(kv_weight, (0, (2 * core + parity) * HD), (shard, HD))
     mine = lax.ppermute(piece, "fsdp", Y_ACROSS)
-    near = lax.ppermute(kv_weight, ("dp", "fsdp"), y_mirror())
+    near = lax.ppermute(tie(kv_weight, mine), ("dp", "fsdp"), y_mirror())
     mate = lax.ppermute(mine, "dp", X_MATE)
 
     flops = 2 * count * shard * KVW
     part, query_rows = call(
         own_body, (place,), (rows, kv_weight, queries[0]),
-        [((count, KVW), F32), ((ROWS, HD), BF16)], [pltpu.VMEM((ROWS, HD), F32)], flops=flops,
+        [((count, KVW), F32), ((ROWS, HD), BF16)], [pltpu.VMEM((ROWS, HD), F32)], flops=flops, limit=8,
     )
     near = tie(near, mate, part)
     across = (mine, mate, swap(mine), swap(mate))
     near_other = swap(near)
-    (part,) = call(near_body, (place,), (rows, near, part), [((count, KVW), F32)], flops=flops)
-    keyval, attn, packed, unit, norm = call(
+    (part,) = call(near_body, (place,), (rows, near, part), [((count, KVW), F32)], flops=flops, limit=8)
+    keyval, attn, spread, unit, norm = call(
         attend_body,
         (place, lengths[0], positives[0]),
         (rows, part, near_other, *across, query_rows),
         [
             ((count, KVW), BF16),
             ((ROWS, count), F32),
-            ((docs, 2 * (HALF + HD)), BF16),
+            ((NZ * NX, FOLD * docs, 2 * (HALF + HD) // FOLD), BF16),
             ((SLOT, QW), F32),
             ((SLOT, HD), F32),
         ],
         [pltpu.VMEM((SLOT, QW), F32)],
         flops=2 * flops,
-    )
-    (mixed,) = call(
-        mix_body, (), (rows, attn), [((ROWS, width), BF16)], flops=2 * ROWS * width * count
-    )
-    everyone = gather_docs(packed, place, mixed)
-    loss, grad_score, grad_rows, grad_query, factors = call(
-        backward_body,
+        limit=16,
+    )
+    everyone = gather_docs(spread)
+    loss, grad_score, grad_rows, grad_query, grad_read = call(
+        contrast_body,
         (place,),
-        (rows, attn, mixed, queries[0], keyval, unit, norm, *everyone),
+        (attn, keyval, unit, norm, *everyone),
         [
             ((1, HD), F32),
             ((ROWS, count), BF16),
             ((ROWS, HD), BF16),
             ((docs, QW), BF16),
-            ((TYPES, SIDE, width), BF16),
+            ((SLOT, QW), F32),
         ],
         [pltpu.VMEM((ROWS, HD), F32), pltpu.VMEM((SLOT, QW), F32)],
-        flops=2 * ROWS * width * count,
+        flops=6_000_000_000,
+        limit=8,
+    )
+    factors = call(
+        factor_body,
+        (place,),
+        (rows, grad_score, attn, queries[0], grad_read),
+        [((SIDE, width), BF16)] * len(ROUNDS),
+        flops=4 * ROWS * width * count,
+        limit=8,
     )
     quads = exchange_types(factors)
     grad_tok, done = call(
@@ -467,6 +440,7 @@
         (grad_score, attn, query_rows, grad_rows, kv_weight, near, near_other, *across),
         [((count, width), BF16), ((SLOT, HD), F32)],
         flops=4 * flops,
+        limit=20,
     )
     quads = [quads[0], *[tie(a, done) for a in quads[1:]]]
     grad_weight = reduce_weight(quads, place)

time: 103 us -> 95.5 us (0.927)
  blocking collectives: 13.7 us -> 39.3 us
  starting transfers between devices: 36.7 us -> 19.9 us
  waiting for transfers between devices: 23.6 us -> 14.2 us
  local copies, waits for them, and re-layouts: 11 us -> 5.07 us
    all_to_all x0 -> x1, blocking collectives: none -> 22.4 us  [gather_docs(): got = lax.all_to_all(spread, 'dp', 0, 0, axis_index_groups=CHIPS)]
    ppermute x17 -> x5, starting transfers between devices: 29.9 us -> 9.25 us  [the longest x3 4.85 us: exchange_types(): lax.ppermute(a, 'dp', parity_shift(k))]
    ppermute x1, waiting for transfers between devices: 14.8 us -> 4.27 us  [local(): mine = lax.ppermute(piece, 'fsdp', Y_ACROSS)]
    unnamed x50 -> x16, local copies, waits for them, and re-layouts: 9.84 us -> 3.94 us
    all_to_all x1, blocking collectives: 13.7 us -> 16.9 us  [reduce_weight(): got = lax.all_to_all(pieces, ('dp', 'fsdp'), 0, 0, axis_index_groups=OWNERS)]
    ppermute x3, starting transfers between devices: 0.69 us -> 2.57 us  [local(): swap = lambda a: lax.ppermute(a, 'dp', OTHER_CORE)]
    ppermute x17 -> x5, waiting for transfers between devices: 6.58 us -> 7.96 us  [the longest x1 5.93 us: local(): near = lax.ppermute(tie(kv_weight, mine), ('dp', 'fsdp'), y_mirror())]
    ppermute x1, starting transfers between devices: 2.71 us -> 3.83 us  [local(): mine = lax.ppermute(piece, 'fsdp', Y_ACROSS)]
  transfers between devices with their start and end apart: 26 -> 14, of which waited for: 10 -> 9; matrix products, arithmetic and copies ran while one was open for 1% -> 0% of each run, Pallas kernels for 8% -> 8%
where the time goes in v3:
time: 95.5 us; the launch traced here: 95.2 us
  blocking collectives  39.3 us (41%)
  starting transfers between devices  19.9 us (21%)
  Pallas kernels  14.9 us (16%)
  waiting for transfers between devices  14.2 us (15%)
  local copies, waits for them, and re-layouts  5.07 us (5%)
  other arithmetic  1.06 us (1%)
    all_to_all x1, blocking collectives, gather_docs(): got = lax.all_to_all(spread, 'dp', 0, 0, axis_index_groups=CHIPS)  22.4 us
    all_to_all x1, blocking collectives, reduce_weight(): got = lax.all_to_all(pieces, ('dp', 'fsdp'), 0, 0, axis_index_groups=OWNERS)  16.9 us
    pallas_call x7, Pallas kernels, call(): pl.pallas_call(body, out_shape=[jax.ShapeDtypeStruct(s, d) for s, d in ou...  14.9 us
    ppermute x1, waiting for transfers between devices, local(): near = lax.ppermute(tie(kv_weight, mine), ('dp', 'fsdp'), y_mirror())  5.93 us
    ppermute x3, starting transfers between devices, exchange_types(): lax.ppermute(a, 'dp', parity_shift(k))  4.85 us
    ppermute x1, waiting for transfers between devices, local(): mine = lax.ppermute(piece, 'fsdp', Y_ACROSS)  4.27 us
    unnamed x16, local copies, waits for them, and re-layouts  3.94 us
    ppermute x1, starting transfers between devices, local(): mine = lax.ppermute(piece, 'fsdp', Y_ACROSS)  3.83 us
  transfers between devices with their start and end apart: 14, of which 9 were waited for; matrix products, arithmetic and copies ran while one was open for 0% of the time, Pallas kernels for 8%

profile of v3, /device:TPU:1, one launch (start us, length us, event | category | flops | bytes accessed | tf_op | source)
XLA Modules:
  0.0 95.2 jit_solution(8790472540566695294)
XLA Ops:
  0.7 1.0 %constant_dynamic-slice_fusion = bf16[896,128]{1,0:T(8,128)(2,1)S(1)} fusion(bf16[896,512]{1,0:T(8,128)(2,1)} %own.1, s32[]{:T(128)S(6)} %select_n.21), kind=kLoop, calls=%fused_computation.2 | loop fusion | bytes 458756 | tf_op jit(solution)/shard_map/dynamic_slice | solution.py:383
  1.6 3.8 %collective-permute-start = (bf16[896,128]{1,0:T(8,128)(2,1)S(1)}, bf16[896,128]{1,0:T(8,128)(2,1)S(1)}, u32[]{:S(2)}, u32[]{:S(2)}) collective-permute-start(bf16[896,128]{1,0:T(8,128)(2,1)S(1)} %constant_dynamic-slice_fusion), channel_id=1, source_target_pairs={{0,2},{1,3},{2,0},{3,1},{4,6},{5,7},{6,4},{7,5},{8,10},{9,11},{10,... | collective-permute-start | bytes 688136 | tf_op jit(solution)/shard_map/ppermute | solution.py:384
  5.5 4.3 %collective-permute-done.w0 = bf16[896,128]{1,0:T(8,128)(2,1)S(1)} collective-permute-done((bf16[896,128]{1,0:T(8,128)(2,1)S(1)}, bf16[896,128]{1,0:T(8,128)(2,1)S(1)}, u32[]{:S(2)}, u32[]{:S(2)}) %collective-permute-start) | collective-permute-done | bytes 229408 | tf_op jit(solution)/shard_map/ppermute | solution.py:384
  9.7 2.1 %collective-permute-start.1 = (bf16[896,512]{1,0:T(8,128)(2,1)}, bf16[896,512]{1,0:T(8,128)(2,1)S(1)}, u32[]{:S(2)}, u32[]{:S(2)}) collective-permute-start(bf16[896,512]{1,0:T(8,128)(2,1)} %own.1), channel_id=1, source_target_pairs={{0,3},{1,0},{2,1},{3,2},{4,5},{5,6},{6,7},{7,4},{8,11},{9,8},{10,9... | collective-permute-start | bytes 2752520 | tf_op jit(solution)/shard_map/ppermute | solution.py:385
  11.8 1.2 %collective-permute-start.2 = (bf16[896,128]{1,0:T(8,128)(2,1)S(1)}, bf16[896,128]{1,0:T(8,128)(2,1)S(1)}, u32[]{:S(2)}, u32[]{:S(2)}) collective-permute-start(bf16[896,128]{1,0:T(8,128)(2,1)S(1)} %collective-permute-done.w0), channel_id=1, source_target_pairs={{0,8},{4,12},{8,0},{12,4},{16,24},{20,28},{24,16},{28,20},{32,40},... | collective-permute-start | bytes 688136 | tf_op jit(solution)/shard_map/ppermute | solution.py:386
  13.0 0.1 pad_add_fusion.place
  13.1 2.0 %copy-done = bf16[1,2,256,3584]{3,2,1,0:T(8,128)(2,1)S(1)} copy-done((bf16[1,2,256,3584]{3,2,1,0:T(8,128)(2,1)S(1)}, bf16[1,2,256,3584]{3,2,1,0:T(8,128)(2,1)}, u32[]{:S(2)}) %copy-start) | copy-done | bytes 3670040
  15.2 1.2 %copy-done.2 = bf16[896,512]{1,0:T(8,128)(2,1)S(1)} copy-done((bf16[896,512]{1,0:T(8,128)(2,1)S(1)}, bf16[896,512]{1,0:T(8,128)(2,1)}, u32[]{:S(2)}) %copy-start.2) | copy-done | bytes 917528
  16.3 0.7 copy-done.4
  17.0 1.2 %shard_map.84 = (f32[512,512]{1,0:T(8,128)S(1)}, bf16[32,128]{1,0:T(8,128)(2,1)S(1)}) custom-call(s32[4]{0:T(128)S(1)} %pad_add_fusion.place, bf16[512,3584]{1,0:T(8,128)(2,1)S(1)} %bitcast.13, bf16[896,512]{1,0:T(8,128)(2,1)S(1)} %copy-done.2, bf16[2,1792]{1,0:T(2,128)(2,1)S(1)} %bitcast.19), custom_call_target="tpu_custom_call" | custom-call | flops 469762048 | tf_op jit(solution)/shard_map/pallas_call | solution.py:101
  18.3 0.0 copy-start.1
  18.3 0.0 copy-start.6
  18.3 0.0 copy-start.7
  18.3 0.0 collective-permute-done.2.w1
  18.3 5.9 %collective-permute-done.1.weight.near = bf16[896,512]{1,0:T(8,128)(2,1)S(1)} collective-permute-done((bf16[896,512]{1,0:T(8,128)(2,1)}, bf16[896,512]{1,0:T(8,128)(2,1)S(1)}, u32[]{:S(2)}, u32[]{:S(2)}) %collective-permute-start.1) | collective-permute-done | bytes 917536 | tf_op jit(solution)/shard_map/ppermute | solution.py:385
  24.3 2.1 %collective-permute-start.3 = (bf16[896,512]{1,0:T(8,128)(2,1)S(1)}, bf16[896,512]{1,0:T(8,128)(2,1)S(1)}, u32[]{:S(2)}, u32[]{:S(2)}) collective-permute-start(bf16[896,512]{1,0:T(8,128)(2,1)S(1)} %collective-permute-done.1.weight.near), channel_id=1, source_target_pairs={{0,4},{4,0},{8,12},{12,8},{16,20},{20,16},{24,28},{28,24},{32,36},... | collective-permute-start | bytes 2752520 | tf_op jit(solution)/shard_map/ppermute | solution.py:381
  26.3 0.0 collective-permute-start.4
  26.3 0.5 collective-permute-start.5
  26.8 1.2 %shard_map.85.before = f32[512,512]{1,0:T(8,128)S(1)} custom-call(s32[4]{0:T(128)S(1)} %pad_add_fusion.place, bf16[512,3584]{1,0:T(8,128)(2,1)S(1)} %bitcast.14, bf16[896,512]{1,0:T(8,128)(2,1)S(1)} %collective-permute-done.1.weight.near, f32[512,512]{1,0:T(8,128)S(1)} %get-tuple-element.28.before), custom_call_target="tpu_custom_call" | custom-call | flops 469762048 | tf_op jit(solution)/shard_map/pallas_call | solution.py:101
  28.1 0.7 collective-permute-done.4.w2
  28.7 0.3 collective-permute-done.5.w3
  29.1 0.0 collective-permute-done.3.near_other
  29.1 2.3 %shard_map.86 = (bf16[512,512]{1,0:T(8,128)(2,1)S(1)}, f32[32,512]{1,0:T(8,128)S(1)}, bf16[32,8,512]{2,1,0:T(8,128)(2,1)S(1)}, f32[8,1792]{1,0:T(8,128)S(1)}, f32[8,128]{1,0:T(8,128)S(1)}) custom-call(s32[4]{0:T(128)S(1)} %pad_add_fusion.place, s32[2]{0:T(128)S(1)} %bitcast.21, s32[2]{0:T(128)S(1)} %bitcast.22, bf16[512,3584]{1,0:T(8,128)(2,1)S(1)} %bitcast.15, ...), custom_call_target="tpu_custom_call" | custom-call | flops 939524096 | tf_op jit(solution)/shard_map/pallas_call | solution.py:101
  31.4 22.4 %all_to_all.10 = bf16[32,8,512]{2,1,0:T(8,128)(2,1)S(1)} all-to-all(bf16[32,8,512]{2,1,0:T(8,128)(2,1)S(1)} %get-tuple-element.35), channel_id=1, replica_groups={{0,8,16,24,32,40,48,56,64,72,80,88,96,104,112,120,128,136,144,152,160,1..., dimensions={0} | all-to-all | bytes 524288 | tf_op jit(solution)/shard_map/all_to_all | solution.py:332
  53.8 2.3 %collective-permute-start.6 = (bf16[256,512]{1,0:T(8,128)(2,1)S(1)}, bf16[256,512]{1,0:T(8,128)(2,1)S(1)}, u32[]{:S(2)}, u32[]{:S(2)}) collective-permute-start(bf16[256,512]{1,0:T(8,128)(2,1)S(1)} %bitcast.17), channel_id=1, source_target_pairs={{0,4},{4,0},{8,12},{12,8},{16,20},{20,16},{24,28},{28,24},{32,36},... | collective-permute-start | bytes 786440 | tf_op jit(solution)/shard_map/ppermute | solution.py:334
  56.1 1.2 %collective-permute-done.6.other = bf16[256,512]{1,0:T(8,128)(2,1)S(1)} collective-permute-done((bf16[256,512]{1,0:T(8,128)(2,1)S(1)}, bf16[256,512]{1,0:T(8,128)(2,1)S(1)}, u32[]{:S(2)}, u32[]{:S(2)}) %collective-permute-start.6) | collective-permute-done | bytes 262176 | tf_op jit(solution)/shard_map/ppermute | solution.py:334
  57.3 2.8 %shard_map.87 = (f32[1,128]{1,0:T(1,128)}, bf16[32,512]{1,0:T(8,128)(2,1)S(1)}, bf16[32,128]{1,0:T(8,128)(2,1)S(1)}, bf16[2,1792]{1,0:T(2,128)(2,1)}, f32[8,1792]{1,0:T(8,128)S(1)}) custom-call(s32[4]{0:T(128)S(1)} %pad_add_fusion.place, f32[32,512]{1,0:T(8,128)S(1)} %get-tuple-element.31.attn, bf16[512,512]{1,0:T(8,128)(2,1)S(1)} %get-tuple-element.32.keyval, ...), custom_call_target="tpu_custom_call" | custom-call | flops 6000000000 | tf_op jit(solution)/shard_map/pallas_call | solution.py:101
  60.1 1.3 %shard_map.89 = (bf16[16,3584]{1,0:T(8,128)(2,1)S(1)}, bf16[16,3584]{1,0:T(8,128)(2,1)S(1)}, bf16[16,3584]{1,0:T(8,128)(2,1)S(1)}, bf16[16,3584]{1,0:T(8,128)(2,1)S(1)}) custom-call(s32[4]{0:T(128)S(1)} %pad_add_fusion.place, bf16[512,3584]{1,0:T(8,128)(2,1)S(1)} %bitcast.16, bf16[32,512]{1,0:T(8,128)(2,1)S(1)} %get-tuple-element.37.grad_score, ...), custom_call_target="tpu_custom_call" | custom-call | flops 234881024 | tf_op jit(solution)/shard_map/pallas_call | solution.py:101
  61.4 0.2 collective-permute-start.7
  61.6 1.8 %collective-permute-start.8 = (bf16[16,3584]{1,0:T(8,128)(2,1)S(1)}, bf16[16,3584]{1,0:T(8,128)(2,1)S(1)}, u32[]{:S(2)}, u32[]{:S(2)}) collective-permute-start(bf16[16,3584]{1,0:T(8,128)(2,1)S(1)} %get-tuple-element.46), channel_id=1, source_target_pairs={{0,160},{4,164},{8,168},{12,172},{16,176},{20,180},{24,184},{28,18... | collective-permute-start | bytes 344072 | tf_op jit(solution)/shard_map/ppermute | solution.py:358
  63.4 2.8 %collective-permute-start.9 = (bf16[16,3584]{1,0:T(8,128)(2,1)S(1)}, bf16[16,3584]{1,0:T(8,128)(2,1)S(1)}, u32[]{:S(2)}, u32[]{:S(2)}) collective-permute-start(bf16[16,3584]{1,0:T(8,128)(2,1)S(1)} %get-tuple-element.48), channel_id=1, source_target_pairs={{0,64},{4,68},{8,72},{12,76},{16,80},{20,84},{24,88},{28,92},{32,2... | collective-permute-start | bytes 344072 | tf_op jit(solution)/shard_map/ppermute | solution.py:358
  66.2 1.2 %collective-permute-start.10 = (bf16[16,3584]{1,0:T(8,128)(2,1)S(1)}, bf16[16,3584]{1,0:T(8,128)(2,1)S(1)}, u32[]{:S(2)}, u32[]{:S(2)}) collective-permute-start(bf16[16,3584]{1,0:T(8,128)(2,1)S(1)} %get-tuple-element.42.a0), channel_id=1, source_target_pairs={{0,4},{4,0},{8,12},{12,8},{16,20},{20,16},{24,28},{28,24},{32,36},... | collective-permute-start | bytes 344072 | tf_op jit(solution)/shard_map/ppermute | solution.py:363
  67.4 0.0 copy-done.3
  67.5 4.9 %shard_map.88 = (bf16[512,3584]{1,0:T(8,128)(2,1)}, f32[8,128]{1,0:T(8,128)}) custom-call(s32[4]{0:T(128)S(1)} %pad_add_fusion.place, bf16[32,512]{1,0:T(8,128)(2,1)S(1)} %get-tuple-element.37.grad_score, f32[32,512]{1,0:T(8,128)S(1)} %get-tuple-element.31.attn, bf16[32,128]{1,0:T(8,128)(2,1)S(1)} %get-tuple-element.30.queries.query_rows, ...), custom_call_target="tpu_custom_call" | custom-call | flops 1879048192 | tf_op jit(solution)/shard_map/pallas_call | solution.py:101
  72.4 0.0 collective-permute-done.7.a1
  72.4 0.9 collective-permute-done.8.a2
  73.2 0.0 collective-permute-done.9.a3
  73.2 1.3 %collective-permute-start.11 = (bf16[16,3584]{1,0:T(8,128)(2,1)S(1)}, bf16[16,3584]{1,0:T(8,128)(2,1)S(1)}, u32[]{:S(2)}, u32[]{:S(2)}) collective-permute-start(bf16[16,3584]{1,0:T(8,128)(2,1)S(1)} %collective-permute-done.7.a1), channel_id=1, source_target_pairs={{0,4},{4,0},{8,12},{12,8},{16,20},{20,16},{24,28},{28,24},{32,36},... | collective-permute-start | bytes 344072 | tf_op jit(solution)/shard_map/ppermute | solution.py:363
  74.5 0.0 collective-permute-start.12
  74.5 0.5 collective-permute-start.13
  75.1 0.0 collective-permute-done.10.b0
  75.1 0.5 collective-permute-done.11.b1
  75.5 0.4 collective-permute-done.12.b2
  75.9 0.2 collective-permute-done.13.b3
  76.0 1.1 %shard_map.90 = bf16[64,3584]{1,0:T(8,128)(2,1)S(1)} custom-call(s32[4]{0:T(128)S(1)} %pad_add_fusion.place, bf16[16,3584]{1,0:T(8,128)(2,1)S(1)} %get-tuple-element.42.a0, bf16[16,3584]{1,0:T(8,128)(2,1)S(1)} %collective-permute-done.7.a1, bf16[16,3584]{1,0:T(8,128)(2,1)S(1)} %collective-permute-done.8.a2, bf16[16,3584]{1,0:T(8,128)(2,1)S(1)} %collective-permute-done.9.a3, ...), custom_call_target="tpu_custom_call" | custom-call | tf_op jit(solution)/shard_map/pallas_call | solution.py:101
  77.2 0.2 reshape.23
  77.4 16.9 %all_to_all.11 = bf16[32,2,3584]{2,1,0:T(2,128)(2,1)S(1)} all-to-all(bf16[32,2,3584]{2,1,0:T(2,128)(2,1)S(1)} %reshape.23), channel_id=1, replica_groups={{0,1,2,3,8,9,10,11,16,17,18,19,24,25,26,27,32,33,34,35,40,41,42,43,48,4..., dimensions={0} | all-to-all | bytes 917504 | tf_op jit(solution)/shard_map/all_to_all | solution.py:367
  94.2 1.0 %convert_reduce_fusion = f32[2,3584]{1,0:T(2,128)} fusion(bf16[32,2,3584]{2,1,0:T(2,128)(2,1)S(1)} %all_to_all.11), kind=kLoop, calls=%fused_computation | loop fusion | flops 451584 | bytes 487424 | tf_op jit(solution)/shard_map/reduce_sum | solution.py:368
  (9 shorter events, 0.0 us)
Async XLA Ops:
  1.6 8.1 %collective-permute-start = (bf16[896,128]{1,0:T(8,128)(2,1)S(1)}, bf16[896,128]{1,0:T(8,128)(2,1)S(1)}, u32[]{:S(2)}, u32[]{:S(2)}) collective-permute-start(bf16[896,128]{1,0:T(8,128)(2,1)S(1)} %constant_dynamic-slice_fusion), channel_id=1, source_target_pairs={{0,2},{1,3},{2,0},{3,1},{4,6},{5,7},{6,4},{7,5},{8,10},{9,11},{10,... | collective-permute-start | bytes 688136 | tf_op jit(solution)/shard_map/ppermute | solution.py:384
  9.7 14.5 %collective-permute-start.1 = (bf16[896,512]{1,0:T(8,128)(2,1)}, bf16[896,512]{1,0:T(8,128)(2,1)S(1)}, u32[]{:S(2)}, u32[]{:S(2)}) collective-permute-start(bf16[896,512]{1,0:T(8,128)(2,1)} %own.1), channel_id=1, source_target_pairs={{0,3},{1,0},{2,1},{3,2},{4,5},{5,6},{6,7},{7,4},{8,11},{9,8},{10,9... | collective-permute-start | bytes 2752520 | tf_op jit(solution)/shard_map/ppermute | solution.py:385
  11.8 6.5 %collective-permute-start.2 = (bf16[896,128]{1,0:T(8,128)(2,1)S(1)}, bf16[896,128]{1,0:T(8,128)(2,1)S(1)}, u32[]{:S(2)}, u32[]{:S(2)}) collective-permute-start(bf16[896,128]{1,0:T(8,128)(2,1)S(1)} %collective-permute-done.w0), channel_id=1, source_target_pairs={{0,8},{4,12},{8,0},{12,4},{16,24},{20,28},{24,16},{28,20},{32,40},... | collective-permute-start | bytes 688136 | tf_op jit(solution)/shard_map/ppermute | solution.py:386
  13.1 2.0 %copy-start = (bf16[1,2,256,3584]{3,2,1,0:T(8,128)(2,1)S(1)}, bf16[1,2,256,3584]{3,2,1,0:T(8,128)(2,1)}, u32[]{:S(2)}) copy-start(bf16[1,2,256,3584]{3,2,1,0:T(8,128)(2,1)} %param.5) | copy-start | bytes 11010052
  15.2 1.2 %copy-start.2 = (bf16[896,512]{1,0:T(8,128)(2,1)S(1)}, bf16[896,512]{1,0:T(8,128)(2,1)}, u32[]{:S(2)}) copy-start(bf16[896,512]{1,0:T(8,128)(2,1)} %own.1) | copy-start | bytes 2752516
  16.3 0.7 copy-start.4
  18.3 10.8 %copy-start.1 = (bf16[1,2,256,3584]{3,2,1,0:T(8,128)(2,1)S(1)}, bf16[1,2,256,3584]{3,2,1,0:T(8,128)(2,1)}, u32[]{:S(2)}) copy-start(bf16[1,2,256,3584]{3,2,1,0:T(8,128)(2,1)} %param.5) | copy-start | bytes 11010052
  18.3 10.8 %copy-start.6 = (s32[1,2]{1,0:T(1,128)S(1)}, s32[1,2]{1,0:T(1,128)}, u32[]{:S(2)}) copy-start(s32[1,2]{1,0:T(1,128)} %param.6) | copy-start | bytes 28
  18.3 10.8 %copy-start.7 = (s32[1,2]{1,0:T(1,128)S(1)}, s32[1,2]{1,0:T(1,128)}, u32[]{:S(2)}) copy-start(s32[1,2]{1,0:T(1,128)} %param.8) | copy-start | bytes 28
  24.3 4.8 %collective-permute-start.3 = (bf16[896,512]{1,0:T(8,128)(2,1)S(1)}, bf16[896,512]{1,0:T(8,128)(2,1)S(1)}, u32[]{:S(2)}, u32[]{:S(2)}) collective-permute-start(bf16[896,512]{1,0:T(8,128)(2,1)S(1)} %collective-permute-done.1.weight.near), channel_id=1, source_target_pairs={{0,4},{4,0},{8,12},{12,8},{16,20},{20,16},{24,28},{28,24},{32,36},... | collective-permute-start | bytes 2752520 | tf_op jit(solution)/shard_map/ppermute | solution.py:381
  26.3 2.4 %collective-permute-start.4 = (bf16[896,128]{1,0:T(8,128)(2,1)S(1)}, bf16[896,128]{1,0:T(8,128)(2,1)S(1)}, u32[]{:S(2)}, u32[]{:S(2)}) collective-permute-start(bf16[896,128]{1,0:T(8,128)(2,1)S(1)} %collective-permute-done.w0), channel_id=1, source_target_pairs={{0,4},{4,0},{8,12},{12,8},{16,20},{20,16},{24,28},{28,24},{32,36},... | collective-permute-start | bytes 688136 | tf_op jit(solution)/shard_map/ppermute | solution.py:381
  26.3 2.8 %collective-permute-start.5 = (bf16[896,128]{1,0:T(8,128)(2,1)S(1)}, bf16[896,128]{1,0:T(8,128)(2,1)S(1)}, u32[]{:S(2)}, u32[]{:S(2)}) collective-permute-start(bf16[896,128]{1,0:T(8,128)(2,1)S(1)} %collective-permute-done.2.w1), channel_id=1, source_target_pairs={{0,4},{4,0},{8,12},{12,8},{16,20},{20,16},{24,28},{28,24},{32,36},... | collective-permute-start | bytes 688136 | tf_op jit(solution)/shard_map/ppermute | solution.py:381
  53.8 3.5 %collective-permute-start.6 = (bf16[256,512]{1,0:T(8,128)(2,1)S(1)}, bf16[256,512]{1,0:T(8,128)(2,1)S(1)}, u32[]{:S(2)}, u32[]{:S(2)}) collective-permute-start(bf16[256,512]{1,0:T(8,128)(2,1)S(1)} %bitcast.17), channel_id=1, source_target_pairs={{0,4},{4,0},{8,12},{12,8},{16,20},{20,16},{24,28},{28,24},{32,36},... | collective-permute-start | bytes 786440 | tf_op jit(solution)/shard_map/ppermute | solution.py:334
  57.3 2.8 %copy-start.5 = (bf16[1,2,1792]{2,1,0:T(2,128)(2,1)S(1)}, bf16[1,2,1792]{2,1,0:T(2,128)(2,1)}, u32[]{:S(2)}) copy-start(bf16[1,2,1792]{2,1,0:T(2,128)(2,1)} %param.7) | copy-start | bytes 21508
  60.1 7.4 %copy-start.3 = (bf16[896,512]{1,0:T(8,128)(2,1)S(1)}, bf16[896,512]{1,0:T(8,128)(2,1)}, u32[]{:S(2)}) copy-start(bf16[896,512]{1,0:T(8,128)(2,1)} %own.1) | copy-start | bytes 2752516
  61.4 11.0 %collective-permute-start.7 = (bf16[16,3584]{1,0:T(8,128)(2,1)S(1)}, bf16[16,3584]{1,0:T(8,128)(2,1)S(1)}, u32[]{:S(2)}, u32[]{:S(2)}) collective-permute-start(bf16[16,3584]{1,0:T(8,128)(2,1)S(1)} %get-tuple-element.43), channel_id=1, source_target_pairs={{0,224},{4,228},{8,232},{12,236},{16,240},{20,244},{24,248},{28,25... | collective-permute-start | bytes 344072 | tf_op jit(solution)/shard_map/ppermute | solution.py:358
  61.6 11.6 %collective-permute-start.8 = (bf16[16,3584]{1,0:T(8,128)(2,1)S(1)}, bf16[16,3584]{1,0:T(8,128)(2,1)S(1)}, u32[]{:S(2)}, u32[]{:S(2)}) collective-permute-start(bf16[16,3584]{1,0:T(8,128)(2,1)S(1)} %get-tuple-element.46), channel_id=1, source_target_pairs={{0,160},{4,164},{8,168},{12,172},{16,176},{20,180},{24,184},{28,18... | collective-permute-start | bytes 344072 | tf_op jit(solution)/shard_map/ppermute | solution.py:358
  63.4 9.8 %collective-permute-start.9 = (bf16[16,3584]{1,0:T(8,128)(2,1)S(1)}, bf16[16,3584]{1,0:T(8,128)(2,1)S(1)}, u32[]{:S(2)}, u32[]{:S(2)}) collective-permute-start(bf16[16,3584]{1,0:T(8,128)(2,1)S(1)} %get-tuple-element.48), channel_id=1, source_target_pairs={{0,64},{4,68},{8,72},{12,76},{16,80},{20,84},{24,88},{28,92},{32,2... | collective-permute-start | bytes 344072 | tf_op jit(solution)/shard_map/ppermute | solution.py:358
  66.2 8.8 %collective-permute-start.10 = (bf16[16,3584]{1,0:T(8,128)(2,1)S(1)}, bf16[16,3584]{1,0:T(8,128)(2,1)S(1)}, u32[]{:S(2)}, u32[]{:S(2)}) collective-permute-start(bf16[16,3584]{1,0:T(8,128)(2,1)S(1)} %get-tuple-element.42.a0), channel_id=1, source_target_pairs={{0,4},{4,0},{8,12},{12,8},{16,20},{20,16},{24,28},{28,24},{32,36},... | collective-permute-start | bytes 344072 | tf_op jit(solution)/shard_map/ppermute | solution.py:363
  73.2 2.3 %collective-permute-start.11 = (bf16[16,3584]{1,0:T(8,128)(2,1)S(1)}, bf16[16,3584]{1,0:T(8,128)(2,1)S(1)}, u32[]{:S(2)}, u32[]{:S(2)}) collective-permute-start(bf16[16,3584]{1,0:T(8,128)(2,1)S(1)} %collective-permute-done.7.a1), channel_id=1, source_target_pairs={{0,4},{4,0},{8,12},{12,8},{16,20},{20,16},{24,28},{28,24},{32,36},... | collective-permute-start | bytes 344072 | tf_op jit(solution)/shard_map/ppermute | solution.py:363
  74.5 1.3 %collective-permute-start.12 = (bf16[16,3584]{1,0:T(8,128)(2,1)S(1)}, bf16[16,3584]{1,0:T(8,128)(2,1)S(1)}, u32[]{:S(2)}, u32[]{:S(2)}) collective-permute-start(bf16[16,3584]{1,0:T(8,128)(2,1)S(1)} %collective-permute-done.8.a2), channel_id=1, source_target_pairs={{0,4},{4,0},{8,12},{12,8},{16,20},{20,16},{24,28},{28,24},{32,36},... | collective-permute-start | bytes 344072 | tf_op jit(solution)/shard_map/ppermute | solution.py:363
  74.5 1.5 %collective-permute-start.13 = (bf16[16,3584]{1,0:T(8,128)(2,1)S(1)}, bf16[16,3584]{1,0:T(8,128)(2,1)S(1)}, u32[]{:S(2)}, u32[]{:S(2)}) collective-permute-start(bf16[16,3584]{1,0:T(8,128)(2,1)S(1)} %collective-permute-done.9.a3), channel_id=1, source_target_pairs={{0,4},{4,0},{8,12},{12,8},{16,20},{20,16},{24,28},{28,24},{32,36},... | collective-permute-start | bytes 344072 | tf_op jit(solution)/shard_map/ppermute | solution.py:363

commit v4 on v3

--- a/solution.py
+++ b/solution.py
@@ -34,10 +34,18 @@
 
 OTHER_CORE = [(i, i ^ 1) for i in range(N_DP)]
 CHIPS = [[dp_index(z, x, c) for z in range(NZ) for x in range(NX)] for c in range(NC)]
-X_MATE = [(i, i ^ NC) for i in range(N_DP)]
 
 
 Y_ACROSS = [(i, (i + 2) % NY) for i in range(NY)]
+
+
+def x_shift(k):
+    return [
+        (dp_index(z, x, c), dp_index(z, (x + k) % NX, c))
+        for z in range(NZ)
+        for x in range(NX)
+        for c in range(NC)
+    ]
 
 
 def y_mirror():
@@ -46,17 +54,6 @@
         for dp in range(N_DP)
         for y in range(NY)
     ]
-
-
-def plane_shift(dz=0, dx=0, mirror=False):
-    pairs = []
-    for z in range(NZ):
-        for x in range(NX):
-            for c in range(NC):
-                sign = -1 if mirror and c == 0 else 1
-                to = dp_index((z + sign * dz) % NZ, (x + sign * dx) % NX, c)
-                pairs.append((dp_index(z, x, c), to))
-    return pairs
 
 
 OWNERS = [
@@ -130,25 +127,31 @@
     return block_at(place, jnp.where(place[1] == 0, NY - 1, 1), shard)
 
 
-def across_block(place, mine, mate, other, other_mate):
-    low, first = place[3] == 0, place[1] == 0
-    a = [jnp.where(low, mine[...], mate[...]), jnp.where(low, mate[...], mine[...])]
-    b = [jnp.where(low, other[...], other_mate[...]), jnp.where(low, other_mate[...], other[...])]
-    keys = [jnp.where(first, p, q) for p, q in zip(a, b)]
-    values = [jnp.where(first, q, p) for p, q in zip(a, b)]
-    return jnp.concatenate(keys + values, axis=1)
-
-
-def own_body(place, tokens, weight, queries, out, rows, flat):
+def half_body(place, a0, a1, a2, a3, out):
+    rows = a0.shape[0]
+    for k, piece in enumerate((a0, a1, a2, a3)):
+        source = lax.rem(place[3] + NX - k, NX)
+        at = pl.multiple_of((source // KVH) * rows, rows)
+        lane = pl.multiple_of(lax.rem(source, KVH) * HD, HD)
+        out[pl.ds(at, rows), pl.ds(lane, HD)] = piece[...]
+
+
+def across_block(place, half, half_other):
+    first = place[1] == 0
+    a, b = half[...], half_other[...]
+    return jnp.concatenate([jnp.where(first, a, b), jnp.where(first, b, a)], axis=1)
+
+
+def own_body(place, tokens, weight, out):
     shard = weight.shape[0]
     out[...] = dot_nn(tokens[:, pl.ds(block_at(place, 0, shard), shard)], weight[...])
-    from_lanes(queries[...].astype(F32), flat)
-    rows[...] = flat[...].astype(BF16)
-
-
-def near_body(place, tokens, weight, before, out):
+
+
+def near_body(place, tokens, weight, half, half_other, before, out):
     shard = weight.shape[0]
+    across = across_block(place, half, half_other)
     part = dot_nn(tokens[:, pl.ds(near_at(place, shard), shard)], weight[...])
+    part += dot_nn(tokens[:, pl.ds(block_at(place, 2, shard), shard)], across)
     out[...] = before[...] + part
 
 
@@ -175,21 +178,19 @@
 
 
 def attend_body(
-    place, lens, marks, tokens, before, near_other, w0, w1, w2, w3, queries,
-    keyval, attn, spread, unit, norm, flat,
+    place, lens, marks, tokens, before, near_other, queries,
+    keyval, attn, spread, unit, norm, rows, flat, lined,
 ):
     shard = near_other.shape[0]
-    blocks = [
-        (near_other_at(place, shard), near_other[...]),
-        (block_at(place, 2, shard), across_block(place, w0, w1, w2, w3)),
-    ]
-    total = before[...]
-    for at, block in blocks:
-        total += dot_nn(tokens[:, pl.ds(at, shard)], block)
+    part = dot_nn(tokens[:, pl.ds(near_other_at(place, shard), shard)], near_other[...])
+    total = before[...] + part
     both = total.astype(BF16)
     keyval[...] = both
+    from_lanes(queries[...].astype(F32), lined)
+    query_rows = lined[...].astype(BF16)
+    rows[...] = query_rows
     scores = jnp.concatenate(
-        [dot_nt(queries[h * SIDE : (h + 1) * SIDE, :], head(both, h)) for h in range(KVH)], axis=0
+        [dot_nt(query_rows[h * SIDE : (h + 1) * SIDE], head(both, h)) for h in range(KVH)], axis=0
     ) * HD ** (-0.5)
     mask = row_mask(lens, both.shape[0] // DOCS)
     expvals = jnp.where(mask, jnp.exp(jnp.where(mask, scores, 0.0)), 0.0)
@@ -221,15 +222,22 @@
 
 def contrast_body(
     place, attn, keyval, unit, norm, mine, other,
-    loss, grad_score, grad_rows, grad_query, grad_read, flat, lanes,
+    loss, grad_score, grad_rows, grad_read, flat,
 ):
     half_docs = mine.shape[0] // FOLD
     total_docs = NC * half_docs
-    to = lax.broadcasted_iota(jnp.int32, (half_docs, mine.shape[0]), 0)
-    at = lax.broadcasted_iota(jnp.int32, (half_docs, mine.shape[0]), 1)
-    base = (to // DOCS) * (FOLD * DOCS) + to % DOCS
-    ones = [jnp.where(at == base + i * DOCS, 1.0, 0.0).astype(BF16) for i in range(FOLD)]
-    unfold = lambda a: jnp.concatenate([dot_nn(one, a[...]) for one in ones], axis=1)
+    count = mine.shape[0]
+    to = lax.broadcasted_iota(jnp.int32, (count, count), 0)
+    at = lax.broadcasted_iota(jnp.int32, (count, count), 1)
+    doc = to % half_docs
+    base = (doc // DOCS) * (FOLD * DOCS) + (to // half_docs) * DOCS + doc % DOCS
+    order = jnp.where(at == base, 1.0, 0.0).astype(BF16)
+
+    def unfold(a):
+        rows = dot_nn(order, a[...])
+        parts = [rows[i * half_docs : (i + 1) * half_docs] for i in range(FOLD)]
+        return jnp.concatenate(parts, axis=1)
+
     gathered = jnp.concatenate([unfold(mine), unfold(other)], axis=0)
     span = HALF + HD
     everyone = jnp.concatenate([gathered[:, :HALF], gathered[:, span : span + HALF]], axis=1)
@@ -278,9 +286,6 @@
     inner = jnp.sum(probs * grad_w, axis=-1, keepdims=True)
     score = (probs * (grad_w - inner) * HD ** (-0.5)).astype(BF16)
     grad_score[...] = score
-    for h in range(KVH):
-        to_lanes(dot_nn(score[sides[h]], head(keyval, h)), h, lanes)
-    grad_query[...] = lanes[:DOCS, :].astype(BF16)
 
 
 def factor_body(place, tokens, grad_score, attn, queries, grad_read, *outs):
@@ -309,7 +314,8 @@
 
 
 def token_body(
-    place, grad_score, attn, query_rows, grad_rows, own, near, near_other, w0, w1, w2, w3, out, done
+    place, grad_score, attn, query_rows, grad_rows, keyval, own, near, near_other, half, half_other,
+    out, grad_query, done, lanes,
 ):
     shard = own.shape[0]
     probs = attn[...].astype(BF16)
@@ -321,10 +327,14 @@
         (block_at(place, 0, shard), own[...]),
         (near_at(place, shard), near[...]),
         (near_other_at(place, shard), near_other[...]),
-        (block_at(place, 2, shard), across_block(place, w0, w1, w2, w3)),
+        (block_at(place, 2, shard), across_block(place, half, half_other)),
     ]
     for at, block in blocks:
         out[:, pl.ds(at, shard)] = dot_nt(grad_keyval, block).astype(BF16)
+    lanes[...] = jnp.zeros_like(lanes)
+    for h in range(KVH):
+        to_lanes(dot_nn(grad_score[sides[h], :], head(keyval, h)), h, lanes)
+    grad_query[...] = lanes[:DOCS, :].astype(BF16)
     done[...] = probs[:SLOT, :HD].astype(F32)
 
 
@@ -374,43 +384,49 @@
     count = docs * block
     dp = lax.axis_index("dp")
     core = dp % NC
-    parity = (dp // NC) % 2
+    x = (dp // NC) % NX
     y = lax.axis_index("fsdp")
-    place = jnp.stack([y, core, dp * docs, parity]).astype(jnp.int32)
+    place = jnp.stack([y, core, dp * docs, x]).astype(jnp.int32)
     rows = tokens.reshape(count, width)
     swap = lambda a: lax.ppermute(a, "dp", OTHER_CORE)
 
-    piece = lax.dynamic_slice(kv_weight, (0, (2 * core + parity) * HD), (shard, HD))
-    mine = lax.ppermute(piece, "fsdp", Y_ACROSS)
+    flops = 2 * count * shard * KVW
+    (part,) = call(
+        own_body, (place,), (rows, kv_weight), [((count, KVW), F32)], flops=flops, limit=8
+    )
+    piece = lax.dynamic_slice(
+        kv_weight, ((x // KVH) * (shard // 2), (KVH * core + x % KVH) * HD), (shard // 2, HD)
+    )
+    mine = tie(lax.ppermute(piece, "fsdp", Y_ACROSS), part)
     near = lax.ppermute(tie(kv_weight, mine), ("dp", "fsdp"), y_mirror())
-    mate = lax.ppermute(mine, "dp", X_MATE)
-
-    flops = 2 * count * shard * KVW
-    part, query_rows = call(
-        own_body, (place,), (rows, kv_weight, queries[0]),
-        [((count, KVW), F32), ((ROWS, HD), BF16)], [pltpu.VMEM((ROWS, HD), F32)], flops=flops, limit=8,
-    )
-    near = tie(near, mate, part)
-    across = (mine, mate, swap(mine), swap(mate))
+    pieces = [mine] + [lax.ppermute(mine, "dp", x_shift(k)) for k in (1, 2, 3)]
+    (half,) = call(half_body, (place,), pieces, [((shard, KVH * HD), BF16)])
+    half_other = swap(half)
+
+    near = tie(near, half_other)
     near_other = swap(near)
-    (part,) = call(near_body, (place,), (rows, near, part), [((count, KVW), F32)], flops=flops, limit=8)
-    keyval, attn, spread, unit, norm = call(
+    (part,) = call(
+        near_body, (place,), (rows, near, half, half_other, part), [((count, KVW), F32)],
+        flops=2 * flops, limit=8,
+    )
+    keyval, attn, spread, unit, norm, query_rows = call(
         attend_body,
         (place, lengths[0], positives[0]),
-        (rows, part, near_other, *across, query_rows),
+        (rows, part, near_other, queries[0]),
         [
             ((count, KVW), BF16),
             ((ROWS, count), F32),
             ((NZ * NX, FOLD * docs, 2 * (HALF + HD) // FOLD), BF16),
             ((SLOT, QW), F32),
             ((SLOT, HD), F32),
+            ((ROWS, HD), BF16),
         ],
-        [pltpu.VMEM((SLOT, QW), F32)],
+        [pltpu.VMEM((SLOT, QW), F32), pltpu.VMEM((ROWS, HD), F32)],
         flops=2 * flops,
         limit=16,
     )
     everyone = gather_docs(spread)
-    loss, grad_score, grad_rows, grad_query, grad_read = call(
+    loss, grad_score, grad_rows, grad_read = call(
         contrast_body,
         (place,),
         (attn, keyval, unit, norm, *everyone),
@@ -418,10 +434,9 @@
             ((1, HD), F32),
             ((ROWS, count), BF16),
             ((ROWS, HD), BF16),
-            ((docs, QW), BF16),
             ((SLOT, QW), F32),
         ],
-        [pltpu.VMEM((ROWS, HD), F32), pltpu.VMEM((SLOT, QW), F32)],
+        [pltpu.VMEM((ROWS, HD), F32)],
         flops=6_000_000_000,
         limit=8,
     )
@@ -434,11 +449,12 @@
         limit=8,
     )
     quads = exchange_types(factors)
-    grad_tok, done = call(
+    grad_tok, grad_query, done = call(
         token_body,
         (place,),
-        (grad_score, attn, query_rows, grad_rows, kv_weight, near, near_other, *across),
-        [((count, width), BF16), ((SLOT, HD), F32)],
+        (grad_score, attn, query_rows, grad_rows, keyval, kv_weight, near, near_other, half, half_other),
+        [((count, width), BF16), ((docs, QW), BF16), ((SLOT, HD), F32)],
+        [pltpu.VMEM((SLOT, QW), F32)],
         flops=4 * flops,
         limit=20,
     )

time: 95.5 us -> 91 us (0.953)
  waiting for transfers between devices: 14.2 us -> 10.3 us
  blocking collectives: 39.3 us -> 37.6 us
  starting transfers between devices: 19.9 us -> 21.5 us
    ppermute x1, waiting for transfers between devices: 5.93 us -> 0.01 us  [local(): near = lax.ppermute(tie(kv_weight, mine), ('dp', 'fsdp'), y_mirror())]
    ppermute x2 -> x4, starting transfers between devices: 5.04 us -> 7.35 us  [the longest x1 3.74 us: local(): mine = tie(lax.ppermute(piece, 'fsdp', Y_ACROSS), part)]
    ppermute x1, starting transfers between devices: 2.09 us -> 0.48 us  [local(): near = lax.ppermute(tie(kv_weight, mine), ('dp', 'fsdp'), y_mirror())]
    ppermute x3 -> x2, starting transfers between devices: 2.57 us -> 4.02 us  [local(): swap = lambda a: lax.ppermute(a, 'dp', OTHER_CORE)]
    all_to_all x1, blocking collectives: 22.4 us -> 21.3 us  [gather_docs(): got = lax.all_to_all(spread, 'dp', 0, 0, axis_index_groups=CHIPS)]
    ppermute x2 -> x4, waiting for transfers between devices: 4.27 us -> 5.25 us  [the longest x3 5.25 us: local(): pieces = [mine] + [lax.ppermute(mine, 'dp', x_shift(k)) for k in (1, 2, 3)]]
    unnamed x16 -> x14, local copies, waits for them, and re-layouts: 3.94 us -> 3.24 us
    pallas_call x7 -> x8, Pallas kernels: 14.9 us -> 15.1 us  [call(): pl.pallas_call(body, out_shape=[jax.ShapeDtypeStruct(s, d) for s, d in ou...]
  transfers between devices with their start and end apart: 14 -> 15, of which waited for: 9 -> 9; matrix products, arithmetic and copies ran while one was open for 0% -> 0% of each run, Pallas kernels for 8% -> 9%
where the time goes in v4:
time: 91 us; the launch traced here: 90.7 us
  blocking collectives  37.6 us (41%)
  starting transfers between devices  21.5 us (24%)
  Pallas kernels  15.1 us (17%)
  waiting for transfers between devices  10.3 us (11%)
  local copies, waits for them, and re-layouts  4.33 us (5%)
  other arithmetic  1.06 us (1%)
    all_to_all x1, blocking collectives, gather_docs(): got = lax.all_to_all(spread, 'dp', 0, 0, axis_index_groups=CHIPS)  21.3 us
    all_to_all x1, blocking collectives, reduce_weight(): got = lax.all_to_all(pieces, ('dp', 'fsdp'), 0, 0, axis_index_groups=OWNERS)  16.2 us
    pallas_call x8, Pallas kernels, call(): pl.pallas_call(body, out_shape=[jax.ShapeDtypeStruct(s, d) for s, d in ou...  15.1 us
    ppermute x3, waiting for transfers between devices, local(): pieces = [mine] + [lax.ppermute(mine, 'dp', x_shift(k)) for k in (1, 2, 3)]  5.25 us
    ppermute x3, starting transfers between devices, exchange_types(): lax.ppermute(a, 'dp', parity_shift(k))  4.85 us
    ppermute x2, starting transfers between devices, local(): swap = lambda a: lax.ppermute(a, 'dp', OTHER_CORE)  4.02 us
    ppermute x1, starting transfers between devices, local(): mine = tie(lax.ppermute(piece, 'fsdp', Y_ACROSS), part)  3.74 us
    ppermute x3, starting transfers between devices, local(): pieces = [mine] + [lax.ppermute(mine, 'dp', x_shift(k)) for k in (1, 2, 3)]  3.6 us
  transfers between devices with their start and end apart: 15, of which 9 were waited for; matrix products, arithmetic and copies ran while one was open for 0% of the time, Pallas kernels for 9%

profile of v4, /device:TPU:1, one launch (start us, length us, event | category | flops | bytes accessed | tf_op | source)
XLA Modules:
  0.0 90.7 jit_solution(5531986732040847279)
XLA Ops:
  0.7 0.9 %dynamic_slice.3 = bf16[448,128]{1,0:T(8,128)(2,1)S(1)} dynamic-slice(bf16[896,512]{1,0:T(8,128)(2,1)} %own.1, s32[]{:T(128)S(6)} %select_n.32, s32[]{:T(128)S(6)} %select_n.34), dynamic_slice_sizes={448,128} | dynamic-slice | bytes 229380 | tf_op jit(solution)/shard_map/dynamic_slice | solution.py:397
  1.6 3.7 %collective-permute-start = (bf16[448,128]{1,0:T(8,128)(2,1)S(1)}, bf16[448,128]{1,0:T(8,128)(2,1)S(1)}, u32[]{:S(2)}, u32[]{:S(2)}) collective-permute-start(bf16[448,128]{1,0:T(8,128)(2,1)S(1)} %dynamic_slice.3), channel_id=1, source_target_pairs={{0,2},{1,3},{2,0},{3,1},{4,6},{5,7},{6,4},{7,5},{8,10},{9,11},{10,... | collective-permute-start | bytes 344072 | tf_op jit(solution)/shard_map/ppermute | solution.py:400
  5.4 0.1 pad_add_fusion.place
  5.4 2.0 %copy-done = bf16[1,2,256,3584]{3,2,1,0:T(8,128)(2,1)S(1)} copy-done((bf16[1,2,256,3584]{3,2,1,0:T(8,128)(2,1)S(1)}, bf16[1,2,256,3584]{3,2,1,0:T(8,128)(2,1)}, u32[]{:S(2)}) %copy-start) | copy-done | bytes 3670040
  7.5 1.2 %copy-done.2 = bf16[896,512]{1,0:T(8,128)(2,1)S(1)} copy-done((bf16[896,512]{1,0:T(8,128)(2,1)S(1)}, bf16[896,512]{1,0:T(8,128)(2,1)}, u32[]{:S(2)}) %copy-start.2) | copy-done | bytes 917528
  8.7 1.2 %shard_map.84.before = f32[512,512]{1,0:T(8,128)S(1)} custom-call(s32[4]{0:T(128)S(1)} %pad_add_fusion.place, bf16[512,3584]{1,0:T(8,128)(2,1)S(1)} %bitcast.13, bf16[896,512]{1,0:T(8,128)(2,1)S(1)} %copy-done.2), custom_call_target="tpu_custom_call" | custom-call | flops 469762048 | tf_op jit(solution)/shard_map/pallas_call | solution.py:98
  9.9 0.0 collective-permute-done.a0
  9.9 0.5 collective-permute-start.1
  10.4 2.5 %collective-permute-start.4 = (bf16[448,128]{1,0:T(8,128)(2,1)S(1)}, bf16[448,128]{1,0:T(8,128)(2,1)S(1)}, u32[]{:S(2)}, u32[]{:S(2)}) collective-permute-start(bf16[448,128]{1,0:T(8,128)(2,1)S(1)} %collective-permute-done.a0), channel_id=1, source_target_pairs={{0,24},{4,28},{8,0},{12,4},{16,8},{20,12},{24,16},{28,20},{32,56},... | collective-permute-start | bytes 344072 | tf_op jit(solution)/shard_map/ppermute | solution.py:402
  12.9 0.5 collective-permute-start.3
  13.4 0.6 collective-permute-start.2
  14.0 1.2 %collective-permute-done.4.a3 = bf16[448,128]{1,0:T(8,128)(2,1)S(1)} collective-permute-done((bf16[448,128]{1,0:T(8,128)(2,1)S(1)}, bf16[448,128]{1,0:T(8,128)(2,1)S(1)}, u32[]{:S(2)}, u32[]{:S(2)}) %collective-permute-start.4) | collective-permute-done | bytes 114720 | tf_op jit(solution)/shard_map/ppermute | solution.py:402
  15.2 2.9 %collective-permute-done.3.a2 = bf16[448,128]{1,0:T(8,128)(2,1)S(1)} collective-permute-done((bf16[448,128]{1,0:T(8,128)(2,1)S(1)}, bf16[448,128]{1,0:T(8,128)(2,1)S(1)}, u32[]{:S(2)}, u32[]{:S(2)}) %collective-permute-start.3) | collective-permute-done | bytes 114720 | tf_op jit(solution)/shard_map/ppermute | solution.py:402
  18.1 1.1 %collective-permute-done.2.a1 = bf16[448,128]{1,0:T(8,128)(2,1)S(1)} collective-permute-done((bf16[448,128]{1,0:T(8,128)(2,1)S(1)}, bf16[448,128]{1,0:T(8,128)(2,1)S(1)}, u32[]{:S(2)}, u32[]{:S(2)}) %collective-permute-start.2) | collective-permute-done | bytes 114720 | tf_op jit(solution)/shard_map/ppermute | solution.py:402
  19.2 0.6 shard_map.85.half
  19.9 0.0 copy-start.4
  19.9 0.0 copy-start.5
  19.9 0.0 copy-start.6
  19.9 3.6 %collective-permute-start.5 = (bf16[896,256]{1,0:T(8,128)(2,1)S(1)}, bf16[896,256]{1,0:T(8,128)(2,1)S(1)}, u32[]{:S(2)}, u32[]{:S(2)}) collective-permute-start(bf16[896,256]{1,0:T(8,128)(2,1)S(1)} %shard_map.85.half), channel_id=1, source_target_pairs={{0,4},{4,0},{8,12},{12,8},{16,20},{20,16},{24,28},{28,24},{32,36},... | collective-permute-start | bytes 1376264 | tf_op jit(solution)/shard_map/ppermute | solution.py:391
  23.6 1.4 %collective-permute-done.5.half_other = bf16[896,256]{1,0:T(8,128)(2,1)S(1)} collective-permute-done((bf16[896,256]{1,0:T(8,128)(2,1)S(1)}, bf16[896,256]{1,0:T(8,128)(2,1)S(1)}, u32[]{:S(2)}, u32[]{:S(2)}) %collective-permute-start.5) | collective-permute-done | bytes 458784 | tf_op jit(solution)/shard_map/ppermute | solution.py:391
  25.0 0.0 collective-permute-done.1.weight.near
  25.0 0.4 collective-permute-start.6
  25.4 1.8 %shard_map.86.before = f32[512,512]{1,0:T(8,128)S(1)} custom-call(s32[4]{0:T(128)S(1)} %pad_add_fusion.place, bf16[512,3584]{1,0:T(8,128)(2,1)S(1)} %bitcast.14, bf16[896,512]{1,0:T(8,128)(2,1)S(1)} %collective-permute-done.1.weight.near, bf16[896,256]{1,0:T(8,128)(2,1)S(1)} %shard_map.85.half, bf16[896,256]{1,0:T(8,128)(2,1)S(1)} %collective-permute-done.5.half_other, ...), custom_call_target="tpu_custom_call" | custom-call | flops 939524096 | tf_op jit(solution)/shard_map/pallas_call | solution.py:98
  27.2 0.3 collective-permute-done.6.near_other
  27.5 1.8 %shard_map.87 = (bf16[512,512]{1,0:T(8,128)(2,1)S(1)}, f32[32,512]{1,0:T(8,128)S(1)}, bf16[32,8,512]{2,1,0:T(8,128)(2,1)S(1)}, f32[8,1792]{1,0:T(8,128)S(1)}, f3...) custom-call(s32[4]{0:T(128)S(1)} %pad_add_fusion.place, s32[2]{0:T(128)S(1)} %bitcast.21, s32[2]{0:T(128)S(1)} %bitcast.22, ...), custom_call_target="tpu_custom_call" | custom-call | flops 939524096 | tf_op jit(solution)/shard_map/pallas_call | solution.py:98
  29.3 21.3 %all_to_all.10 = bf16[32,8,512]{2,1,0:T(8,128)(2,1)S(1)} all-to-all(bf16[32,8,512]{2,1,0:T(8,128)(2,1)S(1)} %get-tuple-element.34), channel_id=1, replica_groups={{0,8,16,24,32,40,48,56,64,72,80,88,96,104,112,120,128,136,144,152,160,1..., dimensions={0} | all-to-all | bytes 524288 | tf_op jit(solution)/shard_map/all_to_all | solution.py:342
  50.6 2.3 %collective-permute-start.7 = (bf16[256,512]{1,0:T(8,128)(2,1)S(1)}, bf16[256,512]{1,0:T(8,128)(2,1)S(1)}, u32[]{:S(2)}, u32[]{:S(2)}) collective-permute-start(bf16[256,512]{1,0:T(8,128)(2,1)S(1)} %bitcast.17), channel_id=1, source_target_pairs={{0,4},{4,0},{8,12},{12,8},{16,20},{20,16},{24,28},{28,24},{32,36},... | collective-permute-start | bytes 786440 | tf_op jit(solution)/shard_map/ppermute | solution.py:344
  52.9 1.2 %collective-permute-done.7.other = bf16[256,512]{1,0:T(8,128)(2,1)S(1)} collective-permute-done((bf16[256,512]{1,0:T(8,128)(2,1)S(1)}, bf16[256,512]{1,0:T(8,128)(2,1)S(1)}, u32[]{:S(2)}, u32[]{:S(2)}) %collective-permute-start.7) | collective-permute-done | bytes 262176 | tf_op jit(solution)/shard_map/ppermute | solution.py:344
  54.1 2.3 %shard_map.88 = (f32[1,128]{1,0:T(1,128)}, bf16[32,512]{1,0:T(8,128)(2,1)S(1)}, bf16[32,128]{1,0:T(8,128)(2,1)S(1)}, f32[8,1792]{1,0:T(8,128)S(1)}) custom-call(s32[4]{0:T(128)S(1)} %pad_add_fusion.place, f32[32,512]{1,0:T(8,128)S(1)} %get-tuple-element.30.attn, bf16[512,512]{1,0:T(8,128)(2,1)S(1)} %get-tuple-element.31.keyval, ...), custom_call_target="tpu_custom_call" | custom-call | flops 6000000000 | tf_op jit(solution)/shard_map/pallas_call | solution.py:98
  56.4 1.3 %shard_map.90 = (bf16[16,3584]{1,0:T(8,128)(2,1)S(1)}, bf16[16,3584]{1,0:T(8,128)(2,1)S(1)}, bf16[16,3584]{1,0:T(8,128)(2,1)S(1)}, bf16[16,3584]{1,0:T(8,128)(2,1)S(1)}) custom-call(s32[4]{0:T(128)S(1)} %pad_add_fusion.place, bf16[512,3584]{1,0:T(8,128)(2,1)S(1)} %bitcast.16, bf16[32,512]{1,0:T(8,128)(2,1)S(1)} %get-tuple-element.36.grad_score, ...), custom_call_target="tpu_custom_call" | custom-call | flops 234881024 | tf_op jit(solution)/shard_map/pallas_call | solution.py:98
  57.7 0.2 collective-permute-start.8
  57.9 1.8 %collective-permute-start.9 = (bf16[16,3584]{1,0:T(8,128)(2,1)S(1)}, bf16[16,3584]{1,0:T(8,128)(2,1)S(1)}, u32[]{:S(2)}, u32[]{:S(2)}) collective-permute-start(bf16[16,3584]{1,0:T(8,128)(2,1)S(1)} %get-tuple-element.46), channel_id=1, source_target_pairs={{0,160},{4,164},{8,168},{12,172},{16,176},{20,180},{24,184},{28,18... | collective-permute-start | bytes 344072 | tf_op jit(solution)/shard_map/ppermute | solution.py:368
  59.7 2.8 %collective-permute-start.10 = (bf16[16,3584]{1,0:T(8,128)(2,1)S(1)}, bf16[16,3584]{1,0:T(8,128)(2,1)S(1)}, u32[]{:S(2)}, u32[]{:S(2)}) collective-permute-start(bf16[16,3584]{1,0:T(8,128)(2,1)S(1)} %get-tuple-element.48), channel_id=1, source_target_pairs={{0,64},{4,68},{8,72},{12,76},{16,80},{20,84},{24,88},{28,92},{32,2... | collective-permute-start | bytes 344072 | tf_op jit(solution)/shard_map/ppermute | solution.py:368
  62.5 1.2 %collective-permute-start.11 = (bf16[16,3584]{1,0:T(8,128)(2,1)S(1)}, bf16[16,3584]{1,0:T(8,128)(2,1)S(1)}, u32[]{:S(2)}, u32[]{:S(2)}) collective-permute-start(bf16[16,3584]{1,0:T(8,128)(2,1)S(1)} %get-tuple-element.42.a0), channel_id=1, source_target_pairs={{0,4},{4,0},{8,12},{12,8},{16,20},{20,16},{24,28},{28,24},{32,36},... | collective-permute-start | bytes 344072 | tf_op jit(solution)/shard_map/ppermute | solution.py:373
  63.8 4.9 %shard_map.89 = (bf16[512,3584]{1,0:T(8,128)(2,1)}, bf16[2,1792]{1,0:T(2,128)(2,1)}, f32[8,128]{1,0:T(8,128)}) custom-call(s32[4]{0:T(128)S(1)} %pad_add_fusion.place, bf16[32,512]{1,0:T(8,128)(2,1)S(1)} %get-tuple-element.36.grad_score, f32[32,512]{1,0:T(8,128)S(1)} %get-tuple-element.30.attn, bf16[32,128]{1,0:T(8,128)(2,1)S(1)} %get-tuple-element.37.query_rows, ...), custom_call_target="tpu_custom_call" | custom-call | flops 1879048192 | tf_op jit(solution)/shard_map/pallas_call | solution.py:98
  68.7 0.0 collective-permute-done.8.a1
  68.7 0.0 collective-permute-start.12
  68.7 0.9 collective-permute-done.9.a2
  69.5 1.3 %collective-permute-start.13 = (bf16[16,3584]{1,0:T(8,128)(2,1)S(1)}, bf16[16,3584]{1,0:T(8,128)(2,1)S(1)}, u32[]{:S(2)}, u32[]{:S(2)}) collective-permute-start(bf16[16,3584]{1,0:T(8,128)(2,1)S(1)} %collective-permute-done.9.a2), channel_id=1, source_target_pairs={{0,4},{4,0},{8,12},{12,8},{16,20},{20,16},{24,28},{28,24},{32,36},... | collective-permute-start | bytes 344072 | tf_op jit(solution)/shard_map/ppermute | solution.py:373
  70.9 0.0 collective-permute-done.10.a3
  70.9 0.0 collective-permute-start.14
  70.9 0.0 collective-permute-done.12.b1
  70.9 0.9 %collective-permute-done.13.b2 = bf16[16,3584]{1,0:T(8,128)(2,1)S(1)} collective-permute-done((bf16[16,3584]{1,0:T(8,128)(2,1)S(1)}, bf16[16,3584]{1,0:T(8,128)(2,1)S(1)}, u32[]{:S(2)}, u32[]{:S(2)}) %collective-permute-start.13) | collective-permute-done | bytes 114720 | tf_op jit(solution)/shard_map/ppermute | solution.py:373
  71.8 0.4 collective-permute-done.14.b3
  72.2 1.1 %shard_map.91 = bf16[64,3584]{1,0:T(8,128)(2,1)S(1)} custom-call(s32[4]{0:T(128)S(1)} %pad_add_fusion.place, bf16[16,3584]{1,0:T(8,128)(2,1)S(1)} %get-tuple-element.42.a0, bf16[16,3584]{1,0:T(8,128)(2,1)S(1)} %collective-permute-done.8.a1, bf16[16,3584]{1,0:T(8,128)(2,1)S(1)} %collective-permute-done.9.a2, bf16[16,3584]{1,0:T(8,128)(2,1)S(1)} %collective-permute-done.10.a3, ...), custom_call_target="tpu_custom_call" | custom-call | tf_op jit(solution)/shard_map/pallas_call | solution.py:98
  73.3 0.2 reshape.23
  73.5 16.2 %all_to_all.11 = bf16[32,2,3584]{2,1,0:T(2,128)(2,1)S(1)} all-to-all(bf16[32,2,3584]{2,1,0:T(2,128)(2,1)S(1)} %reshape.23), channel_id=1, replica_groups={{0,1,2,3,8,9,10,11,16,17,18,19,24,25,26,27,32,33,34,35,40,41,42,43,48,4..., dimensions={0} | all-to-all | bytes 917504 | tf_op jit(solution)/shard_map/all_to_all | solution.py:377
  89.7 1.0 %convert_reduce_fusion = f32[2,3584]{1,0:T(2,128)} fusion(bf16[32,2,3584]{2,1,0:T(2,128)(2,1)S(1)} %all_to_all.11), kind=kLoop, calls=%fused_computation | loop fusion | flops 451584 | bytes 487424 | tf_op jit(solution)/shard_map/reduce_sum | solution.py:378
  (10 shorter events, 0.0 us)
Async XLA Ops:
  1.6 8.3 %collective-permute-start = (bf16[448,128]{1,0:T(8,128)(2,1)S(1)}, bf16[448,128]{1,0:T(8,128)(2,1)S(1)}, u32[]{:S(2)}, u32[]{:S(2)}) collective-permute-start(bf16[448,128]{1,0:T(8,128)(2,1)S(1)} %dynamic_slice.3), channel_id=1, source_target_pairs={{0,2},{1,3},{2,0},{3,1},{4,6},{5,7},{6,4},{7,5},{8,10},{9,11},{10,... | collective-permute-start | bytes 344072 | tf_op jit(solution)/shard_map/ppermute | solution.py:400
  5.4 2.0 %copy-start = (bf16[1,2,256,3584]{3,2,1,0:T(8,128)(2,1)S(1)}, bf16[1,2,256,3584]{3,2,1,0:T(8,128)(2,1)}, u32[]{:S(2)}) copy-start(bf16[1,2,256,3584]{3,2,1,0:T(8,128)(2,1)} %param.5) | copy-start | bytes 11010052
  7.5 1.2 %copy-start.2 = (bf16[896,512]{1,0:T(8,128)(2,1)S(1)}, bf16[896,512]{1,0:T(8,128)(2,1)}, u32[]{:S(2)}) copy-start(bf16[896,512]{1,0:T(8,128)(2,1)} %own.1) | copy-start | bytes 2752516
  8.7 16.7 %copy-start.1 = (bf16[1,2,256,3584]{3,2,1,0:T(8,128)(2,1)S(1)}, bf16[1,2,256,3584]{3,2,1,0:T(8,128)(2,1)}, u32[]{:S(2)}) copy-start(bf16[1,2,256,3584]{3,2,1,0:T(8,128)(2,1)} %param.5) | copy-start | bytes 11010052
  9.9 15.1 %collective-permute-start.1 = (bf16[896,512]{1,0:T(8,128)(2,1)S(1)}, bf16[896,512]{1,0:T(8,128)(2,1)S(1)}, u32[]{:S(2)}, u32[]{:S(2)}) collective-permute-start(bf16[896,512]{1,0:T(8,128)(2,1)S(1)} %copy-done.2), channel_id=1, source_target_pairs={{0,3},{1,0},{2,1},{3,2},{4,5},{5,6},{6,7},{7,4},{8,11},{9,8},{10,9... | collective-permute-start | bytes 2752520 | tf_op jit(solution)/shard_map/ppermute | solution.py:401
  10.4 4.8 %collective-permute-start.4 = (bf16[448,128]{1,0:T(8,128)(2,1)S(1)}, bf16[448,128]{1,0:T(8,128)(2,1)S(1)}, u32[]{:S(2)}, u32[]{:S(2)}) collective-permute-start(bf16[448,128]{1,0:T(8,128)(2,1)S(1)} %collective-permute-done.a0), channel_id=1, source_target_pairs={{0,24},{4,28},{8,0},{12,4},{16,8},{20,12},{24,16},{28,20},{32,56},... | collective-permute-start | bytes 344072 | tf_op jit(solution)/shard_map/ppermute | solution.py:402
  12.9 5.3 %collective-permute-start.3 = (bf16[448,128]{1,0:T(8,128)(2,1)S(1)}, bf16[448,128]{1,0:T(8,128)(2,1)S(1)}, u32[]{:S(2)}, u32[]{:S(2)}) collective-permute-start(bf16[448,128]{1,0:T(8,128)(2,1)S(1)} %collective-permute-done.a0), channel_id=1, source_target_pairs={{0,16},{4,20},{8,24},{12,28},{16,0},{20,4},{24,8},{28,12},{32,48},... | collective-permute-start | bytes 344072 | tf_op jit(solution)/shard_map/ppermute | solution.py:402
  13.4 5.9 %collective-permute-start.2 = (bf16[448,128]{1,0:T(8,128)(2,1)S(1)}, bf16[448,128]{1,0:T(8,128)(2,1)S(1)}, u32[]{:S(2)}, u32[]{:S(2)}) collective-permute-start(bf16[448,128]{1,0:T(8,128)(2,1)S(1)} %collective-permute-done.a0), channel_id=1, source_target_pairs={{0,8},{4,12},{8,16},{12,20},{16,24},{20,28},{24,0},{28,4},{32,40},... | collective-permute-start | bytes 344072 | tf_op jit(solution)/shard_map/ppermute | solution.py:402
  19.9 7.6 %copy-start.4 = (bf16[1,2,1792]{2,1,0:T(2,128)(2,1)S(1)}, bf16[1,2,1792]{2,1,0:T(2,128)(2,1)}, u32[]{:S(2)}) copy-start(bf16[1,2,1792]{2,1,0:T(2,128)(2,1)} %param.7) | copy-start | bytes 21508
  19.9 7.6 %copy-start.5 = (s32[1,2]{1,0:T(1,128)S(1)}, s32[1,2]{1,0:T(1,128)}, u32[]{:S(2)}) copy-start(s32[1,2]{1,0:T(1,128)} %param.6) | copy-start | bytes 28
  19.9 7.6 %copy-start.6 = (s32[1,2]{1,0:T(1,128)S(1)}, s32[1,2]{1,0:T(1,128)}, u32[]{:S(2)}) copy-start(s32[1,2]{1,0:T(1,128)} %param.8) | copy-start | bytes 28
  19.9 5.1 %collective-permute-start.5 = (bf16[896,256]{1,0:T(8,128)(2,1)S(1)}, bf16[896,256]{1,0:T(8,128)(2,1)S(1)}, u32[]{:S(2)}, u32[]{:S(2)}) collective-permute-start(bf16[896,256]{1,0:T(8,128)(2,1)S(1)} %shard_map.85.half), channel_id=1, source_target_pairs={{0,4},{4,0},{8,12},{12,8},{16,20},{20,16},{24,28},{28,24},{32,36},... | collective-permute-start | bytes 1376264 | tf_op jit(solution)/shard_map/ppermute | solution.py:391
  25.0 2.5 %collective-permute-start.6 = (bf16[896,512]{1,0:T(8,128)(2,1)S(1)}, bf16[896,512]{1,0:T(8,128)(2,1)S(1)}, u32[]{:S(2)}, u32[]{:S(2)}) collective-permute-start(bf16[896,512]{1,0:T(8,128)(2,1)S(1)} %collective-permute-done.1.weight.near), channel_id=1, source_target_pairs={{0,4},{4,0},{8,12},{12,8},{16,20},{20,16},{24,28},{28,24},{32,36},... | collective-permute-start | bytes 2752520 | tf_op jit(solution)/shard_map/ppermute | solution.py:391
  50.6 3.5 %collective-permute-start.7 = (bf16[256,512]{1,0:T(8,128)(2,1)S(1)}, bf16[256,512]{1,0:T(8,128)(2,1)S(1)}, u32[]{:S(2)}, u32[]{:S(2)}) collective-permute-start(bf16[256,512]{1,0:T(8,128)(2,1)S(1)} %bitcast.17), channel_id=1, source_target_pairs={{0,4},{4,0},{8,12},{12,8},{16,20},{20,16},{24,28},{28,24},{32,36},... | collective-permute-start | bytes 786440 | tf_op jit(solution)/shard_map/ppermute | solution.py:344
  56.4 7.4 %copy-start.3 = (bf16[896,512]{1,0:T(8,128)(2,1)S(1)}, bf16[896,512]{1,0:T(8,128)(2,1)}, u32[]{:S(2)}) copy-start(bf16[896,512]{1,0:T(8,128)(2,1)} %own.1) | copy-start | bytes 2752516
  57.7 11.0 %collective-permute-start.8 = (bf16[16,3584]{1,0:T(8,128)(2,1)S(1)}, bf16[16,3584]{1,0:T(8,128)(2,1)S(1)}, u32[]{:S(2)}, u32[]{:S(2)}) collective-permute-start(bf16[16,3584]{1,0:T(8,128)(2,1)S(1)} %get-tuple-element.43), channel_id=1, source_target_pairs={{0,224},{4,228},{8,232},{12,236},{16,240},{20,244},{24,248},{28,25... | collective-permute-start | bytes 344072 | tf_op jit(solution)/shard_map/ppermute | solution.py:368
  57.9 11.6 %collective-permute-start.9 = (bf16[16,3584]{1,0:T(8,128)(2,1)S(1)}, bf16[16,3584]{1,0:T(8,128)(2,1)S(1)}, u32[]{:S(2)}, u32[]{:S(2)}) collective-permute-start(bf16[16,3584]{1,0:T(8,128)(2,1)S(1)} %get-tuple-element.46), channel_id=1, source_target_pairs={{0,160},{4,164},{8,168},{12,172},{16,176},{20,180},{24,184},{28,18... | collective-permute-start | bytes 344072 | tf_op jit(solution)/shard_map/ppermute | solution.py:368
  59.7 11.1 %collective-permute-start.10 = (bf16[16,3584]{1,0:T(8,128)(2,1)S(1)}, bf16[16,3584]{1,0:T(8,128)(2,1)S(1)}, u32[]{:S(2)}, u32[]{:S(2)}) collective-permute-start(bf16[16,3584]{1,0:T(8,128)(2,1)S(1)} %get-tuple-element.48), channel_id=1, source_target_pairs={{0,64},{4,68},{8,72},{12,76},{16,80},{20,84},{24,88},{28,92},{32,2... | collective-permute-start | bytes 344072 | tf_op jit(solution)/shard_map/ppermute | solution.py:368
  62.5 8.3 %collective-permute-start.11 = (bf16[16,3584]{1,0:T(8,128)(2,1)S(1)}, bf16[16,3584]{1,0:T(8,128)(2,1)S(1)}, u32[]{:S(2)}, u32[]{:S(2)}) collective-permute-start(bf16[16,3584]{1,0:T(8,128)(2,1)S(1)} %get-tuple-element.42.a0), channel_id=1, source_target_pairs={{0,4},{4,0},{8,12},{12,8},{16,20},{20,16},{24,28},{28,24},{32,36},... | collective-permute-start | bytes 344072 | tf_op jit(solution)/shard_map/ppermute | solution.py:373
  68.7 2.2 %collective-permute-start.12 = (bf16[16,3584]{1,0:T(8,128)(2,1)S(1)}, bf16[16,3584]{1,0:T(8,128)(2,1)S(1)}, u32[]{:S(2)}, u32[]{:S(2)}) collective-permute-start(bf16[16,3584]{1,0:T(8,128)(2,1)S(1)} %collective-permute-done.8.a1), channel_id=1, source_target_pairs={{0,4},{4,0},{8,12},{12,8},{16,20},{20,16},{24,28},{28,24},{32,36},... | collective-permute-start | bytes 344072 | tf_op jit(solution)/shard_map/ppermute | solution.py:373
  69.5 2.3 %collective-permute-start.13 = (bf16[16,3584]{1,0:T(8,128)(2,1)S(1)}, bf16[16,3584]{1,0:T(8,128)(2,1)S(1)}, u32[]{:S(2)}, u32[]{:S(2)}) collective-permute-start(bf16[16,3584]{1,0:T(8,128)(2,1)S(1)} %collective-permute-done.9.a2), channel_id=1, source_target_pairs={{0,4},{4,0},{8,12},{12,8},{16,20},{20,16},{24,28},{28,24},{32,36},... | collective-permute-start | bytes 344072 | tf_op jit(solution)/shard_map/ppermute | solution.py:373
  70.9 1.3 %collective-permute-start.14 = (bf16[16,3584]{1,0:T(8,128)(2,1)S(1)}, bf16[16,3584]{1,0:T(8,128)(2,1)S(1)}, u32[]{:S(2)}, u32[]{:S(2)}) collective-permute-start(bf16[16,3584]{1,0:T(8,128)(2,1)S(1)} %collective-permute-done.10.a3), channel_id=1, source_target_pairs={{0,4},{4,0},{8,12},{12,8},{16,20},{20,16},{24,28},{28,24},{32,36},... | collective-permute-start | bytes 344072 | tf_op jit(solution)/shard_map/ppermute | solution.py:373

commit v5 on v4

--- a/solution.py
+++ b/solution.py
@@ -127,19 +127,13 @@
     return block_at(place, jnp.where(place[1] == 0, NY - 1, 1), shard)
 
 
-def half_body(place, a0, a1, a2, a3, out):
-    rows = a0.shape[0]
-    for k, piece in enumerate((a0, a1, a2, a3)):
+def place_pieces(place, core, pieces, out):
+    rows = pieces[0].shape[0]
+    for k, piece in enumerate(pieces):
         source = lax.rem(place[3] + NX - k, NX)
         at = pl.multiple_of((source // KVH) * rows, rows)
-        lane = pl.multiple_of(lax.rem(source, KVH) * HD, HD)
+        lane = pl.multiple_of((core * KVH + lax.rem(source, KVH)) * HD, HD)
         out[pl.ds(at, rows), pl.ds(lane, HD)] = piece[...]
-
-
-def across_block(place, half, half_other):
-    first = place[1] == 0
-    a, b = half[...], half_other[...]
-    return jnp.concatenate([jnp.where(first, a, b), jnp.where(first, b, a)], axis=1)
 
 
 def own_body(place, tokens, weight, out):
@@ -147,11 +141,14 @@
     out[...] = dot_nn(tokens[:, pl.ds(block_at(place, 0, shard), shard)], weight[...])
 
 
-def near_body(place, tokens, weight, half, half_other, before, out):
+def near_body(
+    place, tokens, weight, a0, a1, a2, a3, b0, b1, b2, b3, before, out, across
+):
     shard = weight.shape[0]
-    across = across_block(place, half, half_other)
+    place_pieces(place, place[1], (a0, a1, a2, a3), across)
+    place_pieces(place, 1 - place[1], (b0, b1, b2, b3), across)
     part = dot_nn(tokens[:, pl.ds(near_at(place, shard), shard)], weight[...])
-    part += dot_nn(tokens[:, pl.ds(block_at(place, 2, shard), shard)], across)
+    part += dot_nn(tokens[:, pl.ds(block_at(place, 2, shard), shard)], across[...])
     out[...] = before[...] + part
 
 
@@ -314,7 +311,7 @@
 
 
 def token_body(
-    place, grad_score, attn, query_rows, grad_rows, keyval, own, near, near_other, half, half_other,
+    place, grad_score, attn, query_rows, grad_rows, keyval, own, near, near_other, across,
     out, grad_query, done, lanes,
 ):
     shard = own.shape[0]
@@ -327,7 +324,7 @@
         (block_at(place, 0, shard), own[...]),
         (near_at(place, shard), near[...]),
         (near_other_at(place, shard), near_other[...]),
-        (block_at(place, 2, shard), across_block(place, half, half_other)),
+        (block_at(place, 2, shard), across[...]),
     ]
     for at, block in blocks:
         out[:, pl.ds(at, shard)] = dot_nt(grad_keyval, block).astype(BF16)
@@ -400,13 +397,12 @@
     mine = tie(lax.ppermute(piece, "fsdp", Y_ACROSS), part)
     near = lax.ppermute(tie(kv_weight, mine), ("dp", "fsdp"), y_mirror())
     pieces = [mine] + [lax.ppermute(mine, "dp", x_shift(k)) for k in (1, 2, 3)]
-    (half,) = call(half_body, (place,), pieces, [((shard, KVH * HD), BF16)])
-    half_other = swap(half)
-
-    near = tie(near, half_other)
+    swapped = [swap(a) for a in pieces]
+    near = tie(near, *swapped)
     near_other = swap(near)
-    (part,) = call(
-        near_body, (place,), (rows, near, half, half_other, part), [((count, KVW), F32)],
+    part, across = call(
+        near_body, (place,), (rows, near, *pieces, *swapped, part),
+        [((count, KVW), F32), ((shard, KVW), BF16)],
         flops=2 * flops, limit=8,
     )
     keyval, attn, spread, unit, norm, query_rows = call(
@@ -452,7 +448,7 @@
     grad_tok, grad_query, done = call(
         token_body,
         (place,),
-        (grad_score, attn, query_rows, grad_rows, keyval, kv_weight, near, near_other, half, half_other),
+        (grad_score, attn, query_rows, grad_rows, keyval, kv_weight, near, near_other, across),
         [((count, width), BF16), ((docs, QW), BF16), ((SLOT, HD), F32)],
         [pltpu.VMEM((SLOT, QW), F32)],
         flops=4 * flops,

time: 91 us -> 91 us (level)
  waiting for transfers between devices: 10.3 us -> 4.43 us
  starting transfers between devices: 21.5 us -> 27 us
    ppermute x2 -> x5, starting transfers between devices: 4.02 us -> 9.52 us  [local(): swap = lambda a: lax.ppermute(a, 'dp', OTHER_CORE)]
    ppermute x3, waiting for transfers between devices: 5.25 us -> 0.01 us  [local(): pieces = [mine] + [lax.ppermute(mine, 'dp', x_shift(k)) for k in (1, 2, 3)]]
    pallas_call x8 -> x7, Pallas kernels: 15.1 us -> 14.6 us  [call(): pl.pallas_call(body, out_shape=[jax.ShapeDtypeStruct(s, d) for s, d in ou...]
  transfers between devices with their start and end apart: 15 -> 18, of which waited for: 9 -> 6; matrix products, arithmetic and copies ran while one was open for 0% -> 0% of each run, Pallas kernels for 9% -> 9%
where the time goes in v5:
time: 91 us; the launch traced here: 90.7 us
  blocking collectives  38.4 us (42%)
  starting transfers between devices  27 us (30%)
  Pallas kernels  14.6 us (16%)
  waiting for transfers between devices  4.43 us (5%)
  local copies, waits for them, and re-layouts  4.33 us (5%)
  other arithmetic  1.06 us (1%)
    all_to_all x1, blocking collectives, gather_docs(): got = lax.all_to_all(spread, 'dp', 0, 0, axis_index_groups=CHIPS)  22.2 us
    all_to_all x1, blocking collectives, reduce_weight(): got = lax.all_to_all(pieces, ('dp', 'fsdp'), 0, 0, axis_index_groups=OWNERS)  16.2 us
    pallas_call x7, Pallas kernels, call(): pl.pallas_call(body, out_shape=[jax.ShapeDtypeStruct(s, d) for s, d in ou...  14.6 us
    ppermute x5, starting transfers between devices, local(): swap = lambda a: lax.ppermute(a, 'dp', OTHER_CORE)  9.52 us
    ppermute x3, starting transfers between devices, exchange_types(): lax.ppermute(a, 'dp', parity_shift(k))  4.85 us
    ppermute x1, starting transfers between devices, local(): mine = tie(lax.ppermute(piece, 'fsdp', Y_ACROSS), part)  3.74 us
    ppermute x3, starting transfers between devices, local(): pieces = [mine] + [lax.ppermute(mine, 'dp', x_shift(k)) for k in (1, 2, 3)]  3.6 us
    unnamed x14, local copies, waits for them, and re-layouts  3.25 us
  transfers between devices with their start and end apart: 18, of which 6 were waited for; matrix products, arithmetic and copies ran while one was open for 0% of the time, Pallas kernels for 9%

profile of v5, /device:TPU:1, one launch (start us, length us, event | category | flops | bytes accessed | tf_op | source)
XLA Modules:
  0.0 90.7 jit_solution(15901024329963465886)
XLA Ops:
  0.7 0.9 %dynamic_slice.3 = bf16[448,128]{1,0:T(8,128)(2,1)S(1)} dynamic-slice(bf16[896,512]{1,0:T(8,128)(2,1)} %own.1, s32[]{:T(128)S(6)} %select_n.32, s32[]{:T(128)S(6)} %select_n.34), dynamic_slice_sizes={448,128} | dynamic-slice | bytes 229380 | tf_op jit(solution)/shard_map/dynamic_slice | solution.py:394
  1.6 3.7 %collective-permute-start = (bf16[448,128]{1,0:T(8,128)(2,1)S(1)}, bf16[448,128]{1,0:T(8,128)(2,1)S(1)}, u32[]{:S(2)}, u32[]{:S(2)}) collective-permute-start(bf16[448,128]{1,0:T(8,128)(2,1)S(1)} %dynamic_slice.3), channel_id=1, source_target_pairs={{0,2},{1,3},{2,0},{3,1},{4,6},{5,7},{6,4},{7,5},{8,10},{9,11},{10,... | collective-permute-start | bytes 344072 | tf_op jit(solution)/shard_map/ppermute | solution.py:397
  5.4 0.1 pad_add_fusion.place
  5.4 2.0 %copy-done = bf16[1,2,256,3584]{3,2,1,0:T(8,128)(2,1)S(1)} copy-done((bf16[1,2,256,3584]{3,2,1,0:T(8,128)(2,1)S(1)}, bf16[1,2,256,3584]{3,2,1,0:T(8,128)(2,1)}, u32[]{:S(2)}) %copy-start) | copy-done | bytes 3670040
  7.5 1.2 %copy-done.2 = bf16[896,512]{1,0:T(8,128)(2,1)S(1)} copy-done((bf16[896,512]{1,0:T(8,128)(2,1)S(1)}, bf16[896,512]{1,0:T(8,128)(2,1)}, u32[]{:S(2)}) %copy-start.2) | copy-done | bytes 917528
  8.7 1.2 %shard_map.84.before = f32[512,512]{1,0:T(8,128)S(1)} custom-call(s32[4]{0:T(128)S(1)} %pad_add_fusion.place, bf16[512,3584]{1,0:T(8,128)(2,1)S(1)} %bitcast.13, bf16[896,512]{1,0:T(8,128)(2,1)S(1)} %copy-done.2), custom_call_target="tpu_custom_call" | custom-call | flops 469762048 | tf_op jit(solution)/shard_map/pallas_call | solution.py:98
  9.9 0.0 copy-start.1
  9.9 0.0 copy-start.4
  9.9 0.0 copy-start.5
  9.9 0.0 copy-start.6
  10.0 0.0 collective-permute-done.a0
  10.0 0.5 collective-permute-start.1
  10.4 2.5 %collective-permute-start.7 = (bf16[448,128]{1,0:T(8,128)(2,1)S(1)}, bf16[448,128]{1,0:T(8,128)(2,1)S(1)}, u32[]{:S(2)}, u32[]{:S(2)}) collective-permute-start(bf16[448,128]{1,0:T(8,128)(2,1)S(1)} %collective-permute-done.a0), channel_id=1, source_target_pairs={{0,24},{4,28},{8,0},{12,4},{16,8},{20,12},{24,16},{28,20},{32,56},... | collective-permute-start | bytes 344072 | tf_op jit(solution)/shard_map/ppermute | solution.py:399
  12.9 0.5 collective-permute-start.5
  13.4 0.6 collective-permute-start.3
  14.0 2.9 %collective-permute-start.2 = (bf16[448,128]{1,0:T(8,128)(2,1)S(1)}, bf16[448,128]{1,0:T(8,128)(2,1)S(1)}, u32[]{:S(2)}, u32[]{:S(2)}) collective-permute-start(bf16[448,128]{1,0:T(8,128)(2,1)S(1)} %collective-permute-done.a0), channel_id=1, source_target_pairs={{0,4},{4,0},{8,12},{12,8},{16,20},{20,16},{24,28},{28,24},{32,36},... | collective-permute-start | bytes 344072 | tf_op jit(solution)/shard_map/ppermute | solution.py:388
  17.0 0.0 collective-permute-done.7.a3
  17.0 2.1 %collective-permute-start.8 = (bf16[448,128]{1,0:T(8,128)(2,1)S(1)}, bf16[448,128]{1,0:T(8,128)(2,1)S(1)}, u32[]{:S(2)}, u32[]{:S(2)}) collective-permute-start(bf16[448,128]{1,0:T(8,128)(2,1)S(1)} %collective-permute-done.7.a3), channel_id=1, source_target_pairs={{0,4},{4,0},{8,12},{12,8},{16,20},{20,16},{24,28},{28,24},{32,36},... | collective-permute-start | bytes 344072 | tf_op jit(solution)/shard_map/ppermute | solution.py:388
  19.1 0.0 collective-permute-done.5.a2
  19.1 2.6 %collective-permute-start.6 = (bf16[448,128]{1,0:T(8,128)(2,1)S(1)}, bf16[448,128]{1,0:T(8,128)(2,1)S(1)}, u32[]{:S(2)}, u32[]{:S(2)}) collective-permute-start(bf16[448,128]{1,0:T(8,128)(2,1)S(1)} %collective-permute-done.5.a2), channel_id=1, source_target_pairs={{0,4},{4,0},{8,12},{12,8},{16,20},{20,16},{24,28},{28,24},{32,36},... | collective-permute-start | bytes 344072 | tf_op jit(solution)/shard_map/ppermute | solution.py:388
  21.7 0.0 collective-permute-done.3.a1
  21.7 1.1 %collective-permute-start.4 = (bf16[448,128]{1,0:T(8,128)(2,1)S(1)}, bf16[448,128]{1,0:T(8,128)(2,1)S(1)}, u32[]{:S(2)}, u32[]{:S(2)}) collective-permute-start(bf16[448,128]{1,0:T(8,128)(2,1)S(1)} %collective-permute-done.3.a1), channel_id=1, source_target_pairs={{0,4},{4,0},{8,12},{12,8},{16,20},{20,16},{24,28},{28,24},{32,36},... | collective-permute-start | bytes 344072 | tf_op jit(solution)/shard_map/ppermute | solution.py:388
  22.8 0.0 collective-permute-done.2.b0
  22.8 1.0 %collective-permute-done.4.b1 = bf16[448,128]{1,0:T(8,128)(2,1)S(1)} collective-permute-done((bf16[448,128]{1,0:T(8,128)(2,1)S(1)}, bf16[448,128]{1,0:T(8,128)(2,1)S(1)}, u32[]{:S(2)}, u32[]{:S(2)}) %collective-permute-start.4) | collective-permute-done | bytes 114720 | tf_op jit(solution)/shard_map/ppermute | solution.py:388
  23.8 0.8 collective-permute-start.9
  24.6 2.0 %shard_map.85 = (f32[512,512]{1,0:T(8,128)S(1)}, bf16[896,512]{1,0:T(8,128)(2,1)S(1)}) custom-call(s32[4]{0:T(128)S(1)} %pad_add_fusion.place, bf16[512,3584]{1,0:T(8,128)(2,1)S(1)} %bitcast.14, bf16[896,512]{1,0:T(8,128)(2,1)S(1)} %collective-permute-done.1.weight.near, bf16[448,128]{1,0:T(8,128)(2,1)S(1)} %collective-permute-done.a0, ...), custom_call_target="tpu_custom_call" | custom-call | flops 939524096 | tf_op jit(solution)/shard_map/pallas_call | solution.py:98
  26.5 0.1 collective-permute-done.9.near_other
  26.7 1.8 %shard_map.86 = (bf16[512,512]{1,0:T(8,128)(2,1)S(1)}, f32[32,512]{1,0:T(8,128)S(1)}, bf16[32,8,512]{2,1,0:T(8,128)(2,1)S(1)}, f32[8,1792]{1,0:T(8,128)S(1)}, f3...) custom-call(s32[4]{0:T(128)S(1)} %pad_add_fusion.place, s32[2]{0:T(128)S(1)} %bitcast.21, s32[2]{0:T(128)S(1)} %bitcast.22, ...), custom_call_target="tpu_custom_call" | custom-call | flops 939524096 | tf_op jit(solution)/shard_map/pallas_call | solution.py:98
  28.4 22.2 %all_to_all.10 = bf16[32,8,512]{2,1,0:T(8,128)(2,1)S(1)} all-to-all(bf16[32,8,512]{2,1,0:T(8,128)(2,1)S(1)} %get-tuple-element.37), channel_id=1, replica_groups={{0,8,16,24,32,40,48,56,64,72,80,88,96,104,112,120,128,136,144,152,160,1..., dimensions={0} | all-to-all | bytes 524288 | tf_op jit(solution)/shard_map/all_to_all | solution.py:339
  50.7 2.3 %collective-permute-start.10 = (bf16[256,512]{1,0:T(8,128)(2,1)S(1)}, bf16[256,512]{1,0:T(8,128)(2,1)S(1)}, u32[]{:S(2)}, u32[]{:S(2)}) collective-permute-start(bf16[256,512]{1,0:T(8,128)(2,1)S(1)} %bitcast.17), channel_id=1, source_target_pairs={{0,4},{4,0},{8,12},{12,8},{16,20},{20,16},{24,28},{28,24},{32,36},... | collective-permute-start | bytes 786440 | tf_op jit(solution)/shard_map/ppermute | solution.py:341
  53.0 1.2 %collective-permute-done.10.other = bf16[256,512]{1,0:T(8,128)(2,1)S(1)} collective-permute-done((bf16[256,512]{1,0:T(8,128)(2,1)S(1)}, bf16[256,512]{1,0:T(8,128)(2,1)S(1)}, u32[]{:S(2)}, u32[]{:S(2)}) %collective-permute-start.10) | collective-permute-done | bytes 262176 | tf_op jit(solution)/shard_map/ppermute | solution.py:341
  54.1 2.3 %shard_map.87 = (f32[1,128]{1,0:T(1,128)}, bf16[32,512]{1,0:T(8,128)(2,1)S(1)}, bf16[32,128]{1,0:T(8,128)(2,1)S(1)}, f32[8,1792]{1,0:T(8,128)S(1)}) custom-call(s32[4]{0:T(128)S(1)} %pad_add_fusion.place, f32[32,512]{1,0:T(8,128)S(1)} %get-tuple-element.33.attn, bf16[512,512]{1,0:T(8,128)(2,1)S(1)} %get-tuple-element.34.keyval, ...), custom_call_target="tpu_custom_call" | custom-call | flops 6000000000 | tf_op jit(solution)/shard_map/pallas_call | solution.py:98
  56.4 1.3 %shard_map.89 = (bf16[16,3584]{1,0:T(8,128)(2,1)S(1)}, bf16[16,3584]{1,0:T(8,128)(2,1)S(1)}, bf16[16,3584]{1,0:T(8,128)(2,1)S(1)}, bf16[16,3584]{1,0:T(8,128)(2,1)S(1)}) custom-call(s32[4]{0:T(128)S(1)} %pad_add_fusion.place, bf16[512,3584]{1,0:T(8,128)(2,1)S(1)} %bitcast.16, bf16[32,512]{1,0:T(8,128)(2,1)S(1)} %get-tuple-element.39.grad_score, ...), custom_call_target="tpu_custom_call" | custom-call | flops 234881024 | tf_op jit(solution)/shard_map/pallas_call | solution.py:98
  57.7 0.2 collective-permute-start.11
  58.0 1.8 %collective-permute-start.12 = (bf16[16,3584]{1,0:T(8,128)(2,1)S(1)}, bf16[16,3584]{1,0:T(8,128)(2,1)S(1)}, u32[]{:S(2)}, u32[]{:S(2)}) collective-permute-start(bf16[16,3584]{1,0:T(8,128)(2,1)S(1)} %get-tuple-element.50), channel_id=1, source_target_pairs={{0,160},{4,164},{8,168},{12,172},{16,176},{20,180},{24,184},{28,18... | collective-permute-start | bytes 344072 | tf_op jit(solution)/shard_map/ppermute | solution.py:365
  59.8 2.8 %collective-permute-start.13 = (bf16[16,3584]{1,0:T(8,128)(2,1)S(1)}, bf16[16,3584]{1,0:T(8,128)(2,1)S(1)}, u32[]{:S(2)}, u32[]{:S(2)}) collective-permute-start(bf16[16,3584]{1,0:T(8,128)(2,1)S(1)} %get-tuple-element.52), channel_id=1, source_target_pairs={{0,64},{4,68},{8,72},{12,76},{16,80},{20,84},{24,88},{28,92},{32,2... | collective-permute-start | bytes 344072 | tf_op jit(solution)/shard_map/ppermute | solution.py:365
  62.6 1.2 %collective-permute-start.14 = (bf16[16,3584]{1,0:T(8,128)(2,1)S(1)}, bf16[16,3584]{1,0:T(8,128)(2,1)S(1)}, u32[]{:S(2)}, u32[]{:S(2)}) collective-permute-start(bf16[16,3584]{1,0:T(8,128)(2,1)S(1)} %get-tuple-element.46.a0), channel_id=1, source_target_pairs={{0,4},{4,0},{8,12},{12,8},{16,20},{20,16},{24,28},{28,24},{32,36},... | collective-permute-start | bytes 344072 | tf_op jit(solution)/shard_map/ppermute | solution.py:370
  63.8 4.9 %shard_map.88 = (bf16[512,3584]{1,0:T(8,128)(2,1)}, bf16[2,1792]{1,0:T(2,128)(2,1)}, f32[8,128]{1,0:T(8,128)}) custom-call(s32[4]{0:T(128)S(1)} %pad_add_fusion.place, bf16[32,512]{1,0:T(8,128)(2,1)S(1)} %get-tuple-element.39.grad_score, f32[32,512]{1,0:T(8,128)S(1)} %get-tuple-element.33.attn, bf16[32,128]{1,0:T(8,128)(2,1)S(1)} %get-tuple-element.40.query_rows, ...), custom_call_target="tpu_custom_call" | custom-call | flops 1879048192 | tf_op jit(solution)/shard_map/pallas_call | solution.py:98
  68.7 0.0 collective-permute-start.15
  68.7 0.9 collective-permute-done.12.a2
  69.6 1.3 %collective-permute-start.16 = (bf16[16,3584]{1,0:T(8,128)(2,1)S(1)}, bf16[16,3584]{1,0:T(8,128)(2,1)S(1)}, u32[]{:S(2)}, u32[]{:S(2)}) collective-permute-start(bf16[16,3584]{1,0:T(8,128)(2,1)S(1)} %collective-permute-done.12.a2), channel_id=1, source_target_pairs={{0,4},{4,0},{8,12},{12,8},{16,20},{20,16},{24,28},{28,24},{32,36},... | collective-permute-start | bytes 344072 | tf_op jit(solution)/shard_map/ppermute | solution.py:370
  70.9 0.0 collective-permute-start.17
  70.9 0.9 %collective-permute-done.16.b2 = bf16[16,3584]{1,0:T(8,128)(2,1)S(1)} collective-permute-done((bf16[16,3584]{1,0:T(8,128)(2,1)S(1)}, bf16[16,3584]{1,0:T(8,128)(2,1)S(1)}, u32[]{:S(2)}, u32[]{:S(2)}) %collective-permute-start.16) | collective-permute-done | bytes 114720 | tf_op jit(solution)/shard_map/ppermute | solution.py:370
  71.9 0.4 collective-permute-done.17.b3
  72.2 1.1 %shard_map.90 = bf16[64,3584]{1,0:T(8,128)(2,1)S(1)} custom-call(s32[4]{0:T(128)S(1)} %pad_add_fusion.place, bf16[16,3584]{1,0:T(8,128)(2,1)S(1)} %get-tuple-element.46.a0, bf16[16,3584]{1,0:T(8,128)(2,1)S(1)} %collective-permute-done.11.a1, bf16[16,3584]{1,0:T(8,128)(2,1)S(1)} %collective-permute-done.12.a2, ...), custom_call_target="tpu_custom_call" | custom-call | tf_op jit(solution)/shard_map/pallas_call | solution.py:98
  73.4 0.2 reshape.23
  73.6 16.2 %all_to_all.11 = bf16[32,2,3584]{2,1,0:T(2,128)(2,1)S(1)} all-to-all(bf16[32,2,3584]{2,1,0:T(2,128)(2,1)S(1)} %reshape.23), channel_id=1, replica_groups={{0,1,2,3,8,9,10,11,16,17,18,19,24,25,26,27,32,33,34,35,40,41,42,43,48,4..., dimensions={0} | all-to-all | bytes 917504 | tf_op jit(solution)/shard_map/all_to_all | solution.py:374
  89.7 1.0 %convert_reduce_fusion = f32[2,3584]{1,0:T(2,128)} fusion(bf16[32,2,3584]{2,1,0:T(2,128)(2,1)S(1)} %all_to_all.11), kind=kLoop, calls=%fused_computation | loop fusion | flops 451584 | bytes 487424 | tf_op jit(solution)/shard_map/reduce_sum | solution.py:375
  (15 shorter events, 0.0 us)
Async XLA Ops:
  1.6 8.3 %collective-permute-start = (bf16[448,128]{1,0:T(8,128)(2,1)S(1)}, bf16[448,128]{1,0:T(8,128)(2,1)S(1)}, u32[]{:S(2)}, u32[]{:S(2)}) collective-permute-start(bf16[448,128]{1,0:T(8,128)(2,1)S(1)} %dynamic_slice.3), channel_id=1, source_target_pairs={{0,2},{1,3},{2,0},{3,1},{4,6},{5,7},{6,4},{7,5},{8,10},{9,11},{10,... | collective-permute-start | bytes 344072 | tf_op jit(solution)/shard_map/ppermute | solution.py:397
  5.4 2.0 %copy-start = (bf16[1,2,256,3584]{3,2,1,0:T(8,128)(2,1)S(1)}, bf16[1,2,256,3584]{3,2,1,0:T(8,128)(2,1)}, u32[]{:S(2)}) copy-start(bf16[1,2,256,3584]{3,2,1,0:T(8,128)(2,1)} %param.5) | copy-start | bytes 11010052
  7.5 1.2 %copy-start.2 = (bf16[896,512]{1,0:T(8,128)(2,1)S(1)}, bf16[896,512]{1,0:T(8,128)(2,1)}, u32[]{:S(2)}) copy-start(bf16[896,512]{1,0:T(8,128)(2,1)} %own.1) | copy-start | bytes 2752516
  9.9 16.7 %copy-start.1 = (bf16[1,2,256,3584]{3,2,1,0:T(8,128)(2,1)S(1)}, bf16[1,2,256,3584]{3,2,1,0:T(8,128)(2,1)}, u32[]{:S(2)}) copy-start(bf16[1,2,256,3584]{3,2,1,0:T(8,128)(2,1)} %param.5) | copy-start | bytes 11010052
  9.9 16.7 %copy-start.4 = (bf16[1,2,1792]{2,1,0:T(2,128)(2,1)S(1)}, bf16[1,2,1792]{2,1,0:T(2,128)(2,1)}, u32[]{:S(2)}) copy-start(bf16[1,2,1792]{2,1,0:T(2,128)(2,1)} %param.7) | copy-start | bytes 21508
  9.9 16.7 %copy-start.5 = (s32[1,2]{1,0:T(1,128)S(1)}, s32[1,2]{1,0:T(1,128)}, u32[]{:S(2)}) copy-start(s32[1,2]{1,0:T(1,128)} %param.6) | copy-start | bytes 28
  9.9 16.7 %copy-start.6 = (s32[1,2]{1,0:T(1,128)S(1)}, s32[1,2]{1,0:T(1,128)}, u32[]{:S(2)}) copy-start(s32[1,2]{1,0:T(1,128)} %param.8) | copy-start | bytes 28
  10.0 13.8 %collective-permute-start.1 = (bf16[896,512]{1,0:T(8,128)(2,1)S(1)}, bf16[896,512]{1,0:T(8,128)(2,1)S(1)}, u32[]{:S(2)}, u32[]{:S(2)}) collective-permute-start(bf16[896,512]{1,0:T(8,128)(2,1)S(1)} %copy-done.2), channel_id=1, source_target_pairs={{0,3},{1,0},{2,1},{3,2},{4,5},{5,6},{6,7},{7,4},{8,11},{9,8},{10,9... | collective-permute-start | bytes 2752520 | tf_op jit(solution)/shard_map/ppermute | solution.py:398
  10.4 6.5 %collective-permute-start.7 = (bf16[448,128]{1,0:T(8,128)(2,1)S(1)}, bf16[448,128]{1,0:T(8,128)(2,1)S(1)}, u32[]{:S(2)}, u32[]{:S(2)}) collective-permute-start(bf16[448,128]{1,0:T(8,128)(2,1)S(1)} %collective-permute-done.a0), channel_id=1, source_target_pairs={{0,24},{4,28},{8,0},{12,4},{16,8},{20,12},{24,16},{28,20},{32,56},... | collective-permute-start | bytes 344072 | tf_op jit(solution)/shard_map/ppermute | solution.py:399
  12.9 6.2 %collective-permute-start.5 = (bf16[448,128]{1,0:T(8,128)(2,1)S(1)}, bf16[448,128]{1,0:T(8,128)(2,1)S(1)}, u32[]{:S(2)}, u32[]{:S(2)}) collective-permute-start(bf16[448,128]{1,0:T(8,128)(2,1)S(1)} %collective-permute-done.a0), channel_id=1, source_target_pairs={{0,16},{4,20},{8,24},{12,28},{16,0},{20,4},{24,8},{28,12},{32,48},... | collective-permute-start | bytes 344072 | tf_op jit(solution)/shard_map/ppermute | solution.py:399
  13.4 8.2 %collective-permute-start.3 = (bf16[448,128]{1,0:T(8,128)(2,1)S(1)}, bf16[448,128]{1,0:T(8,128)(2,1)S(1)}, u32[]{:S(2)}, u32[]{:S(2)}) collective-permute-start(bf16[448,128]{1,0:T(8,128)(2,1)S(1)} %collective-permute-done.a0), channel_id=1, source_target_pairs={{0,8},{4,12},{8,16},{12,20},{16,24},{20,28},{24,0},{28,4},{32,40},... | collective-permute-start | bytes 344072 | tf_op jit(solution)/shard_map/ppermute | solution.py:399
  14.0 8.8 %collective-permute-start.2 = (bf16[448,128]{1,0:T(8,128)(2,1)S(1)}, bf16[448,128]{1,0:T(8,128)(2,1)S(1)}, u32[]{:S(2)}, u32[]{:S(2)}) collective-permute-start(bf16[448,128]{1,0:T(8,128)(2,1)S(1)} %collective-permute-done.a0), channel_id=1, source_target_pairs={{0,4},{4,0},{8,12},{12,8},{16,20},{20,16},{24,28},{28,24},{32,36},... | collective-permute-start | bytes 344072 | tf_op jit(solution)/shard_map/ppermute | solution.py:388
  17.0 5.8 %collective-permute-start.8 = (bf16[448,128]{1,0:T(8,128)(2,1)S(1)}, bf16[448,128]{1,0:T(8,128)(2,1)S(1)}, u32[]{:S(2)}, u32[]{:S(2)}) collective-permute-start(bf16[448,128]{1,0:T(8,128)(2,1)S(1)} %collective-permute-done.7.a3), channel_id=1, source_target_pairs={{0,4},{4,0},{8,12},{12,8},{16,20},{20,16},{24,28},{28,24},{32,36},... | collective-permute-start | bytes 344072 | tf_op jit(solution)/shard_map/ppermute | solution.py:388
  19.1 3.7 %collective-permute-start.6 = (bf16[448,128]{1,0:T(8,128)(2,1)S(1)}, bf16[448,128]{1,0:T(8,128)(2,1)S(1)}, u32[]{:S(2)}, u32[]{:S(2)}) collective-permute-start(bf16[448,128]{1,0:T(8,128)(2,1)S(1)} %collective-permute-done.5.a2), channel_id=1, source_target_pairs={{0,4},{4,0},{8,12},{12,8},{16,20},{20,16},{24,28},{28,24},{32,36},... | collective-permute-start | bytes 344072 | tf_op jit(solution)/shard_map/ppermute | solution.py:388
  21.7 2.1 %collective-permute-start.4 = (bf16[448,128]{1,0:T(8,128)(2,1)S(1)}, bf16[448,128]{1,0:T(8,128)(2,1)S(1)}, u32[]{:S(2)}, u32[]{:S(2)}) collective-permute-start(bf16[448,128]{1,0:T(8,128)(2,1)S(1)} %collective-permute-done.3.a1), channel_id=1, source_target_pairs={{0,4},{4,0},{8,12},{12,8},{16,20},{20,16},{24,28},{28,24},{32,36},... | collective-permute-start | bytes 344072 | tf_op jit(solution)/shard_map/ppermute | solution.py:388
  23.8 2.9 %collective-permute-start.9 = (bf16[896,512]{1,0:T(8,128)(2,1)S(1)}, bf16[896,512]{1,0:T(8,128)(2,1)S(1)}, u32[]{:S(2)}, u32[]{:S(2)}) collective-permute-start(bf16[896,512]{1,0:T(8,128)(2,1)S(1)} %collective-permute-done.1.weight.near), channel_id=1, source_target_pairs={{0,4},{4,0},{8,12},{12,8},{16,20},{20,16},{24,28},{28,24},{32,36},... | collective-permute-start | bytes 2752520 | tf_op jit(solution)/shard_map/ppermute | solution.py:388
  50.7 3.5 %collective-permute-start.10 = (bf16[256,512]{1,0:T(8,128)(2,1)S(1)}, bf16[256,512]{1,0:T(8,128)(2,1)S(1)}, u32[]{:S(2)}, u32[]{:S(2)}) collective-permute-start(bf16[256,512]{1,0:T(8,128)(2,1)S(1)} %bitcast.17), channel_id=1, source_target_pairs={{0,4},{4,0},{8,12},{12,8},{16,20},{20,16},{24,28},{28,24},{32,36},... | collective-permute-start | bytes 786440 | tf_op jit(solution)/shard_map/ppermute | solution.py:341
  56.4 7.4 %copy-start.3 = (bf16[896,512]{1,0:T(8,128)(2,1)S(1)}, bf16[896,512]{1,0:T(8,128)(2,1)}, u32[]{:S(2)}) copy-start(bf16[896,512]{1,0:T(8,128)(2,1)} %own.1) | copy-start | bytes 2752516
  57.7 11.0 %collective-permute-start.11 = (bf16[16,3584]{1,0:T(8,128)(2,1)S(1)}, bf16[16,3584]{1,0:T(8,128)(2,1)S(1)}, u32[]{:S(2)}, u32[]{:S(2)}) collective-permute-start(bf16[16,3584]{1,0:T(8,128)(2,1)S(1)} %get-tuple-element.47), channel_id=1, source_target_pairs={{0,224},{4,228},{8,232},{12,236},{16,240},{20,244},{24,248},{28,25... | collective-permute-start | bytes 344072 | tf_op jit(solution)/shard_map/ppermute | solution.py:365
  58.0 11.6 %collective-permute-start.12 = (bf16[16,3584]{1,0:T(8,128)(2,1)S(1)}, bf16[16,3584]{1,0:T(8,128)(2,1)S(1)}, u32[]{:S(2)}, u32[]{:S(2)}) collective-permute-start(bf16[16,3584]{1,0:T(8,128)(2,1)S(1)} %get-tuple-element.50), channel_id=1, source_target_pairs={{0,160},{4,164},{8,168},{12,172},{16,176},{20,180},{24,184},{28,18... | collective-permute-start | bytes 344072 | tf_op jit(solution)/shard_map/ppermute | solution.py:365
  59.8 11.1 %collective-permute-start.13 = (bf16[16,3584]{1,0:T(8,128)(2,1)S(1)}, bf16[16,3584]{1,0:T(8,128)(2,1)S(1)}, u32[]{:S(2)}, u32[]{:S(2)}) collective-permute-start(bf16[16,3584]{1,0:T(8,128)(2,1)S(1)} %get-tuple-element.52), channel_id=1, source_target_pairs={{0,64},{4,68},{8,72},{12,76},{16,80},{20,84},{24,88},{28,92},{32,2... | collective-permute-start | bytes 344072 | tf_op jit(solution)/shard_map/ppermute | solution.py:365
  62.6 8.3 %collective-permute-start.14 = (bf16[16,3584]{1,0:T(8,128)(2,1)S(1)}, bf16[16,3584]{1,0:T(8,128)(2,1)S(1)}, u32[]{:S(2)}, u32[]{:S(2)}) collective-permute-start(bf16[16,3584]{1,0:T(8,128)(2,1)S(1)} %get-tuple-element.46.a0), channel_id=1, source_target_pairs={{0,4},{4,0},{8,12},{12,8},{16,20},{20,16},{24,28},{28,24},{32,36},... | collective-permute-start | bytes 344072 | tf_op jit(solution)/shard_map/ppermute | solution.py:370
  68.7 2.2 %collective-permute-start.15 = (bf16[16,3584]{1,0:T(8,128)(2,1)S(1)}, bf16[16,3584]{1,0:T(8,128)(2,1)S(1)}, u32[]{:S(2)}, u32[]{:S(2)}) collective-permute-start(bf16[16,3584]{1,0:T(8,128)(2,1)S(1)} %collective-permute-done.11.a1), channel_id=1, source_target_pairs={{0,4},{4,0},{8,12},{12,8},{16,20},{20,16},{24,28},{28,24},{32,36},... | collective-permute-start | bytes 344072 | tf_op jit(solution)/shard_map/ppermute | solution.py:370
  69.6 2.3 %collective-permute-start.16 = (bf16[16,3584]{1,0:T(8,128)(2,1)S(1)}, bf16[16,3584]{1,0:T(8,128)(2,1)S(1)}, u32[]{:S(2)}, u32[]{:S(2)}) collective-permute-start(bf16[16,3584]{1,0:T(8,128)(2,1)S(1)} %collective-permute-done.12.a2), channel_id=1, source_target_pairs={{0,4},{4,0},{8,12},{12,8},{16,20},{20,16},{24,28},{28,24},{32,36},... | collective-permute-start | bytes 344072 | tf_op jit(solution)/shard_map/ppermute | solution.py:370
  70.9 1.3 %collective-permute-start.17 = (bf16[16,3584]{1,0:T(8,128)(2,1)S(1)}, bf16[16,3584]{1,0:T(8,128)(2,1)S(1)}, u32[]{:S(2)}, u32[]{:S(2)}) collective-permute-start(bf16[16,3584]{1,0:T(8,128)(2,1)S(1)} %collective-permute-done.13.a3), channel_id=1, source_target_pairs={{0,4},{4,0},{8,12},{12,8},{16,20},{20,16},{24,28},{28,24},{32,36},... | collective-permute-start | bytes 344072 | tf_op jit(solution)/shard_map/ppermute | solution.py:370
